TPU v7x, 32 devices: a whole 2x2x4 slice. The times are simulated.
32 devices in a mesh: lon: 4 (over z), lat: 4 (over y, core), lev: 2 (over x).
Axes of the slice: x: 2, y: 2, z: 4, core: 2. Of those that a mesh axis runs over, the one named last changes fastest.
Arguments:
- state: float32 [5, 16, 64, 2048], P(None, 'lev', 'lat', 'lon'), may hold values from -6 to 6
- mask: int32 [16, 64, 2048], P('lev', 'lat', 'lon'), may hold values 0 or 1
- coriolis: float32 [64], P('lat'), may hold values from 0.05 to 0.3
- penetration: float32 [16], P('lev'), may hold values from 0.05 to 1
- flux_tiles: float32 [2048, 3, 512], P(('lon', 'lat')), may hold values from -4 to 4
- flux_owner: int32 [2048, 1], P(('lon', 'lat')), may hold values from 0 to 15; in each aligned block of 128 rows (0 to 127, 128 to 255, ...) at most 16 rows name the same one
- flux_row: int32 [2048], P(('lon', 'lat')), may hold values from 0 to 15
- fold_partner: int32 [2048], replicated, may hold values from 0 to 2047, as said below
Outputs:
- new_state: float32 [5, 16, 64, 2048], P(None, 'lev', 'lat', 'lon')
Inputs may be any that keep to these rules, and one draw needn't show every extreme that they name: `flux_owner`: among the 128 tiles of one device at most 16 name the same owner, and some owner receives exactly 16 from some device. fold_partner[i] = (h - i) mod 2048 for one hinge column h.
All inputs are finite; a program needn't handle non-finite values. No bound on the sum of `mask` on one device may be relied on, other than what follows from the above.
Results may differ from a plain program's by a relative error of at most 0.0003.
Values sent between devices are 32-bit elements; how exact they have to be, the bound alone decides.
No kernel may reach another device: no remote copies, remote signals or barrier semaphores. Data moves between devices by JAX's collectives and lax.ppermute only.
A program may use at most 192 MiB of HBM per device.

v0:
```python
import jax
import jax.numpy as jnp
from jax import lax
from jax.sharding import PartitionSpec as P

STEPS = 2


ALPHA = 0.2
BETA = 0.15
PRESS = 0.1
VISCOUS = 0.1
DIFFUSE = 0.1
ADVECT = 0.1


def padded(value, sides, width, wrap):
    for axis, dim in sides:
        peers, length = (lax.axis_size(axis), value.shape[dim])
        up = [(i, (i + 1) % peers) for i in range(peers if wrap else peers - 1)]
        down = [(j, i) for i, j in up]
        last = lax.slice_in_dim(value, length - width, length, axis=dim)
        initial = lax.slice_in_dim(value, 0, width, axis=dim)
        before = lax.ppermute(last, axis, up)
        after = lax.ppermute(initial, axis, down)
        value = jnp.concatenate([before, value, after], axis=dim)
    return value


def carried_in(value, axis, combine, identity):
    peers, place = (lax.axis_size(axis), lax.axis_index(axis))
    everything = lax.all_gather(value, axis)
    start = jnp.broadcast_to(jnp.asarray(identity, value.dtype), value.shape)

    def hop(k, before):
        reached = k < place
        new = combine(before, everything[k])
        return jnp.where(reached, new, before)

    return lax.fori_loop(0, peers, hop, start)


def receive_flux(flux_tiles, flux_owner, flux_row, rows, cols):
    lat_count = lax.axis_size("lat")
    lon_count = lax.axis_size("lon")
    owners = lat_count * lon_count
    tiles = flux_tiles.shape[0]
    capacity = max(2, 2 * tiles // owners)
    owner = flux_owner[:, 0]
    hits = (owner[:, None] == jnp.arange(owners, dtype=jnp.int32)[None, :]).astype(jnp.int32)
    before = jnp.cumsum(hits, axis=0) - hits
    slot = jnp.sum(before * hits, axis=1)
    target = owner * capacity + slot
    placing = target[None, :] == jnp.arange(owners * capacity, dtype=jnp.int32)[:, None]
    packed = jnp.dot(
        placing.astype(jnp.float32),
        flux_tiles.reshape(tiles, 3 * cols),
        precision=lax.Precision.HIGHEST,
    )
    slot_rows = jnp.sum(placing.astype(jnp.int32) * (flux_row[None, :] + 1), axis=1) - 1
    arrived, arrived_rows = (
        lax.all_to_all(
            packed.reshape(owners, capacity, 3 * cols),
            ("lon", "lat"),
            split_axis=0,
            concat_axis=0,
            tiled=True,
        ),
        lax.all_to_all(
            slot_rows.reshape(owners, capacity),
            ("lon", "lat"),
            split_axis=0,
            concat_axis=0,
            tiled=True,
        ),
    )
    arrived = arrived.reshape(owners * capacity, 3 * cols)
    arrived_rows = arrived_rows.reshape(owners * capacity)
    landing = (arrived_rows[None, :] == jnp.arange(rows, dtype=jnp.int32)[:, None]).astype(
        jnp.float32
    )
    summed = jnp.dot(landing, arrived, precision=lax.Precision.HIGHEST)
    return summed.reshape(rows, 3, cols).transpose(1, 0, 2)


def advance(state, wet, turning, absorb, forcing, partner):
    fields, levels, rows, cols = state.shape
    lat_count = lax.axis_size("lat")
    lat_place = lax.axis_index("lat")
    signs = jnp.array([-1.0, -1.0, 1.0, 1.0, 1.0], jnp.float32)
    lon_ext = padded(state, (("lon", 3),), 1, True)
    lat_ext = padded(state, (("lat", 2),), 1, False)
    whole_top = lax.all_gather(state[:, :, rows - 1, :], "lon", axis=2, tiled=True)
    mirrored = jnp.take(whole_top, partner, axis=2) * signs[:, None, None]
    north_edge = jnp.where(lat_place == lat_count - 1, mirrored, lat_ext[:, :, rows + 1, :])
    south_edge = jnp.where(lat_place == 0, state[:, :, 0, :], lat_ext[:, :, 0, :])
    east_all = lon_ext[:, :, :, 2:]
    west_all = lon_ext[:, :, :, :-2]
    north_all = jnp.concatenate([lat_ext[:, :, 2 : rows + 1, :], north_edge[:, :, None, :]], axis=2)
    south_all = jnp.concatenate([south_edge[:, :, None, :], lat_ext[:, :, 1:rows, :]], axis=2)
    sets = jnp.stack([state, east_all, west_all, north_all, south_all])
    buoyancy = ALPHA * sets[:, 2] - BETA * sets[:, 3]
    running = jnp.cumsum(buoyancy, axis=1)
    column_total = running[:, -1]
    prefix = carried_in(
        column_total, "lev", lambda earlier, later: earlier + later, jnp.zeros_like(column_total)
    )
    pressure = PRESS * (prefix[:, None] + running - 0.5 * buoyancy)
    slope_x = 0.5 * (pressure[1] - pressure[2])
    slope_y = 0.5 * (pressure[3] - pressure[4])
    zonal, merid = (state[0], state[1])
    result = []
    for field in range(5):
        value = state[field]
        east = east_all[field]
        west = west_all[field]
        north = north_all[field]
        south = south_all[field]
        laplace = east + west + north + south - 4.0 * value
        if field == 0:
            trend = turning * merid - slope_x + VISCOUS * laplace
        elif field == 1:
            trend = -turning * zonal - slope_y + VISCOUS * laplace
        else:
            trend = (
                DIFFUSE * laplace
                - ADVECT * (zonal * (0.5 * (east - west)) + merid * (0.5 * (north - south)))
                + absorb * forcing[field - 2][None]
            )
        result.append(value + wet * trend)
    return jnp.stack(result)


def body(state, mask, coriolis, penetration, flux_tiles, flux_owner, flux_row, fold_partner):
    fields, levels, rows, cols = state.shape
    forcing = receive_flux(flux_tiles, flux_owner, flux_row, rows, cols)
    partner = lax.dynamic_slice_in_dim(fold_partner, lax.axis_index("lon") * cols, cols)
    wet = mask.astype(jnp.float32)
    turning = coriolis[None, :, None]
    absorb = penetration[:, None, None]
    for substep in range(STEPS):
        state = advance(state, wet, turning, absorb, forcing, partner)
    return state


def solution(mesh):
    return jax.shard_map(
        body,
        mesh=mesh,
        in_specs=(
            P(None, "lev", "lat", "lon"),
            P("lev", "lat", "lon"),
            P("lat"),
            P("lev"),
            P(("lon", "lat"), None, None),
            P(("lon", "lat"), None),
            P(("lon", "lat")),
            P(),
        ),
        out_specs=P(None, "lev", "lat", "lon"),
        check_vma=False,
    )
```

profile of v0, /device:TPU:6, one launch (start us, length us, event | category | flops | bytes accessed | tf_op | source)
XLA Modules:
  0.0 190.3 jit_solution(5659657814675062352)
XLA Ops:
  7.1 2.2 %collective-permute-start = (f32[5,8,16,1]{3,2,1,0:T(8,128)}, f32[5,8,16,1]{3,2,1,0:T(8,128)}, u32[]{:S(2)}, u32[]{:S(2)}) collective-permute-start(f32[5,8,16,1]{3,2,1,0:T(8,128)} %get-tuple-element.230), channel_id=1, source_target_pairs={{8,0},{16,8},{24,16},{0,24},{9,1},{17,9},{25,17},{1,25},{10,2},{18... | collective-permute-start | bytes 7688 | tf_op jit(solution)/shard_map/ppermute | solution.py:25
  10.7 4.6 %all-to-all-start = ((s32[16,1,16]{2,1,0:T(1,128)}), s32[16,1,16]{2,1,0:T(1,128)S(1)}, u32[]{:S(2)}, u32[]{:S(2)}) async-start(s32[16,1,16]{2,1,0:T(1,128)} %sub.160), calls=%async_computation | async-start | bytes 16384 | tf_op jit(solution)/shard_map/all_to_all | solution.py:69
  16.5 16.9 %all-gather = f32[5,8,1,2048]{3,1,2,0:T(8,128)} all-gather(f32[5,8,1,512]{3,1,2,0:T(8,128)S(1)} %copy.146), channel_id=2, replica_groups=mesh['lon'=4,'lat'=4,'lev'=2] {'lon'}, dimensions={3}, use_global_device_ids=true | all-gather | bytes 409600 | tf_op jit(solution)/shard_map/all_gather | solution.py:93
  35.9 2.3 %copy.133 = f32[128,3,512]{0,2,1:T(8,128)} copy(f32[128,3,512]{2,0,1:T(8,128)} %param.20) | data formatting | bytes 1572864 | tf_op args[4]
  39.0 3.1 %fusion.182 = f32[16,16,1536]{2,1,0:T(8,128)} fusion(f32[128,1536,1]{0,1,2:T(8,128)} %bitcast.495, s32[16,16]{1,0:T(8,128)S(1)} %multiply_add_fusion.6, s32[128]{0:T(128)S(1)} %get-tuple-element.243), kind=kOutput, calls=%fused_computation.314 | convolution fusion | flops 604012544 | bytes 2360832 | tf_op jit(solution)/shard_map/dot_general | solution.py:55
  42.1 5.8 %copy.126 = f32[5,8,1,2048]{1,0,3,2:T(8,128)} copy(f32[5,8,1,2048]{3,1,2,0:T(8,128)} %all-gather) | data formatting | bytes 655360 | tf_op jit(solution)/shard_map/all_gather | solution.py:93
  48.5 5.7 %gather_fusion = f32[512,5,8]{2,1,0:T(8,128)} fusion(f32[5,8,2048]{1,0,2:T(8,128)} %bitcast.490, s32[1024]{0:T(1024)S(1)} %pad_clamp_fusion), kind=kCustom, calls=%fused_computation.clone | custom fusion | bytes 165888 | tf_op jit(solution)/shard_map/jit(_take)/gather | solution.py:94
  54.2 5.6 %all-to-all-start.1 = ((f32[16,16,1536]{2,1,0:T(8,128)}), f32[16,16,1536]{2,1,0:T(8,128)}, u32[]{:S(2)}, u32[]{:S(2)}) async-start(f32[16,16,1536]{2,1,0:T(8,128)} %fusion.182), calls=%async_computation.1 | async-start | bytes 3145728 | tf_op jit(solution)/shard_map/all_to_all | solution.py:62
  62.8 2.9 %fusion.27 = f32[5,5,8,16,512]{4,3,2,1,0:T(8,128)} fusion(f32[5,5,8,16,512]{4,3,2,1,0:T(8,128)} %bitcast_dynamic-update-slice_fusion.1, f32[5,8,16,513]{3,2,1,0:T(8,128)} %constant_dynamic-update-slice_fusion), kind=kLoop, calls=%fused_computation.94 | loop fusion | bytes 2621440
  73.5 4.2 %fusion.1 = f32[5,8,1,512]{1,0,3,2:T(8,128)} fusion(f32[5,8,1,512]{1,0,3,2:T(8,128)} %copy.128, f32[512,5,8]{2,1,0:T(8,128)} %gather_fusion, f32[5]{0:T(128)S(1)} %copy-done.31, pred[512]{0:T(512)(128)(4,1)S(1)} %get-tuple-element.222, pred[]{:T(512)S(6)} %eq.66), kind=kLoop, calls=%fused_computation.47 | loop fusion | flops 61440 | bytes 246293 | tf_op jit(solution)/shard_map/broadcast_in_dim | solution.py:99
  84.8 6.1 %all-gather.1 = f32[10,1,16,512]{3,2,1,0:T(8,128)} all-gather(f32[5,1,16,512]{3,2,1,0:T(8,128)S(1)} %slice.354), channel_id=3, replica_groups=mesh['lon'=4,'lat'=4,'lev'=2] {'lev'}, dimensions={0}, use_global_device_ids=true | all-gather | bytes 491520 | tf_op jit(solution)/shard_map/all_gather | solution.py:32
  92.9 2.4 %subtract_multiply_fusion.1 = f32[5,8,16,512]{3,2,1,0:T(8,128)S(1)} fusion(f32[5,8,16,512]{3,2,1,0:T(8,128)S(1)} %fusion.28, f32[5,16,512]{2,1,0:T(8,128)S(1)} %get-tuple-element.164, f32[5,5,8,16,512]{4,3,2,1,0:T(8,128)} %fusion.16), kind=kLoop, calls=%fused_computation.98 | loop fusion | flops 2293760 | bytes 5406720 | tf_op jit(solution)/shard_map/mul | solution.py:108
  99.5 3.1 %copy.135 = f32[1536,256]{1,0:T(8,128)} copy(f32[1536,256]{0,1:T(8,128)} %bitcast.29) | data formatting | bytes 3145728 | tf_op jit(solution)/shard_map/dot_general | solution.py:82
  102.5 2.3 %convolution_bitcast_fusion = f32[3,16,512]{2,1,0:T(8,128)S(1)} fusion(f32[3,512,256]{2,1,0:T(8,128)} %bitcast.492, s32[256]{0:T(256)S(1)} %eq.74), kind=kOutput, calls=%fused_computation.99 | convolution fusion | flops 75501568 | bytes 1672192 | tf_op jit(solution)/shard_map/dot_general | solution.py:82
  115.3 2.4 %collective-permute-start.4 = (f32[5,8,16,1]{3,2,1,0:T(8,128)}, f32[5,8,16,1]{3,2,1,0:T(8,128)S(1)}, u32[]{:S(2)}, u32[]{:S(2)}) collective-permute-start(f32[5,8,16,1]{3,2,1,0:T(8,128)} %get-tuple-element.226), channel_id=1, source_target_pairs={{8,0},{16,8},{24,16},{0,24},{9,1},{17,9},{25,17},{1,25},{10,2},{18... | collective-permute-start | bytes 7688 | tf_op jit(solution)/shard_map/ppermute | solution.py:25
  120.2 15.4 %all-gather.2 = f32[5,8,1,2048]{3,1,2,0:T(8,128)} all-gather(f32[5,8,1,512]{3,1,2,0:T(8,128)} %copy.150), channel_id=4, replica_groups=mesh['lon'=4,'lat'=4,'lev'=2] {'lon'}, dimensions={3}, use_global_device_ids=true | all-gather | bytes 409600 | tf_op jit(solution)/shard_map/all_gather | solution.py:93
  136.9 5.8 %copy.137 = f32[5,8,1,2048]{1,0,3,2:T(8,128)} copy(f32[5,8,1,2048]{3,1,2,0:T(8,128)} %all-gather.2) | data formatting | bytes 655360 | tf_op jit(solution)/shard_map/all_gather | solution.py:93
  142.8 5.7 %gather_fusion.1 = f32[512,5,8]{2,1,0:T(8,128)} fusion(f32[5,8,2048]{1,0,2:T(8,128)} %bitcast.491, s32[1024]{0:T(1024)S(1)} %pad_clamp_fusion), kind=kCustom, calls=%fused_computation.1.clone | custom fusion | bytes 165888 | tf_op jit(solution)/shard_map/jit(_take)/gather | solution.py:94
  155.1 2.8 %copy.139 = f32[5,8,1,512]{1,0,3,2:T(8,128)} copy(f32[5,8,1,512]{3,1,2,0:T(8,128)} %collective-permute-done.6) | data formatting | bytes 163840 | tf_op jit(solution)/shard_map/ppermute | solution.py:25
  158.0 4.2 %fusion = f32[5,8,1,512]{1,0,3,2:T(8,128)} fusion(f32[5,8,1,512]{1,0,3,2:T(8,128)} %copy.139, f32[512,5,8]{2,1,0:T(8,128)} %gather_fusion.1, f32[5]{0:T(128)S(1)} %copy-done.32, pred[512]{0:T(512)(128)(4,1)S(1)} %get-tuple-element.222, pred[]{:T(512)S(6)} %eq.66), kind=kLoop, calls=%fused_computation.44 | loop fusion | flops 61440 | bytes 246293 | tf_op jit(solution)/shard_map/broadcast_in_dim | solution.py:99
  162.1 2.6 %copy.140 = f32[5,8,1,512]{3,2,1,0:T(1,128)} copy(f32[5,8,1,512]{1,0,3,2:T(8,128)} %fusion) | data formatting | bytes 163840 | tf_op jit(solution)/shard_map/broadcast_in_dim | solution.py:99
  171.4 7.7 %all-gather.3 = f32[10,1,16,512]{3,2,1,0:T(8,128)} all-gather(f32[5,1,16,512]{3,2,1,0:T(8,128)S(1)} %slice.407), channel_id=5, replica_groups=mesh['lon'=4,'lat'=4,'lev'=2] {'lev'}, dimensions={0}, use_global_device_ids=true | all-gather | bytes 491520 | tf_op jit(solution)/shard_map/all_gather | solution.py:32
  179.1 3.3 %while.29 = (s32[]{:T(128)}, f32[5,16,512]{2,1,0:T(8,128)}, s32[]{:T(128)}, f32[2,5,16,512]{3,2,1,0:T(8,128)}, s32[]{:T(128)}, /*index=5*/s32[]{:T(128)}) while((s32[]{:T(128)}, f32[5,16,512]{2,1,0:T(8,128)}, s32[]{:T(128)}, f32[2,5,16,512]{3,2,1,0:T(8,128)}, s32[]{:T(128)}, /*index=5*/s32[]{:T(128)}) %tuple.83), condition=%wide.region_8.10_spmd.clone, body=%wide.region_7.9_spmd.clone.sunk | while | flops 122884 | bytes 491621 | solution.py:40
  182.4 2.8 %subtract_multiply_fusion = f32[5,8,16,512]{3,2,1,0:T(8,128)S(1)} fusion(f32[5,8,16,512]{3,2,1,0:T(8,128)} %copy-done.12, f32[5,16,512]{2,1,0:T(8,128)} %get-tuple-element.165, f32[5,5,8,16,512]{4,3,2,1,0:T(8,128)} %fusion.12), kind=kLoop, calls=%fused_computation.97 | loop fusion | flops 2293760 | bytes 5406720 | tf_op jit(solution)/shard_map/mul | solution.py:108
  (149 shorter events, 75.4 us)
Async XLA Ops:
  0.0 15.2 %copy-start = (f32[5,8,16,512]{3,2,1,0:T(8,128)S(1)}, f32[5,8,16,512]{3,2,1,0:T(8,128)}, u32[]{:S(2)}) copy-start(f32[5,8,16,512]{3,2,1,0:T(8,128)} %param.16) | copy-start | bytes 3932164
  0.0 9.4 %copy-start.28 = (s32[128,1]{0,1:T(1,128)S(1)}, s32[128,1]{0,1:T(1,128)}, u32[]{:S(2)}) copy-start(s32[128,1]{0,1:T(1,128)} %param.21) | copy-start | bytes 1540
  0.0 9.8 %copy-start.35 = (s32[128]{0:T(128)S(1)}, s32[128]{0:T(128)}, u32[]{:S(2)}) copy-start(s32[128]{0:T(128)} %param.22) | copy-start | bytes 1540
  1.6 64.2 %collective-permute-start.3 = (f32[5,8,1,512]{3,1,2,0:T(8,128)S(1)}, f32[5,8,1,512]{3,1,2,0:T(8,128)S(1)}, u32[]{:S(2)}, u32[]{:S(2)}) collective-permute-start(f32[5,8,1,512]{3,1,2,0:T(8,128)S(1)} %copy.146), channel_id=1, source_target_pairs={{0,2},{2,4},{4,6},{1,3},{3,5},{5,7},{8,10},{10,12},{12,14},{9,11},... | collective-permute-start | bytes 245768 | tf_op jit(solution)/shard_map/ppermute | solution.py:24
  5.6 62.2 %collective-permute-start.1 = (f32[5,8,16,1]{3,2,1,0:T(8,128)}, f32[5,8,16,1]{3,2,1,0:T(8,128)S(1)}, u32[]{:S(2)}, u32[]{:S(2)}) collective-permute-start(f32[5,8,16,1]{3,2,1,0:T(8,128)} %get-tuple-element.231), channel_id=1, source_target_pairs={{0,8},{8,16},{16,24},{24,0},{1,9},{9,17},{17,25},{25,1},{2,10},{10... | collective-permute-start | bytes 7688 | tf_op jit(solution)/shard_map/ppermute | solution.py:24
  7.1 53.9 %collective-permute-start = (f32[5,8,16,1]{3,2,1,0:T(8,128)}, f32[5,8,16,1]{3,2,1,0:T(8,128)}, u32[]{:S(2)}, u32[]{:S(2)}) collective-permute-start(f32[5,8,16,1]{3,2,1,0:T(8,128)} %get-tuple-element.230), channel_id=1, source_target_pairs={{8,0},{16,8},{24,16},{0,24},{9,1},{17,9},{25,17},{1,25},{10,2},{18... | collective-permute-start | bytes 7688 | tf_op jit(solution)/shard_map/ppermute | solution.py:25
  10.7 43.5 %all-to-all-start = ((s32[16,1,16]{2,1,0:T(1,128)}), s32[16,1,16]{2,1,0:T(1,128)S(1)}, u32[]{:S(2)}, u32[]{:S(2)}) async-start(s32[16,1,16]{2,1,0:T(1,128)} %sub.160), calls=%async_computation | async-start | bytes 16384 | tf_op jit(solution)/shard_map/all_to_all | solution.py:69
  16.5 63.2 %copy-start.1 = (f32[5,8,15,512]{3,2,1,0:T(8,128)}, f32[5,8,15,512]{3,2,1,0:T(8,128)S(1)}, u32[]{:S(2)}) copy-start(f32[5,8,15,512]{3,2,1,0:T(8,128)S(1)} %get-tuple-element.232) | copy-start | bytes 3686404
  42.1 5.9 %copy-start.29 = (f32[16]{0:T(128)S(1)}, f32[16]{0:T(128)}, u32[]{:S(2)}) copy-start(f32[16]{0:T(128)} %param.18) | copy-start | bytes 196
  54.2 45.3 %all-to-all-start.1 = ((f32[16,16,1536]{2,1,0:T(8,128)}), f32[16,16,1536]{2,1,0:T(8,128)}, u32[]{:S(2)}, u32[]{:S(2)}) async-start(f32[16,16,1536]{2,1,0:T(8,128)} %fusion.182), calls=%async_computation.1 | async-start | bytes 3145728 | tf_op jit(solution)/shard_map/all_to_all | solution.py:62
  65.8 5.8 %collective-permute-start.2 = (f32[5,8,1,512]{3,1,2,0:T(8,128)S(1)}, f32[5,8,1,512]{3,1,2,0:T(8,128)S(1)}, u32[]{:S(2)}, u32[]{:S(2)}) collective-permute-start(f32[5,8,1,512]{3,1,2,0:T(8,128)S(1)} %get-tuple-element.241), channel_id=1, source_target_pairs={{2,0},{4,2},{6,4},{3,1},{5,3},{7,5},{10,8},{12,10},{14,12},{11,9},... | collective-permute-start | bytes 245768 | tf_op jit(solution)/shard_map/ppermute | solution.py:25
  69.3 4.2 %copy-start.31 = (f32[5]{0:T(128)S(1)}, f32[5]{0:T(128)}, u32[]{:S(2)}) copy-start(f32[5]{0:T(128)} %constant.106.clone) | copy-start | bytes 64
  104.9 4.2 %copy-start.20 = (f32[16,512]{1,0:T(8,128)}, f32[16,512]{1,0:T(8,128)S(1)}, u32[]{:S(2)}) copy-start(f32[16,512]{1,0:T(8,128)S(1)} %get-tuple-element.236) | copy-start | bytes 98308
  115.3 33.1 %collective-permute-start.4 = (f32[5,8,16,1]{3,2,1,0:T(8,128)}, f32[5,8,16,1]{3,2,1,0:T(8,128)S(1)}, u32[]{:S(2)}, u32[]{:S(2)}) collective-permute-start(f32[5,8,16,1]{3,2,1,0:T(8,128)} %get-tuple-element.226), channel_id=1, source_target_pairs={{8,0},{16,8},{24,16},{0,24},{9,1},{17,9},{25,17},{1,25},{10,2},{18... | collective-permute-start | bytes 7688 | tf_op jit(solution)/shard_map/ppermute | solution.py:25
  118.3 31.7 %collective-permute-start.7 = (f32[5,8,1,512]{3,1,2,0:T(8,128)}, f32[5,8,1,512]{3,1,2,0:T(8,128)}, u32[]{:S(2)}, u32[]{:S(2)}) collective-permute-start(f32[5,8,1,512]{3,1,2,0:T(8,128)} %copy.150), channel_id=1, source_target_pairs={{0,2},{2,4},{4,6},{1,3},{3,5},{5,7},{8,10},{10,12},{12,14},{9,11},... | collective-permute-start | bytes 245768 | tf_op jit(solution)/shard_map/ppermute | solution.py:24
  135.6 17.2 %collective-permute-start.5 = (f32[5,8,16,1]{3,2,1,0:T(8,128)}, f32[5,8,16,1]{3,2,1,0:T(8,128)S(1)}, u32[]{:S(2)}, u32[]{:S(2)}) collective-permute-start(f32[5,8,16,1]{3,2,1,0:T(8,128)} %get-tuple-element.227), channel_id=1, source_target_pairs={{0,8},{8,16},{16,24},{24,0},{1,9},{9,17},{17,25},{25,1},{2,10},{10... | collective-permute-start | bytes 7688 | tf_op jit(solution)/shard_map/ppermute | solution.py:24
  150.9 4.2 %collective-permute-start.6 = (f32[5,8,1,512]{3,1,2,0:T(8,128)S(1)}, f32[5,8,1,512]{3,1,2,0:T(8,128)}, u32[]{:S(2)}, u32[]{:S(2)}) collective-permute-start(f32[5,8,1,512]{3,1,2,0:T(8,128)S(1)} %get-tuple-element.239), channel_id=1, source_target_pairs={{2,0},{4,2},{6,4},{3,1},{5,3},{7,5},{10,8},{12,10},{14,12},{11,9},... | collective-permute-start | bytes 245768 | tf_op jit(solution)/shard_map/ppermute | solution.py:25
  154.4 3.6 %copy-start.32 = (f32[5]{0:T(128)S(1)}, f32[5]{0:T(128)}, u32[]{:S(2)}) copy-start(f32[5]{0:T(128)} %constant.106.clone) | copy-start | bytes 64
  182.4 2.8 %copy-start.8 = (f32[5,8,15,512]{3,2,1,0:T(8,128)S(1)}, f32[5,8,15,512]{3,2,1,0:T(8,128)}, u32[]{:S(2)}) copy-start(f32[5,8,15,512]{3,2,1,0:T(8,128)} %get-tuple-element.229) | copy-start | bytes 3686404
  182.4 2.8 %copy-start.10 = (f32[8,16,512]{2,1,0:T(8,128)S(1)}, f32[8,16,512]{2,1,0:T(8,128)}, u32[]{:S(2)}) copy-start(f32[8,16,512]{2,1,0:T(8,128)} %get-tuple-element.221) | copy-start | bytes 786436
  182.4 2.8 %copy-start.11 = (f32[8,16,512]{2,1,0:T(8,128)S(1)}, f32[8,16,512]{2,1,0:T(8,128)}, u32[]{:S(2)}) copy-start(f32[8,16,512]{2,1,0:T(8,128)} %get-tuple-element.219) | copy-start | bytes 786436
  182.4 2.9 %copy-start.13 = (f32[5,8,1,512]{3,2,1,0:T(1,128)S(1)}, f32[5,8,1,512]{3,2,1,0:T(1,128)}, u32[]{:S(2)}) copy-start(f32[5,8,1,512]{3,2,1,0:T(1,128)} %copy.140) | copy-start | bytes 245764
  182.4 2.9 %copy-start.15 = (f32[5,8,1,512]{3,2,1,0:T(1,128)S(1)}, f32[5,8,1,512]{3,2,1,0:T(1,128)}, u32[]{:S(2)}) copy-start(f32[5,8,1,512]{3,2,1,0:T(1,128)} %copy.141) | copy-start | bytes 245764
  182.4 2.9 %copy-start.30 = (f32[16]{0:T(128)S(1)}, f32[16]{0:T(128)}, u32[]{:S(2)}) copy-start(f32[16]{0:T(128)} %param.18) | copy-start | bytes 196
  (22 other events, 38.2 us)
where the time goes:
time: 192 us; the launch traced here: 190 us
  local copies, waits for them, and re-layouts  61.2 us (32%)
  other arithmetic  49.6 us (26%)
  blocking collectives  46.1 us (24%)
  starting transfers between devices  25.4 us (13%)
  matrix products  5.41 us (3%)
  waiting for transfers between devices  2.21 us (1%)
    all_gather x2, blocking collectives, advance(): lax.all_gather(state[:, :, rows - 1, :], 'lon', axis=2, tiled=True)  32.3 us
    unnamed x17, other arithmetic  18.6 us
    unnamed x79, local copies, waits for them, and re-layouts  13.9 us
    all_gather x2, blocking collectives, carried_in(): everything = lax.all_gather(value, axis)  13.8 us
    all_gather x2, local copies, waits for them, and re-layouts, advance(): lax.all_gather(state[:, :, rows - 1, :], 'lon', axis=2, tiled=True)  11.7 us
    gather x2, local copies, waits for them, and re-layouts, advance(): mirrored = jnp.take(whole_top, partner, axis=2) * signs[:, None, None]  11.3 us
    ppermute x4, starting transfers between devices, padded(): after = lax.ppermute(initial, axis, down)  8.54 us
    broadcast_in_dim x2, other arithmetic, advance(): north_edge[:, :, None, :]  8.38 us
  transfers between devices with their start and end apart: 10, of which 1 were waited for; matrix products, arithmetic and copies ran while one was open for 37% of the time, Pallas kernels for 0%

commit v1 on v0

v1 whole, which is shorter than its diff:
```python
import functools

import jax
import jax.numpy as jnp
from jax import lax
from jax.experimental import pallas as pl
from jax.experimental.pallas import tpu as pltpu
from jax.sharding import PartitionSpec as P

ALPHA = 0.2
BETA = 0.15
PRESS = 0.1
VISCOUS = 0.1
DIFFUSE = 0.1
ADVECT = 0.1

F32 = jnp.float32
I32 = jnp.int32
LANES = 128
DEEP = 8
FAR = 64
WET = 48
SLABS = 11
CORNERS = SLABS
VMEM_BYTES = 24 * 1024 * 1024
PREPARE_BYTES = 58 * 1024 * 1024

VMEM = pl.BlockSpec(memory_space=pltpu.VMEM)
SMEM = pl.BlockSpec(memory_space=pltpu.SMEM)
ANY = pl.BlockSpec(memory_space=pl.ANY)
HBM = pl.BlockSpec(memory_space=pltpu.HBM)


def iota(shape, dim):
    return lax.broadcasted_iota(I32, shape, dim)


def roll(value, shift, axis):
    return pltpu.roll(value, shift % value.shape[axis], axis)


def call(kernel, out_shape, in_specs, args, scratch=(), name=None, vmem=VMEM_BYTES):
    return pl.pallas_call(
        kernel,
        out_shape=out_shape,
        in_specs=in_specs,
        out_specs=jax.tree.map(lambda _: VMEM, out_shape),
        scratch_shapes=list(scratch),
        compiler_params=pltpu.CompilerParams(vmem_limit_bytes=vmem),
        name=name,
    )(*args)


def after(values, *others):
    return lax.optimization_barrier((values, others))[0]


def shape(*dims):
    return jax.ShapeDtypeStruct(dims, F32)


def prepare_kernel(
    n_lon, n_lat, state_hbm, mask_hbm, tiles_hbm, owner_hbm, row_hbm, partner_hbm, keep_ref, send_ref, west_ref, east_ref,
    top_ref, state_ref, mask_ref, x_ref, owners_ref, rows_ref, hinge_ref, sem,
):
    tiles, cols = tiles_hbm.shape[1], tiles_hbm.shape[2]
    half_cols = cols // 2
    rows = 2 * DEEP
    n_y = n_lat // 2
    half = lax.axis_index("lev")
    lat = lax.axis_index("lat")
    core = lax.rem(lat, 2)
    begin = pl.multiple_of(half * half_cols, LANES)
    indices = [
        pltpu.make_async_copy(owner_hbm, owners_ref, sem.at[0]),
        pltpu.make_async_copy(row_hbm, rows_ref, sem.at[1]),
        pltpu.make_async_copy(partner_hbm, hinge_ref, sem.at[2]),
    ]
    fluxes = [
        pltpu.make_async_copy(
            tiles_hbm.at[c, :, pl.ds(begin, half_cols)], x_ref.at[:, pl.ds(c * half_cols, half_cols)], sem.at[3 + c]
        )
        for c in range(3)
    ]
    fields = [
        pltpu.make_async_copy(state_hbm, state_ref, sem.at[6]),
        pltpu.make_async_copy(mask_hbm, mask_ref, sem.at[7]),
    ]
    for copy in indices + fluxes + fields:
        copy.start()
    for copy in indices:
        copy.wait()

    key = owners_ref[...] * rows + rows_ref[...]
    hinge_block = hinge_ref[0] // cols
    slots = keep_ref.shape[0]
    slot = iota((slots, tiles), 0)
    group, sub = slot >> 3, slot & 7
    at_y = (group >> (n_lon.bit_length() - 1)) ^ (lat // 2)
    at_lon = (group & (n_lon - 1)) ^ lax.axis_index("lon")

    def wrapped(lon):
        return jnp.where(lon < 0, lon + n_lon, jnp.where(lon >= n_lon, lon - n_lon, lon))

    def one_hot(hit):
        return jnp.where(hit, 1.0, 0.0).astype(jnp.bfloat16)

    def weights(to_core):
        lat = 2 * at_y + to_core
        owner = at_lon * n_lat + lat
        last = lat == n_lat - 1
        top = n_lat * rows - 1
        south = jnp.where(lat == 0, owner * rows, owner * rows - 1)
        north = jnp.where(last, wrapped(hinge_block - at_lon) * (n_lat * rows) + top, (owner + 1) * rows)
        third = jnp.where(last, wrapped(hinge_block - at_lon - 1) * (n_lat * rows) + top, -1)
        kind = sub >> 1
        extra_key = jnp.where(kind == 0, south, jnp.where(kind == 1, north, jnp.where(kind == 2, third, -1)))
        extra = key == extra_key
        beside = wrapped(at_lon + 1 - 2 * half) * n_lat + lat
        return (
            one_hot(key == owner * rows + sub),
            one_hot(key == owner * rows + DEEP + sub),
            one_hot(extra & ((sub & 1) == 0)),
            one_hot(extra & ((sub & 1) == 1)),
            one_hot(((key >> 4) == beside) & (sub == 6)),
        )

    def split(x):
        first = x.astype(jnp.bfloat16)
        rest = x - first.astype(F32)
        second = rest.astype(jnp.bfloat16)
        third = (rest - second.astype(F32)).astype(jnp.bfloat16)
        return first, second, third

    square = iota((tiles, tiles), 0) == iota((tiles, tiles), 1)
    row_of = jnp.sum(jnp.where(square, (key & (rows - 1)).astype(F32), 0.0), axis=1, keepdims=True).astype(I32)

    for copy in fluxes:
        copy.wait()
    x = x_ref[...]
    lane = iota((tiles, LANES), 1)
    edge = jnp.zeros((tiles, LANES), F32)
    for c in range(3):
        begin = c * half_cols
        value = jnp.where(half == 0, x[:, begin : begin + 1], x[:, begin + half_cols - 1 : begin + half_cols])
        edge = jnp.where(((lane >> 4) == c) & ((lane & 15) == row_of), value, edge)
    parts, edges = split(x), split(edge)
    wide = 3 * half_cols
    quarter = wide // 2

    def dot(hot, terms, begin, end):
        products = [
            jnp.dot(hot, term[:, begin:end], preferred_element_type=F32) for term in reversed(terms)
        ]
        return products[0] + products[1] + products[2]

    for out_ref, to_core in ((keep_ref, core), (send_ref, 1 - core)):
        low, high, even, odd, ring = weights(to_core)
        out_ref[:, 0:wide] = dot(low, parts, 0, wide)
        out_ref[:, wide : 2 * wide] = dot(high, parts, 0, wide)
        rest = dot(even, parts, 0, quarter) + dot(odd, parts, quarter, wide)
        beside = dot(ring, edges, 0, LANES)
        out_ref[:, 2 * wide : 2 * wide + LANES] = rest[:, 0:LANES] + beside
        out_ref[:, 2 * wide + LANES :] = rest[:, LANES:]

    for copy in fields:
        copy.wait()
    edge_rows(state_ref, mask_ref, top_ref, rows, rows - 1, rows - 2)
    edge_columns(state_ref, mask_ref, west_ref, east_ref)


def merge_kernel(kept_ref, got_ref, keep_ref, send_ref):
    half = keep_ref.shape[0]
    send_ref[...] = kept_ref[half:, :] + got_ref[half:, :]
    keep_ref[...] = kept_ref[0:half, :] + got_ref[0:half, :]


def prepare(state, mask, flux_tiles, flux_owner, flux_row, fold_partner, n_lon, n_lat):
    tiles, _, cols = flux_tiles.shape
    wide = 3 * (cols // 2)
    slots = shape(n_lon * n_lat // 2 * DEEP, 2 * wide + wide // 2)
    side = shape(2 * DEEP, LANES)
    return call(
        functools.partial(prepare_kernel, n_lon, n_lat),
        (slots, slots, side, side, shape(SLABS, DEEP, cols)),
        [HBM] * 6,
        (
            state,
            mask,
            flux_tiles.transpose(1, 0, 2),
            flux_owner.reshape(1, tiles),
            flux_row.reshape(1, tiles),
            fold_partner,
        ),
        [
            pltpu.VMEM(state.shape, F32),
            pltpu.VMEM(mask.shape, I32),
            pltpu.VMEM((tiles, wide), F32),
            pltpu.VMEM((1, tiles), I32),
            pltpu.VMEM((1, tiles), I32),
            pltpu.SMEM(fold_partner.shape, I32),
            pltpu.SemaphoreType.DMA((8,)),
        ],
        name="prepare",
        vmem=PREPARE_BYTES,
    )


def level_rows(ref, row, rows):
    return jnp.concatenate([ref[k * rows + row : k * rows + row + 1, :] for k in range(DEEP)], axis=0)


def buoyancy_of(temper, saline):
    return ALPHA * temper - BETA * saline


def edge_rows(state_ref, mask_ref, out_ref, rows, near, far):
    for f in range(5):
        out_ref[2 * f] = level_rows(state_ref.at[f], near, rows)
        out_ref[2 * f + 1] = level_rows(state_ref.at[f], far, rows)
    out_ref[10] = level_rows(mask_ref, near, rows).astype(F32)


def edge_columns(state_ref, mask_ref, west_ref, east_ref):
    rows, cols = west_ref.shape[0], state_ref.shape[2]
    lane = iota((rows, LANES), 1)
    last = slice(cols - LANES, cols)
    west = jnp.zeros((rows, LANES), F32)
    east = jnp.zeros((rows, LANES), F32)
    for k in range(DEEP):
        at = slice(k * rows, (k + 1) * rows)
        for f in range(5):
            to = f * DEEP + k
            left, right = state_ref[f, at, 0:LANES], state_ref[f, at, last]
            west = jnp.where(lane == to, roll(left, to, 1), west)
            west = jnp.where(lane == FAR + to, roll(left, FAR + to - 1, 1), west)
            east = jnp.where(lane == to, roll(right, to + 1, 1), east)
            east = jnp.where(lane == FAR + to, roll(right, FAR + to + 2, 1), east)
        west = jnp.where(lane == WET + k, roll(mask_ref[at, 0:LANES].astype(F32), WET + k, 1), west)
        east = jnp.where(lane == WET + k, roll(mask_ref[at, last].astype(F32), WET + k + 1, 1), east)
    west_ref[...] = west
    east_ref[...] = east


def rows_kernel(state_ref, mask_ref, turn_ref, from_west_ref, from_east_ref, pair_ref, cross_ref):
    rows, cols = from_west_ref.shape[0], state_ref.shape[2]
    odd = lax.rem(lax.axis_index("lat"), 2) == 1

    def fill(out_ref, near, far):
        edge_rows(state_ref, mask_ref, out_ref, rows, near, far)
        out_ref[CORNERS] = jnp.full((DEEP, cols), turn_ref[near], F32)
        out_ref[CORNERS, 0:1, 0:LANES] = from_west_ref[near : near + 1, :]
        out_ref[CORNERS, 1:2, 0:LANES] = from_east_ref[near : near + 1, :]

    @pl.when(odd)
    def _():
        fill(pair_ref, 0, 1)
        fill(cross_ref, rows - 1, rows - 2)

    @pl.when(jnp.logical_not(odd))
    def _():
        fill(pair_ref, rows - 1, rows - 2)
        fill(cross_ref, 0, 1)


def around(value, west, east, south, north):
    rows, cols = value.shape
    row, col = iota((rows, cols), 0), iota((rows, cols), 1)
    return (
        jnp.where(col == cols - 1, east, roll(value, -1, 1)),
        jnp.where(col == 0, west, roll(value, 1, 1)),
        jnp.where(row == rows - 1, north, roll(value, -1, 0)),
        jnp.where(row == 0, south, roll(value, 1, 0)),
    )


def advanced(values, sides, wet, turn, pressed, heat=None):
    zonal, merid = values[0], values[1]
    sums = [(e + w) + (n + s) for e, w, n, s in sides]
    across = [(e - w, n - s) for e, w, n, s in sides]
    press_x, press_y = pressed(
        0.5 * buoyancy_of(across[2][0], across[3][0]), 0.5 * buoyancy_of(across[2][1], across[3][1])
    )
    out = []
    carry_x, carry_y = (0.5 * ADVECT) * zonal, (0.5 * ADVECT) * merid
    for f in range(5):
        spread = (VISCOUS if f < 2 else DIFFUSE) * (sums[f] - 4.0 * values[f])
        if f == 0:
            trend = spread + (turn * merid - press_x)
        elif f == 1:
            trend = spread - (turn * zonal + press_y)
        else:
            trend = spread - (carry_x * across[f][0] + carry_y * across[f][1])
        new = values[f] + wet * trend
        out.append(new if heat is None or f < 2 else new + heat[f - 2])
    return out


class Tiles:
    def __init__(self, grid, west=None, east=None, south=None, north=None):
        self.grid, self.ghosts, self.turned = grid, (west, east, south, north), {}
        self.lane, self.sub = iota((DEEP, LANES), 1), iota((DEEP, LANES), 0)

    def rolled(self, r, j, shift, axis):
        at = (r, j, shift, axis)
        if at not in self.turned:
            self.turned[at] = roll(self.grid[r][j], shift, axis)
        return self.turned[at]

    def side(self, r, j, shift, axis):
        here = self.rolled(r, j, shift, axis)
        r_from, j_from = (r, j - shift) if axis else (r - shift, j)
        edge = (0 if shift == 1 else LANES - 1) if axis else (0 if shift == 1 else DEEP - 1)
        if 0 <= r_from < len(self.grid) and 0 <= j_from < len(self.grid[0]):
            other = self.rolled(r_from, j_from, shift, axis)
        else:
            ghost = self.ghosts[(0 if shift == 1 else 1) + (0 if axis else 2)]
            if ghost is None:
                return here
            other = ghost[r if axis else j]
        return jnp.where((self.lane if axis else self.sub) == edge, other, here)

    def around(self, r, j):
        return self.side(r, j, -1, 1), self.side(r, j, 1, 1), self.side(r, j, -1, 0), self.side(r, j, 1, 0)


def tile(r, j, k, rows):
    return slice(k * rows + r * DEEP, k * rows + (r + 1) * DEEP), slice(j * LANES, (j + 1) * LANES)


def turn_column(turn_ref, rows):
    row = iota((rows, LANES), 0)
    column = jnp.zeros((rows, LANES), F32)
    for j in range(rows):
        column = jnp.where(row == j, turn_ref[j], column)
    return column


def mirrored(value, width):
    back = LANES - 1 - iota((value.shape[0], LANES), 1)
    blocks = [
        jnp.take_along_axis(value[:, begin : begin + LANES], back, axis=1)
        for begin in range(width - LANES, -1, -LANES)
    ]
    return jnp.concatenate(blocks, axis=1)


def scan_down(value):
    row = iota(value.shape, 0)
    for step in (1, 2, 4):
        value = value + jnp.where(row >= step, roll(value, step, 0), 0.0)
    return value


def scan_lanes(value):
    lane = iota(value.shape, 1) & 7
    for step in (1, 2, 4):
        value = value + jnp.where(lane >= step, roll(value, step, 1), 0.0)
    return value


def lanes_between(value, begin, end):
    lane = iota(value.shape, 1)
    return jnp.where((lane >= begin) & (lane < end), value, 0.0)


def buoyancy_sum(column):
    here = lanes_between(buoyancy_of(roll(column, -16, 1), roll(column, -24, 1)), 0, 8)
    return jnp.sum(here, axis=1, keepdims=True)


def interior_kernel(state_ref, mask_ref, turn_ref, share_ref, new_ref, sums_ref):
    rows, cols = sums_ref.shape[0], state_ref.shape[2]
    n_r, n_j = rows // DEEP, cols // LANES
    turn = turn_column(turn_ref, rows)
    grid = [(r, j) for r in range(n_r) for j in range(n_j)]
    zero = jnp.zeros((DEEP, LANES), F32)
    run = {at: [zero] * 5 for at in grid}
    for k in range(DEEP):
        fields = [Tiles([[state_ref[(f, *tile(r, j, k, rows))] for j in range(n_j)] for r in range(n_r)]) for f in range(5)]
        for r, j in grid:
            at = tile(r, j, k, rows)
            above_x, above_y, before, total, absorbed = run[r, j]
            slopes = []

            def pressed(x, y):
                slopes.extend((x, y))
                return PRESS * (above_x + 0.5 * x), PRESS * (above_y + 0.5 * y)

            values = [field.grid[r][j] for field in fields]
            wet = mask_ref[at].astype(F32)
            new = advanced(
                values, [field.around(r, j) for field in fields], wet, turn[r * DEEP : (r + 1) * DEEP, 0:1], pressed
            )
            for f in range(5):
                new_ref[(f, *at)] = new[f]
            run[r, j] = [
                above_x + slopes[0],
                above_y + slopes[1],
                before + buoyancy_of(values[2], values[3]),
                total + buoyancy_of(new[2], new[3]),
                absorbed + wet * share_ref[k],
            ]
    for r, j in grid:
        for kind in range(3):
            at = slice(kind * cols + j * LANES, kind * cols + (j + 1) * LANES)
            sums_ref[r * DEEP : (r + 1) * DEEP, at] = run[r, j][2 + kind]


def rim_kernel(
    n_lon, n_lat, state_ref, mask_ref, turn_ref, share_ref, partner_ref, own_west_ref, own_east_ref,
    from_west_ref, from_east_ref, pair_ref, cross_ref, inside_ref, *refs,
):
    blocks = refs[:n_lon]
    ring_rows_ref, ring_cols_ref, edge_rows_ref, edge_cols_ref, sums_ref, south_ref, north_ref, fold_ref, sem = refs[n_lon:]
    rows, cols = from_west_ref.shape[0], state_ref.shape[2]
    lon, lat = lax.axis_index("lon"), lax.axis_index("lat")
    odd = lax.rem(lat, 2) == 1
    hinge = partner_ref[0]
    hinge_block = hinge // cols
    within = hinge - hinge_block * cols
    at_top = lat == n_lat - 1
    wanted = [lax.rem(2 * lon - hinge_block + offset + 2 * n_lon, n_lon) for offset in (1, 0, -1)]

    @pl.when(at_top)
    def _():
        for place in range(3):
            for d in range(n_lon):

                @pl.when(wanted[place] == d)
                def _(place=place, d=d):
                    pltpu.make_async_copy(blocks[d], fold_ref.at[place], sem.at[place]).start()

    @pl.when(odd)
    def _():
        south_ref[...] = pair_ref[...]

    @pl.when(jnp.logical_not(odd))
    def _():
        north_ref[...] = pair_ref[...]

    @pl.when(jnp.logical_not(odd) & (lat > 0))
    def _():
        south_ref[...] = cross_ref[...]

    @pl.when(odd & (lat < n_lat - 1))
    def _():
        north_ref[...] = cross_ref[...]

    @pl.when(lat == 0)
    def _():
        edge_rows(state_ref, mask_ref, south_ref, rows, 0, 0)
        south_ref[CORNERS] = jnp.full((DEEP, cols), turn_ref[0], F32)
        south_ref[CORNERS, 0:1, 0:LANES] = from_west_ref[0:1, :]
        south_ref[CORNERS, 1:2, 0:LANES] = from_east_ref[0:1, :]

    sub8, lane8 = iota((DEEP, LANES), 0), iota((DEEP, LANES), 1)

    @pl.when(at_top)
    def _():
        for place in range(3):
            pltpu.make_async_copy(blocks[0], fold_ref.at[place], sem.at[place]).wait()
        west = jnp.zeros((DEEP, LANES), F32)
        east = jnp.zeros((DEEP, LANES), F32)
        for slab in range(SLABS):
            row = jnp.concatenate([fold_ref[0, slab], fold_ref[1, slab], fold_ref[2, slab]], axis=1)
            row = pltpu.roll(row, 3 * cols - 1 - within, 1)
            if slab < 4:
                row = -row
            north_ref[slab] = mirrored(row, cols)
            if slab < 10 and slab % 2 == 0:
                here = lane8 == (slab // 2) * DEEP + sub8
                west = jnp.where(here, row[:, cols : cols + 1], west)
                east = jnp.where(here, row[:, 3 * cols - 1 :], east)
        north_ref[CORNERS] = jnp.full((DEEP, cols), turn_ref[rows - 1], F32)
        north_ref[CORNERS, 0:1, 0:LANES] = jnp.sum(west, axis=0, keepdims=True)
        north_ref[CORNERS, 1:2, 0:LANES] = jnp.sum(east, axis=0, keepdims=True)

    tail = slice(3 * cols, 3 * cols + LANES)
    sums_ref[rows:, :] = jnp.zeros((DEEP, sums_ref.shape[1]), F32)
    sums_ref[0:rows, 0 : 3 * cols] = inside_ref[...]

    share_down = jnp.zeros((DEEP, LANES), F32)
    for k in range(DEEP):
        share_down = jnp.where(sub8 == k, share_ref[k], share_down)

    def down(line, f):
        return jnp.sum(jnp.where(lane8 == f * DEEP + sub8, line, 0.0), axis=1, keepdims=True)

    def pressed_rows(x, y):
        return PRESS * (scan_down(x) - 0.5 * x), PRESS * (scan_down(y) - 0.5 * y)

    def row_step(near, south, north, west_line, east_line, wet, turn):
        col = iota((DEEP, cols), 1)
        sides = [
            (
                jnp.where(col == cols - 1, down(east_line, f), roll(near[f], -1, 1)),
                jnp.where(col == 0, down(west_line, f), roll(near[f], 1, 1)),
                north[f],
                south[f],
            )
            for f in range(5)
        ]
        return advanced(near, sides, wet, turn, pressed_rows)

    for side, ghost_ref, edge, inner in ((0, south_ref, 0, 1), (1, north_ref, rows - 1, rows - 2)):
        near = [ghost_ref[2 * f] for f in range(5)]
        far = [ghost_ref[2 * f + 1] for f in range(5)]
        own = [level_rows(state_ref.at[f], edge, rows) for f in range(5)]
        own_next = [level_rows(state_ref.at[f], inner, rows) for f in range(5)]
        ring_wet = ghost_ref[10]
        corners = ghost_ref[CORNERS, :, 0:LANES]
        south, north = (far, own) if side == 0 else (own, far)
        ring = row_step(near, south, north, corners[0:1, :], corners[1:2, :], ring_wet, corners[2:3, 0:1])
        south, north = (near, own_next) if side == 0 else (own_next, near)
        wet = level_rows(mask_ref, edge, rows).astype(F32)
        edge_line = slice(edge, edge + 1)
        new = row_step(own, south, north, from_west_ref[edge_line, :], from_east_ref[edge_line, :], wet, turn_ref[edge])
        for f in range(5):
            edge_rows_ref[side, f] = new[f]
            ring_rows_ref[side, f] = jnp.where(lat == 0, new[f], ring[f]) if side == 0 else ring[f]
        ring_rows_ref[side, 5] = ring_wet
        at = slice(rows + side, rows + side + 1)
        below = slice(rows + 2 + side, rows + 3 + side)
        sums_ref[at, 0:cols] = jnp.sum(buoyancy_of(near[2], near[3]), axis=0, keepdims=True)
        sums_ref[below, 0:cols] = jnp.sum(buoyancy_of(far[2], far[3]), axis=0, keepdims=True)
        here = buoyancy_of(ring_rows_ref[side, 2], ring_rows_ref[side, 3])
        sums_ref[at, cols : 2 * cols] = jnp.sum(here, axis=0, keepdims=True)
        sums_ref[at, 2 * cols : 3 * cols] = jnp.sum(ring_wet * share_down[:, 0:1], axis=0, keepdims=True)
        corner_sums = buoyancy_sum(corners)
        for at_col in range(2):
            sums_ref[at, 3 * cols + at_col : 3 * cols + at_col + 1] = corner_sums[at_col : at_col + 1, :]

    row, lane = iota((rows, LANES), 0), iota((rows, LANES), 1)
    turn = turn_column(turn_ref, rows)
    share_lanes = jnp.zeros((rows, LANES), F32)
    for k in range(DEEP):
        share_lanes = jnp.where((lane & 7) == k, share_ref[k], share_lanes)

    def column_step(near, east, west, north, south):
        dx, dy = 0.5 * (east - west), 0.5 * (north - south)
        lap = (east + west) + (north + south) - 4.0 * near
        zonal, merid = lanes_between(near, 0, 8), lanes_between(near, 8, 16)
        wet = lanes_between(near, WET, WET + 8)
        wet_all = sum(roll(wet, -8 * n, 1) for n in range(2, 7))
        zonal_all = sum(roll(zonal, 8 * n, 1) for n in (2, 3, 4))
        merid_all = sum(roll(merid, 8 * n, 1) for n in (1, 2, 3))
        bx = lanes_between(buoyancy_of(roll(dx, -16, 1), roll(dx, -24, 1)), 0, 8)
        by = lanes_between(buoyancy_of(roll(dy, -8, 1), roll(dy, -16, 1)), 8, 16)
        press_x, press_y = PRESS * (scan_lanes(bx) - 0.5 * bx), PRESS * (scan_lanes(by) - 0.5 * by)
        trend = VISCOUS * lap - ADVECT * (zonal_all * dx + merid_all * dy) - press_x - press_y
        trend = trend + lanes_between(turn * roll(near, -8, 1), 0, 8) - lanes_between(turn * roll(near, 8, 1), 8, 16)
        return near + wet_all * trend, wet

    block = jnp.zeros((rows, LANES), F32)
    sides = ((0, from_west_ref, own_west_ref), (1, from_east_ref, own_east_ref))
    for side, ghost_ref, own_ref in sides:
        near, own = ghost_ref[...], own_ref[...]
        far, own_next = roll(near, -FAR, 1), roll(own, -FAR, 1)
        north = jnp.where(row == rows - 1, north_ref[CORNERS, side : side + 1, 0:LANES], roll(near, -1, 0))
        south = jnp.where(row == 0, south_ref[CORNERS, side : side + 1, 0:LANES], roll(near, 1, 0))
        east, west = (own, far) if side == 0 else (far, own)
        new, wet = column_step(near, east, west, north, south)
        ring_cols_ref[side] = new
        found = (buoyancy_sum(near), buoyancy_sum(far), buoyancy_sum(new), jnp.sum(wet * share_lanes, axis=1, keepdims=True))
        for kind in range(4):
            block = jnp.where(lane == 2 * kind + side, found[kind], block)
        east, west = (own_next, near) if side == 0 else (near, own_next)
        new, _ = column_step(own, east, west, roll(own, -1, 0), roll(own, 1, 0))
        edge_cols_ref[side] = new
        column = cols if side == 0 else 2 * cols - 1
        sums_ref[0:rows, column : column + 1] = buoyancy_sum(new)
    sums_ref[0:rows, tail] = block
    for side, edge in ((0, 0), (1, rows - 1)):
        here = buoyancy_of(edge_rows_ref[side, 2], edge_rows_ref[side, 3])
        sums_ref[edge : edge + 1, cols : 2 * cols] = jnp.sum(here, axis=0, keepdims=True)


def last_kernel(
    n_lon, n_lat, state_ref, mask_ref, ring_rows_ref, ring_cols_ref, edge_rows_ref, edge_cols_ref, sums_ref, mine_ref,
    theirs_ref, turn_ref, share_ref, partner_ref, out_ref,
):
    rows, cols = mask_ref.shape[0] // DEEP, mask_ref.shape[1]
    n_r, n_j = rows // DEEP, cols // LANES
    half_cols = cols // 2
    wide = 3 * half_cols
    mine, theirs = mine_ref[...], theirs_ref[...]
    first = lax.axis_index("lev") == 0
    halves = (jnp.where(first, mine, theirs), jnp.where(first, theirs, mine))
    lat = lax.axis_index("lat")
    at_top, at_bottom = lat == n_lat - 1, lat == 0
    hinge = partner_ref[0]
    within = hinge - (hinge // cols) * cols

    def extra(kind, c):
        found = []
        for part in halves:
            line = jnp.concatenate(
                [part[2 * kind : 2 * kind + 1, 2 * wide :], part[2 * kind + 1 : 2 * kind + 2, 2 * wide :]], axis=1
            )
            found.append(line[:, c * half_cols : (c + 1) * half_cols])
        return jnp.concatenate(found, axis=1)

    flux, flux_south, flux_north, flux_west, flux_east = [], [], [], [], []
    sub8 = iota((DEEP, LANES), 0)
    lane8 = iota((DEEP, LANES), 1)
    crossed = jnp.zeros((DEEP, 2 * cols), F32)
    for c in range(3):
        pair = jnp.concatenate([extra(2, c), extra(1, c)], axis=1)
        crossed = jnp.where(iota(crossed.shape, 0) == c, pair, crossed)
    crossed = mirrored(pltpu.roll(crossed, 2 * cols - 1 - within, 1), cols)
    row, lane = iota((rows, LANES), 0), iota((rows, LANES), 1)
    for c in range(3):
        bands = [
            jnp.concatenate([part[:, b * wide + c * half_cols : b * wide + (c + 1) * half_cols] for part in halves], axis=1)
            for b in range(2)
        ]
        flux.append(jnp.concatenate(bands, axis=0))
        flux_south.append(extra(0, c))
        flux_north.append(jnp.where(at_top, crossed[c : c + 1, :], extra(1, c)))
        here = lane == c * 16 + row
        for side, part in ((flux_west, halves[1]), (flux_east, halves[0])):
            line = part[6:7, 2 * wide : 2 * wide + LANES]
            side.append(jnp.sum(jnp.where(here, line, 0.0), axis=1, keepdims=True))

    turn = turn_column(turn_ref, rows)
    share_down = jnp.zeros((DEEP, LANES), F32)
    share_lanes = jnp.zeros((rows, LANES), F32)
    for k in range(DEEP):
        share_down = jnp.where(sub8 == k, share_ref[k], share_down)
        share_lanes = jnp.where((lane & 7) == k, share_ref[k], share_lanes)

    shallow = sums_ref[0:rows, 0:cols]
    tail = sums_ref[:, 3 * cols : 3 * cols + LANES]
    shallow_rows = [sums_ref[rows + n : rows + n + 1, 0:cols] for n in range(4)]
    east, west, north, south = around(shallow, tail[0:rows, 0:1], tail[0:rows, 1:2], shallow_rows[0], shallow_rows[1])
    half_press = 0.5 * PRESS
    push_x, push_y = half_press * (east - west), half_press * (north - south)
    col_row = iota((1, cols), 1)
    push_rows, push_cols = [], []
    for side in range(2):
        near, far = shallow_rows[side], shallow_rows[2 + side]
        west = jnp.where(col_row == 0, tail[rows + side : rows + side + 1, 0:1], roll(near, 1, 1))
        east = jnp.where(col_row == cols - 1, tail[rows + side : rows + side + 1, 1:2], roll(near, -1, 1))
        inner = shallow[0:1, :] if side == 0 else shallow[rows - 1 :, :]
        rise = inner - far if side == 0 else far - inner
        along, across = half_press * (east - west), half_press * rise
        if side == 0:
            along = jnp.where(at_bottom, push_x[0:1, :], along)
            across = jnp.where(at_bottom, push_y[0:1, :], across)
        push_rows.append((along, across))
    for side in range(2):
        near = jnp.broadcast_to(tail[0:rows, side : side + 1], (rows, LANES))
        far = tail[0:rows, 2 + side : 3 + side]
        inner = shallow[:, 0:1] if side == 0 else shallow[:, cols - 1 :]
        north = jnp.where(row == rows - 1, tail[rows + 1 : rows + 2, side : side + 1], roll(near, -1, 0))
        south = jnp.where(row == 0, tail[rows : rows + 1, side : side + 1], roll(near, 1, 0))
        push_cols.append((half_press * (inner - far if side == 0 else far - inner), half_press * (north - south)))

    ring_rows, above_rows = [], []
    for side, source in ((0, flux_south), (1, flux_north)):
        at = slice(rows + side, rows + side + 1)
        wet = ring_rows_ref[side, 5]
        taken = wet * share_down[:, 0:1]
        values = [ring_rows_ref[side, f] - wet * push_rows[side][f] for f in range(2)]
        values += [ring_rows_ref[side, 2 + c] + taken * source[c] for c in range(3)]
        ring_rows.append(values)
        above_rows.append(
            sums_ref[at, cols : 2 * cols] + sums_ref[at, 2 * cols : 3 * cols] * buoyancy_of(source[0], source[1])
        )
    ring_cols, above_cols = [], []
    for side, source in ((0, flux_west), (1, flux_east)):
        found = ring_cols_ref[side]
        wet = lanes_between(found, WET, WET + 8)
        taken = wet * share_lanes
        found = found - roll(wet, -WET, 1) * push_cols[side][0] - roll(wet, 8 - WET, 1) * push_cols[side][1]
        for c in range(3):
            found = found + roll(taken, 8 * (2 + c) - WET, 1) * source[c]
        ring_cols.append(found)
        above_cols.append(tail[0:rows, 4 + side : 5 + side] + tail[0:rows, 6 + side : 7 + side] * buoyancy_of(source[0], source[1]))
    above = sums_ref[0:rows, cols : 2 * cols] + sums_ref[0:rows, 2 * cols : 3 * cols] * buoyancy_of(flux[0], flux[1])
    east, west, north, south = around(above, above_cols[0], above_cols[1], above_rows[0], above_rows[1])
    above_x, above_y = 0.5 * (east - west), 0.5 * (north - south)

    grid = [(r, j) for r in range(n_r) for j in range(n_j)]

    def cut(value, r, j):
        return value[r * DEEP : (r + 1) * DEEP, j * LANES : (j + 1) * LANES]

    run = {at: (cut(above_x, *at), cut(above_y, *at)) for at in grid}
    edge_cols = [edge_cols_ref[side] for side in range(2)]

    def column(value, r, n):
        return jnp.broadcast_to(value[r * DEEP : (r + 1) * DEEP, n : n + 1], (DEEP, LANES))

    for k in range(DEEP):
        wets, heats, grids = {}, {}, [[[None] * n_j for _ in range(n_r)] for _ in range(5)]
        for r, j in grid:
            at = tile(r, j, k, rows)
            wet = mask_ref[at].astype(F32)
            taken = wet * share_ref[k]
            wets[r, j] = wet
            heats[r, j] = [taken * cut(flux[c], r, j) for c in range(3)]
            for f in range(5):
                value = state_ref[(f, *at)]
                if j == 0:
                    value = jnp.where(lane8 == 0, column(edge_cols[0], r, f * DEEP + k), value)
                if j == n_j - 1:
                    value = jnp.where(lane8 == LANES - 1, column(edge_cols[1], r, f * DEEP + k), value)
                if r == 0:
                    value = jnp.where(sub8 == 0, edge_rows_ref[0, f, k : k + 1, at[1]], value)
                if r == n_r - 1:
                    value = jnp.where(sub8 == DEEP - 1, edge_rows_ref[1, f, k : k + 1, at[1]], value)
                if f < 2:
                    value = value - wet * cut((push_x, push_y)[f], r, j)
                else:
                    value = value + heats[r, j][f - 2]
                grids[f][r][j] = value
        fields = [
            Tiles(
                grids[f],
                [column(ring_cols[0], r, f * DEEP + k) for r in range(n_r)],
                [column(ring_cols[1], r, f * DEEP + k) for r in range(n_r)],
                [ring_rows[0][f][k : k + 1, j * LANES : (j + 1) * LANES] for j in range(n_j)],
                [ring_rows[1][f][k : k + 1, j * LANES : (j + 1) * LANES] for j in range(n_j)],
            )
            for f in range(5)
        ]
        for r, j in grid:
            at = tile(r, j, k, rows)
            over_x, over_y = run[r, j]

            def pressed(x, y):
                run[r, j] = (over_x + x, over_y + y)
                return PRESS * (over_x + 0.5 * x), PRESS * (over_y + 0.5 * y)

            new = advanced(
                [field.grid[r][j] for field in fields],
                [field.around(r, j) for field in fields],
                wets[r, j],
                turn[r * DEEP : (r + 1) * DEEP, 0:1],
                pressed,
                heats[r, j],
            )
            for f in range(5):
                out_ref[(f, *at)] = new[f]


def body(n_lon, n_lat, state, mask, coriolis, penetration, flux_tiles, flux_owner, flux_row, fold_partner):
    fields, levels, rows, cols = state.shape
    flat_state = state.reshape(fields, levels * rows, cols)
    flat_mask = mask.reshape(levels * rows, cols)
    last = n_lat - 1

    def across(d):
        return [(a * n_lat + last, (a + d) % n_lon * n_lat + last) for a in range(n_lon)]

    keep, send, west, east, top = prepare(
        flat_state, flat_mask, flux_tiles, flux_owner, flux_row, fold_partner, n_lon, n_lat
    )

    stages = []
    for axis, size, least in (("lat", n_lat, 2), ("lon", n_lon, 1)):
        bit = size // 2
        while bit >= least:
            stages.append((axis, size, bit))
            bit //= 2
    got = lax.ppermute(send, "lat", [(i, i ^ 1) for i in range(n_lat)])

    def merged(keep, got):
        half = shape(keep.shape[0] // 2, keep.shape[1])
        return call(merge_kernel, (half, half), [VMEM] * 2, (keep, got), name="merge_flux")

    def passed_on(send, stage):
        axis, size, bit = stage
        return lax.ppermute(send, axis, [(i, i ^ bit) for i in range(size)])

    keep, send = merged(keep, got)
    got = passed_on(send, stages[0])

    west, east, top = after((west, east, top), send)
    from_west = lax.ppermute(east, "lon", [(i, (i + 1) % n_lon) for i in range(n_lon)])
    from_east = lax.ppermute(west, "lon", [((i + 1) % n_lon, i) for i in range(n_lon)])
    folded = {d: lax.ppermute(top, ("lon", "lat"), across(d)) for d in (1, n_lon - 1)}
    message = shape(SLABS + 1, DEEP, cols)
    pair, cross = call(
        rows_kernel,
        (message, message),
        [VMEM, VMEM, SMEM, VMEM, VMEM],
        (flat_state, flat_mask, coriolis, from_west, from_east),
        name="edge_rows",
    )
    keep = after(keep, (pair, cross, folded))
    keep, send = merged(keep, got)
    got = passed_on(send, stages[1])

    pair, cross, top = after((pair, cross, top), send)
    folded.update({d: lax.ppermute(top, ("lon", "lat"), across(d)) for d in range(2, n_lon - 1)})
    from_pair = lax.ppermute(pair, "lat", [(i, i ^ 1) for i in range(n_lat)])
    from_cross = lax.ppermute(cross, "lat", [(i, i + 1 if i % 2 else i - 1) for i in range(1, last)])
    keep = after(keep, (from_pair, from_cross, folded))
    for stage in stages[2:]:
        keep, send = merged(keep, got)
        got = passed_on(send, stage)

    near_state, near_mask = after((flat_state, flat_mask), send)
    new_state, inside = call(
        interior_kernel,
        (shape(fields, levels * rows, cols), shape(rows, 3 * cols)),
        [VMEM, VMEM, SMEM, SMEM],
        (near_state, near_mask, coriolis, penetration),
        name="first_inside",
    )
    keep = after(keep, inside)
    mine = keep + got
    theirs = lax.ppermute(mine, "lev", [(0, 1), (1, 0)])

    inside = after(inside, mine)
    ring = (shape(2, 6, DEEP, cols), shape(2, rows, LANES), shape(2, 5, DEEP, cols), shape(2, rows, LANES))
    blocks = [top] + [folded[d] for d in range(1, n_lon)]
    *ring, sums = call(
        functools.partial(rim_kernel, n_lon, n_lat),
        (*ring, shape(rows + DEEP, 3 * cols + LANES)),
        [VMEM, VMEM, SMEM, SMEM, SMEM] + [VMEM] * 7 + [ANY] * n_lon,
        (
            flat_state, flat_mask, coriolis, penetration, fold_partner, west, east, from_west, from_east, from_pair,
            from_cross, inside, *blocks,
        ),
        [
            pltpu.VMEM((SLABS + 1, DEEP, cols), F32),
            pltpu.VMEM((SLABS + 1, DEEP, cols), F32),
            pltpu.VMEM((3, SLABS, DEEP, cols), F32),
            pltpu.SemaphoreType.DMA((3,)),
        ],
        name="first_rim",
    )
    sums = lax.ppermute(sums, "lev", [(0, 1)])

    out = call(
        functools.partial(last_kernel, n_lon, n_lat),
        shape(fields, levels * rows, cols),
        [VMEM] * 9 + [SMEM] * 3,
        (new_state, flat_mask, *ring, sums, mine, theirs, coriolis, penetration, fold_partner),
        name="last_substep",
    )
    return out.reshape(fields, levels, rows, cols)


def solution(mesh):
    n_lon, n_lat = mesh.shape["lon"], mesh.shape["lat"]
    assert mesh.shape["lev"] == 2 and n_lat % 2 == 0 and n_lon > 2
    return jax.shard_map(
        functools.partial(body, n_lon, n_lat),
        mesh=mesh,
        in_specs=(
            P(None, "lev", "lat", "lon"),
            P("lev", "lat", "lon"),
            P("lat"),
            P("lev"),
            P(("lon", "lat"), None, None),
            P(("lon", "lat"), None),
            P(("lon", "lat")),
            P(),
        ),
        out_specs=P(None, "lev", "lat", "lon"),
        check_vma=False,
    )
```

time: 192 us -> 55.3 us (0.29)
  local copies, waits for them, and re-layouts: 61.2 us -> 1.07 us
  other arithmetic: 49.6 us -> 0.01 us
  blocking collectives: 46.1 us -> 0 us
  waiting for transfers between devices: 2.21 us -> 21.2 us
  Pallas kernels: 0 us -> 12.2 us
  starting transfers between devices: 25.4 us -> 19.5 us
  matrix products: 5.41 us -> 0 us
    all_gather x4 -> x0, blocking collectives: 46.1 us -> none  [the longest x2 32.3 us: advance(): lax.all_gather(state[:, :, rows - 1, :], 'lon', axis=2, tiled=True)]
    ppermute x8 -> x13, waiting for transfers between devices: 2.21 us -> 21.2 us  [the longest x3 8.12 us: passed_on(): return lax.ppermute(send, axis, [(i, i ^ bit) for i in range(size)])]
    unnamed x17 -> x0, other arithmetic: 18.6 us -> none
    unnamed x79 -> x18, local copies, waits for them, and re-layouts: 13.9 us -> 1.07 us
    pallas_call x0 -> x8, Pallas kernels: none -> 12.2 us  [call(): pl.pallas_call(kernel, out_shape=out_shape, in_specs=in_specs, out_specs=...]
    all_gather x2 -> x0, local copies, waits for them, and re-layouts: 11.7 us -> none  [advance(): lax.all_gather(state[:, :, rows - 1, :], 'lon', axis=2, tiled=True)]
    gather x2 -> x0, local copies, waits for them, and re-layouts: 11.3 us -> none  [advance(): mirrored = jnp.take(whole_top, partner, axis=2) * signs[:, None, None]]
    all_to_all x2 -> x0, starting transfers between devices: 10.1 us -> none  [the longest x1 5.56 us: receive_flux(): lax.all_to_all(packed.reshape(owners, capacity, 3 * cols), ('lon', 'lat')...]
  transfers between devices with their start and end apart: 10 -> 13, of which waited for: 1 -> 6; matrix products, arithmetic and copies ran while one was open for 37% -> 0% of each run, Pallas kernels for 0% -> 4%
where the time goes in v1:
time: 55.3 us; the launch traced here: 54.2 us
  waiting for transfers between devices  21.2 us (38%)
  starting transfers between devices  19.5 us (35%)
  Pallas kernels  12.2 us (22%)
  local copies, waits for them, and re-layouts  1.07 us (2%)
    pallas_call x8, Pallas kernels, call(): pl.pallas_call(kernel, out_shape=out_shape, in_specs=in_specs, out_specs=...  12.2 us
    ppermute x3, waiting for transfers between devices, passed_on(): return lax.ppermute(send, axis, [(i, i ^ bit) for i in range(size)])  8.12 us
    ppermute x1, starting transfers between devices, body(): from_pair = lax.ppermute(pair, 'lat', [(i, i ^ 1) for i in range(n_lat)])  6.4 us
    ppermute x1, waiting for transfers between devices, body(): theirs = lax.ppermute(mine, 'lev', [(0, 1), (1, 0)])  5.31 us
    ppermute x1, waiting for transfers between devices, body(): lax.ppermute(cross, 'lat', [(i, i + 1 if i % 2 else i - 1) for i in range...  3.73 us
    ppermute x1, starting transfers between devices, body(): theirs = lax.ppermute(mine, 'lev', [(0, 1), (1, 0)])  2.71 us
    ppermute x1, starting transfers between devices, body(): lax.ppermute(west, 'lon', [((i + 1) % n_lon, i) for i in range(n_lon)])  2.25 us
    ppermute x1, waiting for transfers between devices, body(): got = lax.ppermute(send, 'lat', [(i, i ^ 1) for i in range(n_lat)])  2.06 us
  transfers between devices with their start and end apart: 13, of which 6 were waited for; matrix products, arithmetic and copies ran while one was open for 0% of the time, Pallas kernels for 4%

profile of v1, /device:TPU:6, one launch (start us, length us, event | category | flops | bytes accessed | tf_op | source)
XLA Modules:
  0.0 54.2 jit_solution(7209089016263791772)
XLA Ops:
  0.0 3.3 %prepare.1 = (f32[64,1920]{1,0:T(8,128)}, f32[64,1920]{1,0:T(8,128)}, f32[16,128]{1,0:T(8,128)}, f32[16,128]{1,0:T(8,128)}, f32[11,8,512]{2,1,0:T(8,128)}) custom-call(f32[5,128,512]{2,1,0:T(8,128)} %bitcast.6, s32[128,512]{1,0:T(8,128)} %bitcast.10, f32[3,128,512]{2,1,0:T(8,128)} %bitcast.15, s32[1,128]{1,0:T(1,128)} %bitcast.16, s32[1,128]{1,0:T(1,128)} %bitcast.17, ...), custom_call_target="tpu_custom_call" | custom-call | tf_op jit(solution)/shard_map/prepare/pallas_call | solution.py:43
  3.4 2.1 %collective-permute-done.got_ref = f32[64,1920]{1,0:T(8,128)S(1)} collective-permute-done((f32[64,1920]{1,0:T(8,128)}, f32[64,1920]{1,0:T(8,128)S(1)}, u32[]{:S(2)}, u32[]{:S(2)}) %collective-permute-start) | collective-permute-done | bytes 491552 | tf_op jit(solution)/shard_map/ppermute | solution.py:768
  5.5 1.0 %copy-done.2 = f32[64,1920]{1,0:T(8,128)S(1)} copy-done((f32[64,1920]{1,0:T(8,128)S(1)}, f32[64,1920]{1,0:T(8,128)}, u32[]{:S(2)}) %copy-start.2) | copy-done | bytes 491544
  6.6 0.6 %collective-permute-start.5 = (f32[32,1920]{1,0:T(8,128)S(1)}, f32[32,1920]{1,0:T(8,128)S(1)}, u32[]{:S(2)}, u32[]{:S(2)}) collective-permute-start(f32[32,1920]{1,0:T(8,128)S(1)} %get-tuple-element.43), channel_id=1, source_target_pairs={{0,4},{2,6},{4,0},{6,2},{1,5},{3,7},{5,1},{7,3},{8,12},{10,14},{12... | collective-permute-start | bytes 737288 | tf_op jit(solution)/shard_map/ppermute | solution.py:776
  7.2 0.7 %collective-permute-start.4 = (f32[11,8,512]{2,1,0:T(8,128)}, f32[11,8,512]{2,1,0:T(8,128)S(1)}, u32[]{:S(2)}, u32[]{:S(2)}) collective-permute-start(f32[11,8,512]{2,1,0:T(8,128)} %get-tuple-element.54.refs_0_), channel_id=1, source_target_pairs={{6,30},{14,6},{22,14},{30,22},{7,31},{15,7},{23,15},{31,23}} | collective-permute-start | bytes 540680 | tf_op jit(solution)/shard_map/ppermute | solution.py:784
  7.8 0.7 %collective-permute-start.3 = (f32[11,8,512]{2,1,0:T(8,128)}, f32[11,8,512]{2,1,0:T(8,128)S(1)}, u32[]{:S(2)}, u32[]{:S(2)}) collective-permute-start(f32[11,8,512]{2,1,0:T(8,128)} %get-tuple-element.54.refs_0_), channel_id=1, source_target_pairs={{6,14},{14,22},{22,30},{30,6},{7,15},{15,23},{23,31},{31,7}} | collective-permute-start | bytes 540680 | tf_op jit(solution)/shard_map/ppermute | solution.py:784
  8.5 1.6 %collective-permute-start.1 = (f32[16,128]{1,0:T(8,128)}, f32[16,128]{1,0:T(8,128)S(1)}, u32[]{:S(2)}, u32[]{:S(2)}) collective-permute-start(f32[16,128]{1,0:T(8,128)} %get-tuple-element.44.own_east_ref), channel_id=1, source_target_pairs={{0,8},{8,16},{16,24},{24,0},{1,9},{9,17},{17,25},{25,1},{2,10},{10... | collective-permute-start | bytes 24584 | tf_op jit(solution)/shard_map/ppermute | solution.py:782
  10.1 2.2 %collective-permute-start.2 = (f32[16,128]{1,0:T(8,128)}, f32[16,128]{1,0:T(8,128)S(1)}, u32[]{:S(2)}, u32[]{:S(2)}) collective-permute-start(f32[16,128]{1,0:T(8,128)} %get-tuple-element.45.own_west_ref), channel_id=1, source_target_pairs={{8,0},{16,8},{24,16},{0,24},{9,1},{17,9},{25,17},{1,25},{10,2},{18... | collective-permute-start | bytes 24584 | tf_op jit(solution)/shard_map/ppermute | solution.py:783
  12.4 1.9 %collective-permute-done.1.from_west_ref = f32[16,128]{1,0:T(8,128)S(1)} collective-permute-done((f32[16,128]{1,0:T(8,128)}, f32[16,128]{1,0:T(8,128)S(1)}, u32[]{:S(2)}, u32[]{:S(2)}) %collective-permute-start.1) | collective-permute-done | bytes 8224 | tf_op jit(solution)/shard_map/ppermute | solution.py:782
  14.4 0.7 %edge_rows.1 = (f32[12,8,512]{2,1,0:T(8,128)S(1)}, f32[12,8,512]{2,1,0:T(8,128)S(1)}) custom-call(f32[5,128,512]{2,1,0:T(8,128)S(1)} %bitcast.7, s32[128,512]{1,0:T(8,128)S(1)} %bitcast.11, f32[16]{0:T(128)S(1)} %copy-done.7, f32[16,128]{1,0:T(8,128)S(1)} %collective-permute-done.1.from_west_ref, f32[16,128]{1,0:T(8,128)S(1)} %collective-permute-done.2.from_east_ref), custom_call_target="tpu_custom_call" | custom-call | tf_op jit(solution)/shard_map/edge_rows/pallas_call | solution.py:43
  15.2 6.4 %collective-permute-start.6 = (f32[12,8,512]{2,1,0:T(8,128)S(1)}, f32[12,8,512]{2,1,0:T(8,128)S(1)}, u32[]{:S(2)}, u32[]{:S(2)}) collective-permute-start(f32[12,8,512]{2,1,0:T(8,128)S(1)} %get-tuple-element.52), channel_id=1, source_target_pairs={{0,2},{2,0},{4,6},{6,4},{1,3},{3,1},{5,7},{7,5},{8,10},{10,8},{12,... | collective-permute-start | bytes 589832 | tf_op jit(solution)/shard_map/ppermute | solution.py:799
  21.6 1.9 %collective-permute-start.7 = (f32[12,8,512]{2,1,0:T(8,128)S(1)}, f32[12,8,512]{2,1,0:T(8,128)S(1)}, u32[]{:S(2)}, u32[]{:S(2)}) collective-permute-start(f32[12,8,512]{2,1,0:T(8,128)S(1)} %get-tuple-element.53), channel_id=1, source_target_pairs={{2,4},{4,2},{3,5},{5,3},{10,12},{12,10},{11,13},{13,11},{18,20},{2... | collective-permute-start | bytes 589832 | tf_op jit(solution)/shard_map/ppermute | solution.py:800
  23.5 0.7 %collective-permute-start.8 = (f32[11,8,512]{2,1,0:T(8,128)S(1)}, f32[11,8,512]{2,1,0:T(8,128)S(1)}, u32[]{:S(2)}, u32[]{:S(2)}) collective-permute-start(f32[11,8,512]{2,1,0:T(8,128)S(1)} %copy-done.3), channel_id=1, source_target_pairs={{6,22},{14,30},{22,6},{30,14},{7,23},{15,31},{23,7},{31,15}} | collective-permute-start | bytes 540680 | tf_op jit(solution)/shard_map/ppermute | solution.py:798
  24.2 0.6 %collective-permute-start.9 = (f32[16,1920]{1,0:T(8,128)S(1)}, f32[16,1920]{1,0:T(8,128)S(1)}, u32[]{:S(2)}, u32[]{:S(2)}) collective-permute-start(f32[16,1920]{1,0:T(8,128)S(1)} %get-tuple-element.51), channel_id=1, source_target_pairs={{0,16},{8,24},{16,0},{24,8},{1,17},{9,25},{17,1},{25,9},{2,18},{10... | collective-permute-start | bytes 368648 | tf_op jit(solution)/shard_map/ppermute | solution.py:776
  24.8 3.7 %collective-permute-done.7.cross_ref = f32[12,8,512]{2,1,0:T(8,128)S(1)} collective-permute-done((f32[12,8,512]{2,1,0:T(8,128)S(1)}, f32[12,8,512]{2,1,0:T(8,128)S(1)}, u32[]{:S(2)}, u32[]{:S(2)}) %collective-permute-start.7) | collective-permute-done | bytes 196640 | tf_op jit(solution)/shard_map/ppermute | solution.py:800
  28.5 5.5 %collective-permute-done.9.got_ref = f32[16,1920]{1,0:T(8,128)S(1)} collective-permute-done((f32[16,1920]{1,0:T(8,128)S(1)}, f32[16,1920]{1,0:T(8,128)S(1)}, u32[]{:S(2)}, u32[]{:S(2)}) %collective-permute-start.9) | collective-permute-done | bytes 122912 | tf_op jit(solution)/shard_map/ppermute | solution.py:776
  34.1 0.1 collective-permute-start.10
  34.2 1.6 %first_inside.1 = (f32[5,128,512]{2,1,0:T(8,128)S(1)}, f32[16,1536]{1,0:T(8,128)S(1)}) custom-call(f32[5,128,512]{2,1,0:T(8,128)S(1)} %bitcast.8, s32[128,512]{1,0:T(8,128)S(1)} %bitcast.12, f32[16]{0:T(128)S(1)} %copy-done.7, f32[8]{0:T(128)S(1)} %copy-done.8), custom_call_target="tpu_custom_call" | custom-call | tf_op jit(solution)/shard_map/first_inside/pallas_call | solution.py:43
  35.8 2.6 %collective-permute-done.10 = f32[8,1920]{1,0:T(8,128)S(1)} collective-permute-done((f32[8,1920]{1,0:T(8,128)S(1)}, f32[8,1920]{1,0:T(8,128)S(1)}, u32[]{:S(2)}, u32[]{:S(2)}) %collective-permute-start.10) | collective-permute-done | bytes 61472 | tf_op jit(solution)/shard_map/ppermute | solution.py:776
  38.4 2.9 %first_rim.1 = (f32[2,6,8,512]{3,2,1,0:T(8,128)S(1)}, f32[2,16,128]{2,1,0:T(8,128)S(1)}, f32[2,5,8,512]{3,2,1,0:T(8,128)S(1)}, f32[2,16,128]{2,1,0:T(8,128)S(1)}, f32[24,1664]{1,0:T(8,128)S(1)}) custom-call(f32[5,128,512]{2,1,0:T(8,128)S(1)} %bitcast.9, s32[128,512]{1,0:T(8,128)S(1)} %bitcast.13, f32[16]{0:T(128)S(1)} %copy-done.7, f32[8]{0:T(128)S(1)} %copy-done.8, ...), custom_call_target="tpu_custom_call" | custom-call | tf_op jit(solution)/shard_map/first_rim/pallas_call | solution.py:43
  41.4 1.3 %collective-permute-start.11 = (f32[24,1664]{1,0:T(8,128)S(1)}, f32[24,1664]{1,0:T(8,128)S(1)}, u32[]{:S(2)}, u32[]{:S(2)}) collective-permute-start(f32[24,1664]{1,0:T(8,128)S(1)} %get-tuple-element.68), channel_id=1, source_target_pairs={{0,1},{2,3},{4,5},{6,7},{8,9},{10,11},{12,13},{14,15},{16,17},{18,... | collective-permute-start | bytes 479240 | tf_op jit(solution)/shard_map/ppermute | solution.py:837
  42.7 2.7 %collective-permute-start.12 = (f32[8,1920]{1,0:T(8,128)S(1)}, f32[8,1920]{1,0:T(8,128)S(1)}, u32[]{:S(2)}, u32[]{:S(2)}) collective-permute-start(f32[8,1920]{1,0:T(8,128)S(1)} %add.3.mine_ref), channel_id=1, source_target_pairs={{0,1},{1,0},{2,3},{3,2},{4,5},{5,4},{6,7},{7,6},{8,9},{9,8},{10,11... | collective-permute-start | bytes 184328 | tf_op jit(solution)/shard_map/ppermute | solution.py:816
  45.4 5.3 %collective-permute-done.12.theirs_ref = f32[8,1920]{1,0:T(8,128)S(1)} collective-permute-done((f32[8,1920]{1,0:T(8,128)S(1)}, f32[8,1920]{1,0:T(8,128)S(1)}, u32[]{:S(2)}, u32[]{:S(2)}) %collective-permute-start.12) | collective-permute-done | bytes 61472 | tf_op jit(solution)/shard_map/ppermute | solution.py:816
  50.7 3.5 %last_substep.1 = f32[5,128,512]{2,1,0:T(8,128)} custom-call(f32[5,128,512]{2,1,0:T(8,128)S(1)} %get-tuple-element.59.state_ref, s32[128,512]{1,0:T(8,128)S(1)} %bitcast.14, f32[2,6,8,512]{3,2,1,0:T(8,128)S(1)} %get-tuple-element.64.ring_rows_ref, f32[2,16,128]{2,1,0:T(8,128)S(1)} %get-tuple-element.65.ring_cols_ref, ...), custom_call_target="tpu_custom_call" | custom-call | tf_op jit(solution)/shard_map/last_substep/pallas_call | solution.py:43
  (29 shorter events, 0.2 us)
Async XLA Ops:
  0.0 14.3 %copy-start = (f32[5,8,16,512]{3,2,1,0:T(8,128)S(1)}, f32[5,8,16,512]{3,2,1,0:T(8,128)}, u32[]{:S(2)}) copy-start(f32[5,8,16,512]{3,2,1,0:T(8,128)} %param.8) | copy-start | bytes 3932164
  0.0 14.3 %copy-start.1 = (s32[8,16,512]{2,1,0:T(8,128)S(1)}, s32[8,16,512]{2,1,0:T(8,128)}, u32[]{:S(2)}) copy-start(s32[8,16,512]{2,1,0:T(8,128)} %param.9) | copy-start | bytes 786436
  0.0 14.3 %copy-start.7 = (f32[16]{0:T(128)S(1)}, f32[16]{0:T(128)}, u32[]{:S(2)}) copy-start(f32[16]{0:T(128)} %turn_ref.7) | copy-start | bytes 196
  3.4 2.1 %collective-permute-start = (f32[64,1920]{1,0:T(8,128)}, f32[64,1920]{1,0:T(8,128)S(1)}, u32[]{:S(2)}, u32[]{:S(2)}) collective-permute-start(f32[64,1920]{1,0:T(8,128)} %get-tuple-element.38), channel_id=1, source_target_pairs={{0,2},{2,0},{4,6},{6,4},{1,3},{3,1},{5,7},{7,5},{8,10},{10,8},{12,... | collective-permute-start | bytes 1474568 | tf_op jit(solution)/shard_map/ppermute | solution.py:768
  5.5 1.0 %copy-start.2 = (f32[64,1920]{1,0:T(8,128)S(1)}, f32[64,1920]{1,0:T(8,128)}, u32[]{:S(2)}) copy-start(f32[64,1920]{1,0:T(8,128)} %get-tuple-element.37.kept_ref) | copy-start | bytes 1474564
  6.5 17.0 %copy-start.3 = (f32[11,8,512]{2,1,0:T(8,128)S(1)}, f32[11,8,512]{2,1,0:T(8,128)}, u32[]{:S(2)}) copy-start(f32[11,8,512]{2,1,0:T(8,128)} %get-tuple-element.54.refs_0_) | copy-start | bytes 540676
  6.6 27.6 %copy-start.8 = (f32[8]{0:T(128)S(1)}, f32[8]{0:T(128)}, u32[]{:S(2)}) copy-start(f32[8]{0:T(128)} %share_ref.5) | copy-start | bytes 100
  6.6 8.5 %collective-permute-start.5 = (f32[32,1920]{1,0:T(8,128)S(1)}, f32[32,1920]{1,0:T(8,128)S(1)}, u32[]{:S(2)}, u32[]{:S(2)}) collective-permute-start(f32[32,1920]{1,0:T(8,128)S(1)} %get-tuple-element.43), channel_id=1, source_target_pairs={{0,4},{2,6},{4,0},{6,2},{1,5},{3,7},{5,1},{7,3},{8,12},{10,14},{12... | collective-permute-start | bytes 737288 | tf_op jit(solution)/shard_map/ppermute | solution.py:776
  7.2 7.9 %collective-permute-start.4 = (f32[11,8,512]{2,1,0:T(8,128)}, f32[11,8,512]{2,1,0:T(8,128)S(1)}, u32[]{:S(2)}, u32[]{:S(2)}) collective-permute-start(f32[11,8,512]{2,1,0:T(8,128)} %get-tuple-element.54.refs_0_), channel_id=1, source_target_pairs={{6,30},{14,6},{22,14},{30,22},{7,31},{15,7},{23,15},{31,23}} | collective-permute-start | bytes 540680 | tf_op jit(solution)/shard_map/ppermute | solution.py:784
  7.8 7.3 %collective-permute-start.3 = (f32[11,8,512]{2,1,0:T(8,128)}, f32[11,8,512]{2,1,0:T(8,128)S(1)}, u32[]{:S(2)}, u32[]{:S(2)}) collective-permute-start(f32[11,8,512]{2,1,0:T(8,128)} %get-tuple-element.54.refs_0_), channel_id=1, source_target_pairs={{6,14},{14,22},{22,30},{30,6},{7,15},{15,23},{23,31},{31,7}} | collective-permute-start | bytes 540680 | tf_op jit(solution)/shard_map/ppermute | solution.py:784
  8.5 5.8 %collective-permute-start.1 = (f32[16,128]{1,0:T(8,128)}, f32[16,128]{1,0:T(8,128)S(1)}, u32[]{:S(2)}, u32[]{:S(2)}) collective-permute-start(f32[16,128]{1,0:T(8,128)} %get-tuple-element.44.own_east_ref), channel_id=1, source_target_pairs={{0,8},{8,16},{16,24},{24,0},{1,9},{9,17},{17,25},{25,1},{2,10},{10... | collective-permute-start | bytes 24584 | tf_op jit(solution)/shard_map/ppermute | solution.py:782
  10.1 4.2 %collective-permute-start.2 = (f32[16,128]{1,0:T(8,128)}, f32[16,128]{1,0:T(8,128)S(1)}, u32[]{:S(2)}, u32[]{:S(2)}) collective-permute-start(f32[16,128]{1,0:T(8,128)} %get-tuple-element.45.own_west_ref), channel_id=1, source_target_pairs={{8,0},{16,8},{24,16},{0,24},{9,1},{17,9},{25,17},{1,25},{10,2},{18... | collective-permute-start | bytes 24584 | tf_op jit(solution)/shard_map/ppermute | solution.py:783
  15.1 23.3 %copy-start.4 = (s32[2048]{0:T(1024)S(1)}, s32[2048]{0:T(1024)}, u32[]{:S(2)}) copy-start(s32[2048]{0:T(1024)} %partner_ref.3) | copy-start | bytes 24580
  15.1 23.3 %copy-start.5 = (f32[16,128]{1,0:T(8,128)S(1)}, f32[16,128]{1,0:T(8,128)}, u32[]{:S(2)}) copy-start(f32[16,128]{1,0:T(8,128)} %get-tuple-element.45.own_west_ref) | copy-start | bytes 24580
  15.1 23.3 %copy-start.6 = (f32[16,128]{1,0:T(8,128)S(1)}, f32[16,128]{1,0:T(8,128)}, u32[]{:S(2)}) copy-start(f32[16,128]{1,0:T(8,128)} %get-tuple-element.44.own_east_ref) | copy-start | bytes 24580
  15.2 9.6 %collective-permute-start.6 = (f32[12,8,512]{2,1,0:T(8,128)S(1)}, f32[12,8,512]{2,1,0:T(8,128)S(1)}, u32[]{:S(2)}, u32[]{:S(2)}) collective-permute-start(f32[12,8,512]{2,1,0:T(8,128)S(1)} %get-tuple-element.52), channel_id=1, source_target_pairs={{0,2},{2,0},{4,6},{6,4},{1,3},{3,1},{5,7},{7,5},{8,10},{10,8},{12,... | collective-permute-start | bytes 589832 | tf_op jit(solution)/shard_map/ppermute | solution.py:799
  21.6 7.0 %collective-permute-start.7 = (f32[12,8,512]{2,1,0:T(8,128)S(1)}, f32[12,8,512]{2,1,0:T(8,128)S(1)}, u32[]{:S(2)}, u32[]{:S(2)}) collective-permute-start(f32[12,8,512]{2,1,0:T(8,128)S(1)} %get-tuple-element.53), channel_id=1, source_target_pairs={{2,4},{4,2},{3,5},{5,3},{10,12},{12,10},{11,13},{13,11},{18,20},{2... | collective-permute-start | bytes 589832 | tf_op jit(solution)/shard_map/ppermute | solution.py:800
  23.5 1.3 %collective-permute-start.8 = (f32[11,8,512]{2,1,0:T(8,128)S(1)}, f32[11,8,512]{2,1,0:T(8,128)S(1)}, u32[]{:S(2)}, u32[]{:S(2)}) collective-permute-start(f32[11,8,512]{2,1,0:T(8,128)S(1)} %copy-done.3), channel_id=1, source_target_pairs={{6,22},{14,30},{22,6},{30,14},{7,23},{15,31},{23,7},{31,15}} | collective-permute-start | bytes 540680 | tf_op jit(solution)/shard_map/ppermute | solution.py:798
  24.2 9.9 %collective-permute-start.9 = (f32[16,1920]{1,0:T(8,128)S(1)}, f32[16,1920]{1,0:T(8,128)S(1)}, u32[]{:S(2)}, u32[]{:S(2)}) collective-permute-start(f32[16,1920]{1,0:T(8,128)S(1)} %get-tuple-element.51), channel_id=1, source_target_pairs={{0,16},{8,24},{16,0},{24,8},{1,17},{9,25},{17,1},{25,9},{2,18},{10... | collective-permute-start | bytes 368648 | tf_op jit(solution)/shard_map/ppermute | solution.py:776
  34.1 4.3 %collective-permute-start.10 = (f32[8,1920]{1,0:T(8,128)S(1)}, f32[8,1920]{1,0:T(8,128)S(1)}, u32[]{:S(2)}, u32[]{:S(2)}) collective-permute-start(f32[8,1920]{1,0:T(8,128)S(1)} %get-tuple-element.56), channel_id=1, source_target_pairs={{0,8},{8,0},{16,24},{24,16},{1,9},{9,1},{17,25},{25,17},{2,10},{10... | collective-permute-start | bytes 184328 | tf_op jit(solution)/shard_map/ppermute | solution.py:776
  41.4 9.3 %collective-permute-start.11 = (f32[24,1664]{1,0:T(8,128)S(1)}, f32[24,1664]{1,0:T(8,128)S(1)}, u32[]{:S(2)}, u32[]{:S(2)}) collective-permute-start(f32[24,1664]{1,0:T(8,128)S(1)} %get-tuple-element.68), channel_id=1, source_target_pairs={{0,1},{2,3},{4,5},{6,7},{8,9},{10,11},{12,13},{14,15},{16,17},{18,... | collective-permute-start | bytes 479240 | tf_op jit(solution)/shard_map/ppermute | solution.py:837
  42.7 8.0 %collective-permute-start.12 = (f32[8,1920]{1,0:T(8,128)S(1)}, f32[8,1920]{1,0:T(8,128)S(1)}, u32[]{:S(2)}, u32[]{:S(2)}) collective-permute-start(f32[8,1920]{1,0:T(8,128)S(1)} %add.3.mine_ref), channel_id=1, source_target_pairs={{0,1},{1,0},{2,3},{3,2},{4,5},{5,4},{6,7},{7,6},{8,9},{9,8},{10,11... | collective-permute-start | bytes 184328 | tf_op jit(solution)/shard_map/ppermute | solution.py:816

commit v2 on v1

--- a/solution.py
+++ b/solution.py
@@ -20,10 +20,10 @@
 DEEP = 8
 FAR = 64
 WET = 48
+ABOVE = 56
 SLABS = 11
 CORNERS = SLABS
 VMEM_BYTES = 24 * 1024 * 1024
-PREPARE_BYTES = 58 * 1024 * 1024
 
 VMEM = pl.BlockSpec(memory_space=pltpu.VMEM)
 SMEM = pl.BlockSpec(memory_space=pltpu.SMEM)
@@ -39,14 +39,15 @@
     return pltpu.roll(value, shift % value.shape[axis], axis)
 
 
-def call(kernel, out_shape, in_specs, args, scratch=(), name=None, vmem=VMEM_BYTES):
+def call(kernel, out_shape, in_specs, args, scratch=(), name=None, out_specs=None, aliases=None):
     return pl.pallas_call(
         kernel,
         out_shape=out_shape,
         in_specs=in_specs,
-        out_specs=jax.tree.map(lambda _: VMEM, out_shape),
+        out_specs=out_specs or jax.tree.map(lambda _: VMEM, out_shape),
+        input_output_aliases=aliases or {},
         scratch_shapes=list(scratch),
-        compiler_params=pltpu.CompilerParams(vmem_limit_bytes=vmem),
+        compiler_params=pltpu.CompilerParams(vmem_limit_bytes=VMEM_BYTES),
         name=name,
     )(*args)
 
@@ -56,12 +57,16 @@
 
 
 def shape(*dims):
-    return jax.ShapeDtypeStruct(dims, F32)
+    return pltpu.VMEM(dims, F32)
+
+
+def in_hbm(*arrays):
+    return tuple(pltpu.with_memory_space_constraint(array, pltpu.HBM) for array in arrays)
 
 
 def prepare_kernel(
     n_lon, n_lat, state_hbm, mask_hbm, tiles_hbm, owner_hbm, row_hbm, partner_hbm, keep_ref, send_ref, west_ref, east_ref,
-    top_ref, state_ref, mask_ref, x_ref, owners_ref, rows_ref, hinge_ref, sem,
+    total_ref, state_ref, mask_ref, x_ref, owners_ref, rows_ref, hinge_ref, sem,
 ):
     tiles, cols = tiles_hbm.shape[1], tiles_hbm.shape[2]
     half_cols = cols // 2
@@ -165,7 +170,11 @@
 
     for copy in fields:
         copy.wait()
-    edge_rows(state_ref, mask_ref, top_ref, rows, rows - 1, rows - 2)
+    total = jnp.zeros(total_ref.shape, F32)
+    for k in range(DEEP):
+        at = slice(k * rows, (k + 1) * rows)
+        total = total + buoyancy_of(state_ref[2, at, :], state_ref[3, at, :])
+    total_ref[...] = total
     edge_columns(state_ref, mask_ref, west_ref, east_ref)
 
 
@@ -182,9 +191,9 @@
     side = shape(2 * DEEP, LANES)
     return call(
         functools.partial(prepare_kernel, n_lon, n_lat),
-        (slots, slots, side, side, shape(SLABS, DEEP, cols)),
+        (slots, slots, side, side, shape(2 * DEEP, cols)),
         [HBM] * 6,
-        (
+        in_hbm(
             state,
             mask,
             flux_tiles.transpose(1, 0, 2),
@@ -202,7 +211,6 @@
             pltpu.SemaphoreType.DMA((8,)),
         ],
         name="prepare",
-        vmem=PREPARE_BYTES,
     )
 
 
@@ -242,15 +250,30 @@
     east_ref[...] = east
 
 
-def rows_kernel(state_ref, mask_ref, turn_ref, from_west_ref, from_east_ref, pair_ref, cross_ref):
-    rows, cols = from_west_ref.shape[0], state_ref.shape[2]
+def columns_kernel(west_ref, east_ref, prefix_ref, west_out_ref, east_out_ref):
+    rows, cols = prefix_ref.shape
+    lane = iota((rows, LANES), 1)
+    for side, in_ref, out_ref in ((0, west_ref, west_out_ref), (1, east_ref, east_out_ref)):
+        near, far = (0, 1) if side == 0 else (cols - 1, cols - 2)
+        value = jnp.where(lane == ABOVE, prefix_ref[:, near : near + 1], in_ref[...])
+        out_ref[...] = jnp.where(lane == FAR + ABOVE, prefix_ref[:, far : far + 1], value)
+
+
+def corner_slab(out_ref, prefix_ref, turn_ref, from_west_ref, from_east_ref, near, far):
+    out_ref[CORNERS] = jnp.full(out_ref.shape[1:], turn_ref[near], F32)
+    out_ref[CORNERS, 0:1, 0:LANES] = from_west_ref[near : near + 1, :]
+    out_ref[CORNERS, 1:2, 0:LANES] = from_east_ref[near : near + 1, :]
+    out_ref[CORNERS, 3:4, :] = prefix_ref[near : near + 1, :]
+    out_ref[CORNERS, 4:5, :] = prefix_ref[far : far + 1, :]
+
+
+def rows_kernel(state_ref, mask_ref, prefix_ref, turn_ref, from_west_ref, from_east_ref, pair_ref, cross_ref):
+    rows = prefix_ref.shape[0]
     odd = lax.rem(lax.axis_index("lat"), 2) == 1
 
     def fill(out_ref, near, far):
         edge_rows(state_ref, mask_ref, out_ref, rows, near, far)
-        out_ref[CORNERS] = jnp.full((DEEP, cols), turn_ref[near], F32)
-        out_ref[CORNERS, 0:1, 0:LANES] = from_west_ref[near : near + 1, :]
-        out_ref[CORNERS, 1:2, 0:LANES] = from_east_ref[near : near + 1, :]
+        corner_slab(out_ref, prefix_ref, turn_ref, from_west_ref, from_east_ref, near, far)
 
     @pl.when(odd)
     def _():
@@ -369,18 +392,22 @@
     return jnp.sum(here, axis=1, keepdims=True)
 
 
-def interior_kernel(state_ref, mask_ref, turn_ref, share_ref, new_ref, sums_ref):
-    rows, cols = sums_ref.shape[0], state_ref.shape[2]
+def inside_kernel(state_ref, mask_ref, prefix_ref, turn_ref, share_ref, new_ref, sums_ref):
+    rows, cols = prefix_ref.shape
     n_r, n_j = rows // DEEP, cols // LANES
     turn = turn_column(turn_ref, rows)
     grid = [(r, j) for r in range(n_r) for j in range(n_j)]
     zero = jnp.zeros((DEEP, LANES), F32)
-    run = {at: [zero] * 5 for at in grid}
+    prefix = Tiles([[prefix_ref[tile(r, j, 0, rows)] for j in range(n_j)] for r in range(n_r)])
+    run = {}
+    for at in grid:
+        east, west, north, south = prefix.around(*at)
+        run[at] = [0.5 * (east - west), 0.5 * (north - south), zero, zero]
     for k in range(DEEP):
         fields = [Tiles([[state_ref[(f, *tile(r, j, k, rows))] for j in range(n_j)] for r in range(n_r)]) for f in range(5)]
         for r, j in grid:
             at = tile(r, j, k, rows)
-            above_x, above_y, before, total, absorbed = run[r, j]
+            above_x, above_y, total, absorbed = run[r, j]
             slopes = []
 
             def pressed(x, y):
@@ -397,39 +424,26 @@
             run[r, j] = [
                 above_x + slopes[0],
                 above_y + slopes[1],
-                before + buoyancy_of(values[2], values[3]),
                 total + buoyancy_of(new[2], new[3]),
                 absorbed + wet * share_ref[k],
             ]
     for r, j in grid:
-        for kind in range(3):
+        for kind in range(2):
             at = slice(kind * cols + j * LANES, kind * cols + (j + 1) * LANES)
             sums_ref[r * DEEP : (r + 1) * DEEP, at] = run[r, j][2 + kind]
 
 
 def rim_kernel(
-    n_lon, n_lat, state_ref, mask_ref, turn_ref, share_ref, partner_ref, own_west_ref, own_east_ref,
-    from_west_ref, from_east_ref, pair_ref, cross_ref, inside_ref, *refs,
+    n_lat, state_ref, mask_ref, prefix_ref, turn_ref, share_ref, partner_ref, own_west_ref, own_east_ref,
+    from_west_ref, from_east_ref, pair_ref, cross_ref, first_ref, second_ref, inside_ref, ring_rows_ref, ring_cols_ref,
+    edge_rows_ref, edge_cols_ref, sums_ref, south_ref, north_ref,
 ):
-    blocks = refs[:n_lon]
-    ring_rows_ref, ring_cols_ref, edge_rows_ref, edge_cols_ref, sums_ref, south_ref, north_ref, fold_ref, sem = refs[n_lon:]
-    rows, cols = from_west_ref.shape[0], state_ref.shape[2]
-    lon, lat = lax.axis_index("lon"), lax.axis_index("lat")
+    rows, cols = prefix_ref.shape
+    lat = lax.axis_index("lat")
     odd = lax.rem(lat, 2) == 1
     hinge = partner_ref[0]
-    hinge_block = hinge // cols
-    within = hinge - hinge_block * cols
+    within = hinge - (hinge // cols) * cols
     at_top = lat == n_lat - 1
-    wanted = [lax.rem(2 * lon - hinge_block + offset + 2 * n_lon, n_lon) for offset in (1, 0, -1)]
-
-    @pl.when(at_top)
-    def _():
-        for place in range(3):
-            for d in range(n_lon):
-
-                @pl.when(wanted[place] == d)
-                def _(place=place, d=d):
-                    pltpu.make_async_copy(blocks[d], fold_ref.at[place], sem.at[place]).start()
 
     @pl.when(odd)
     def _():
@@ -450,35 +464,39 @@
     @pl.when(lat == 0)
     def _():
         edge_rows(state_ref, mask_ref, south_ref, rows, 0, 0)
-        south_ref[CORNERS] = jnp.full((DEEP, cols), turn_ref[0], F32)
-        south_ref[CORNERS, 0:1, 0:LANES] = from_west_ref[0:1, :]
-        south_ref[CORNERS, 1:2, 0:LANES] = from_east_ref[0:1, :]
+        corner_slab(south_ref, prefix_ref, turn_ref, from_west_ref, from_east_ref, 0, 0)
 
     sub8, lane8 = iota((DEEP, LANES), 0), iota((DEEP, LANES), 1)
 
     @pl.when(at_top)
     def _():
-        for place in range(3):
-            pltpu.make_async_copy(blocks[0], fold_ref.at[place], sem.at[place]).wait()
         west = jnp.zeros((DEEP, LANES), F32)
         east = jnp.zeros((DEEP, LANES), F32)
-        for slab in range(SLABS):
-            row = jnp.concatenate([fold_ref[0, slab], fold_ref[1, slab], fold_ref[2, slab]], axis=1)
-            row = pltpu.roll(row, 3 * cols - 1 - within, 1)
+        for slab in range(SLABS + 1):
+            row = jnp.concatenate([second_ref[slab], first_ref[slab]], axis=1)
+            row = pltpu.roll(row, 2 * cols - 1 - within, 1)
             if slab < 4:
                 row = -row
             north_ref[slab] = mirrored(row, cols)
             if slab < 10 and slab % 2 == 0:
                 here = lane8 == (slab // 2) * DEEP + sub8
-                west = jnp.where(here, row[:, cols : cols + 1], west)
-                east = jnp.where(here, row[:, 3 * cols - 1 :], east)
-        north_ref[CORNERS] = jnp.full((DEEP, cols), turn_ref[rows - 1], F32)
-        north_ref[CORNERS, 0:1, 0:LANES] = jnp.sum(west, axis=0, keepdims=True)
+            elif slab == CORNERS:
+                here = (lane8 == ABOVE) & (sub8 == 3)
+            else:
+                continue
+            west = jnp.where(here, row[:, cols : cols + 1], west)
+            east = jnp.where(here, row[:, 2 * cols - 1 :], east)
+        beyond = first_ref[CORNERS, 1:2, 0:LANES]
+        beyond = jnp.where(iota((1, LANES), 1) < 16, -beyond, beyond)
+        west = jnp.where(within == cols - 1, beyond, jnp.sum(west, axis=0, keepdims=True))
+        north_ref[CORNERS, 0:1, 0:LANES] = west
         north_ref[CORNERS, 1:2, 0:LANES] = jnp.sum(east, axis=0, keepdims=True)
-
-    tail = slice(3 * cols, 3 * cols + LANES)
-    sums_ref[rows:, :] = jnp.zeros((DEEP, sums_ref.shape[1]), F32)
-    sums_ref[0:rows, 0 : 3 * cols] = inside_ref[...]
+        north_ref[CORNERS, 2:3, :] = jnp.full((1, cols), turn_ref[rows - 1], F32)
+
+    wide = cols + LANES
+    sums_ref[rows:, :] = jnp.zeros((DEEP, 2 * wide), F32)
+    for kind in range(2):
+        sums_ref[0:rows, kind * wide : kind * wide + cols] = inside_ref[:, kind * cols : (kind + 1) * cols]
 
     share_down = jnp.zeros((DEEP, LANES), F32)
     for k in range(DEEP):
@@ -487,10 +505,7 @@
     def down(line, f):
         return jnp.sum(jnp.where(lane8 == f * DEEP + sub8, line, 0.0), axis=1, keepdims=True)
 
-    def pressed_rows(x, y):
-        return PRESS * (scan_down(x) - 0.5 * x), PRESS * (scan_down(y) - 0.5 * y)
-
-    def row_step(near, south, north, west_line, east_line, wet, turn):
+    def row_step(near, south, north, west_line, east_line, wet, turn, above, above_south, above_north):
         col = iota((DEEP, cols), 1)
         sides = [
             (
@@ -501,7 +516,14 @@
             )
             for f in range(5)
         ]
-        return advanced(near, sides, wet, turn, pressed_rows)
+        east = jnp.where(col[0:1] == cols - 1, east_line[:, ABOVE : ABOVE + 1], roll(above, -1, 1))
+        west = jnp.where(col[0:1] == 0, west_line[:, ABOVE : ABOVE + 1], roll(above, 1, 1))
+        above_x, above_y = 0.5 * (east - west), 0.5 * (above_north - above_south)
+
+        def pressed(x, y):
+            return PRESS * (above_x + scan_down(x) - 0.5 * x), PRESS * (above_y + scan_down(y) - 0.5 * y)
+
+        return advanced(near, sides, wet, turn, pressed)
 
     for side, ghost_ref, edge, inner in ((0, south_ref, 0, 1), (1, north_ref, rows - 1, rows - 2)):
         near = [ghost_ref[2 * f] for f in range(5)]
@@ -510,26 +532,29 @@
         own_next = [level_rows(state_ref.at[f], inner, rows) for f in range(5)]
         ring_wet = ghost_ref[10]
         corners = ghost_ref[CORNERS, :, 0:LANES]
-        south, north = (far, own) if side == 0 else (own, far)
-        ring = row_step(near, south, north, corners[0:1, :], corners[1:2, :], ring_wet, corners[2:3, 0:1])
-        south, north = (near, own_next) if side == 0 else (own_next, near)
+        above_near, above_far = ghost_ref[CORNERS, 3:4, :], ghost_ref[CORNERS, 4:5, :]
+        above_own, above_next = prefix_ref[edge : edge + 1, :], prefix_ref[inner : inner + 1, :]
+        outward, inward = (far, above_far), (own, above_own)
+        (south, above_south), (north, above_north) = (outward, inward) if side == 0 else (inward, outward)
+        ring = row_step(
+            near, south, north, corners[0:1, :], corners[1:2, :], ring_wet, corners[2:3, 0:1], above_near, above_south, above_north
+        )
+        outward, inward = (near, above_near), (own_next, above_next)
+        (south, above_south), (north, above_north) = (outward, inward) if side == 0 else (inward, outward)
         wet = level_rows(mask_ref, edge, rows).astype(F32)
         edge_line = slice(edge, edge + 1)
-        new = row_step(own, south, north, from_west_ref[edge_line, :], from_east_ref[edge_line, :], wet, turn_ref[edge])
+        new = row_step(
+            own, south, north, from_west_ref[edge_line, :], from_east_ref[edge_line, :], wet, turn_ref[edge],
+            above_own, above_south, above_north,
+        )
         for f in range(5):
             edge_rows_ref[side, f] = new[f]
             ring_rows_ref[side, f] = jnp.where(lat == 0, new[f], ring[f]) if side == 0 else ring[f]
         ring_rows_ref[side, 5] = ring_wet
         at = slice(rows + side, rows + side + 1)
-        below = slice(rows + 2 + side, rows + 3 + side)
-        sums_ref[at, 0:cols] = jnp.sum(buoyancy_of(near[2], near[3]), axis=0, keepdims=True)
-        sums_ref[below, 0:cols] = jnp.sum(buoyancy_of(far[2], far[3]), axis=0, keepdims=True)
         here = buoyancy_of(ring_rows_ref[side, 2], ring_rows_ref[side, 3])
-        sums_ref[at, cols : 2 * cols] = jnp.sum(here, axis=0, keepdims=True)
-        sums_ref[at, 2 * cols : 3 * cols] = jnp.sum(ring_wet * share_down[:, 0:1], axis=0, keepdims=True)
-        corner_sums = buoyancy_sum(corners)
-        for at_col in range(2):
-            sums_ref[at, 3 * cols + at_col : 3 * cols + at_col + 1] = corner_sums[at_col : at_col + 1, :]
+        sums_ref[at, 0:cols] = jnp.sum(here, axis=0, keepdims=True)
+        sums_ref[at, wide : wide + cols] = jnp.sum(ring_wet * share_down[:, 0:1], axis=0, keepdims=True)
 
     row, lane = iota((rows, LANES), 0), iota((rows, LANES), 1)
     turn = turn_column(turn_ref, rows)
@@ -547,12 +572,13 @@
         merid_all = sum(roll(merid, 8 * n, 1) for n in (1, 2, 3))
         bx = lanes_between(buoyancy_of(roll(dx, -16, 1), roll(dx, -24, 1)), 0, 8)
         by = lanes_between(buoyancy_of(roll(dy, -8, 1), roll(dy, -16, 1)), 8, 16)
-        press_x, press_y = PRESS * (scan_lanes(bx) - 0.5 * bx), PRESS * (scan_lanes(by) - 0.5 * by)
+        press_x = lanes_between(PRESS * (dx[:, ABOVE : ABOVE + 1] + scan_lanes(bx) - 0.5 * bx), 0, 8)
+        press_y = lanes_between(PRESS * (dy[:, ABOVE : ABOVE + 1] + scan_lanes(by) - 0.5 * by), 8, 16)
         trend = VISCOUS * lap - ADVECT * (zonal_all * dx + merid_all * dy) - press_x - press_y
         trend = trend + lanes_between(turn * roll(near, -8, 1), 0, 8) - lanes_between(turn * roll(near, 8, 1), 8, 16)
         return near + wet_all * trend, wet
 
-    block = jnp.zeros((rows, LANES), F32)
+    blocks = [jnp.zeros((rows, LANES), F32)] * 2
     sides = ((0, from_west_ref, own_west_ref), (1, from_east_ref, own_east_ref))
     for side, ghost_ref, own_ref in sides:
         near, own = ghost_ref[...], own_ref[...]
@@ -562,23 +588,23 @@
         east, west = (own, far) if side == 0 else (far, own)
         new, wet = column_step(near, east, west, north, south)
         ring_cols_ref[side] = new
-        found = (buoyancy_sum(near), buoyancy_sum(far), buoyancy_sum(new), jnp.sum(wet * share_lanes, axis=1, keepdims=True))
-        for kind in range(4):
-            block = jnp.where(lane == 2 * kind + side, found[kind], block)
+        blocks[0] = jnp.where(lane == side, buoyancy_sum(new), blocks[0])
+        blocks[1] = jnp.where(lane == side, jnp.sum(wet * share_lanes, axis=1, keepdims=True), blocks[1])
         east, west = (own_next, near) if side == 0 else (near, own_next)
         new, _ = column_step(own, east, west, roll(own, -1, 0), roll(own, 1, 0))
         edge_cols_ref[side] = new
-        column = cols if side == 0 else 2 * cols - 1
+        column = 0 if side == 0 else cols - 1
         sums_ref[0:rows, column : column + 1] = buoyancy_sum(new)
-    sums_ref[0:rows, tail] = block
+    for kind in range(2):
+        sums_ref[0:rows, kind * wide + cols : (kind + 1) * wide] = blocks[kind]
     for side, edge in ((0, 0), (1, rows - 1)):
         here = buoyancy_of(edge_rows_ref[side, 2], edge_rows_ref[side, 3])
-        sums_ref[edge : edge + 1, cols : 2 * cols] = jnp.sum(here, axis=0, keepdims=True)
-
-
-def last_kernel(
-    n_lon, n_lat, state_ref, mask_ref, ring_rows_ref, ring_cols_ref, edge_rows_ref, edge_cols_ref, sums_ref, mine_ref,
-    theirs_ref, turn_ref, share_ref, partner_ref, out_ref,
+        sums_ref[edge : edge + 1, 0:cols] = jnp.sum(here, axis=0, keepdims=True)
+
+
+def second_kernel(
+    n_lat, state_ref, mask_ref, ring_rows_ref, ring_cols_ref, edge_rows_ref, edge_cols_ref, mine_ref, theirs_ref,
+    turn_ref, share_ref, partner_ref, out_hbm, flow_ref, drive_ref, tracers_ref, sem,
 ):
     rows, cols = mask_ref.shape[0] // DEEP, mask_ref.shape[1]
     n_r, n_j = rows // DEEP, cols // LANES
@@ -587,8 +613,7 @@
     mine, theirs = mine_ref[...], theirs_ref[...]
     first = lax.axis_index("lev") == 0
     halves = (jnp.where(first, mine, theirs), jnp.where(first, theirs, mine))
-    lat = lax.axis_index("lat")
-    at_top, at_bottom = lat == n_lat - 1, lat == 0
+    at_top = lax.axis_index("lat") == n_lat - 1
     hinge = partner_ref[0]
     within = hinge - (hinge // cols) * cols
 
@@ -630,65 +655,32 @@
         share_down = jnp.where(sub8 == k, share_ref[k], share_down)
         share_lanes = jnp.where((lane & 7) == k, share_ref[k], share_lanes)
 
-    shallow = sums_ref[0:rows, 0:cols]
-    tail = sums_ref[:, 3 * cols : 3 * cols + LANES]
-    shallow_rows = [sums_ref[rows + n : rows + n + 1, 0:cols] for n in range(4)]
-    east, west, north, south = around(shallow, tail[0:rows, 0:1], tail[0:rows, 1:2], shallow_rows[0], shallow_rows[1])
-    half_press = 0.5 * PRESS
-    push_x, push_y = half_press * (east - west), half_press * (north - south)
-    col_row = iota((1, cols), 1)
-    push_rows, push_cols = [], []
-    for side in range(2):
-        near, far = shallow_rows[side], shallow_rows[2 + side]
-        west = jnp.where(col_row == 0, tail[rows + side : rows + side + 1, 0:1], roll(near, 1, 1))
-        east = jnp.where(col_row == cols - 1, tail[rows + side : rows + side + 1, 1:2], roll(near, -1, 1))
-        inner = shallow[0:1, :] if side == 0 else shallow[rows - 1 :, :]
-        rise = inner - far if side == 0 else far - inner
-        along, across = half_press * (east - west), half_press * rise
-        if side == 0:
-            along = jnp.where(at_bottom, push_x[0:1, :], along)
-            across = jnp.where(at_bottom, push_y[0:1, :], across)
-        push_rows.append((along, across))
-    for side in range(2):
-        near = jnp.broadcast_to(tail[0:rows, side : side + 1], (rows, LANES))
-        far = tail[0:rows, 2 + side : 3 + side]
-        inner = shallow[:, 0:1] if side == 0 else shallow[:, cols - 1 :]
-        north = jnp.where(row == rows - 1, tail[rows + 1 : rows + 2, side : side + 1], roll(near, -1, 0))
-        south = jnp.where(row == 0, tail[rows : rows + 1, side : side + 1], roll(near, 1, 0))
-        push_cols.append((half_press * (inner - far if side == 0 else far - inner), half_press * (north - south)))
-
-    ring_rows, above_rows = [], []
+    drive_ref[...] = jnp.zeros(drive_ref.shape, F32)
+    drive_ref[0:rows, 0:cols] = buoyancy_of(flux[0], flux[1])
+
+    ring_rows, ring_cols = [], []
     for side, source in ((0, flux_south), (1, flux_north)):
-        at = slice(rows + side, rows + side + 1)
-        wet = ring_rows_ref[side, 5]
-        taken = wet * share_down[:, 0:1]
-        values = [ring_rows_ref[side, f] - wet * push_rows[side][f] for f in range(2)]
-        values += [ring_rows_ref[side, 2 + c] + taken * source[c] for c in range(3)]
-        ring_rows.append(values)
-        above_rows.append(
-            sums_ref[at, cols : 2 * cols] + sums_ref[at, 2 * cols : 3 * cols] * buoyancy_of(source[0], source[1])
-        )
-    ring_cols, above_cols = [], []
+        taken = ring_rows_ref[side, 5] * share_down[:, 0:1]
+        values = [ring_rows_ref[side, f] for f in range(2)]
+        ring_rows.append(values + [ring_rows_ref[side, 2 + c] + taken * source[c] for c in range(3)])
+        drive_ref[rows + side : rows + side + 1, 0:cols] = buoyancy_of(source[0], source[1])
     for side, source in ((0, flux_west), (1, flux_east)):
         found = ring_cols_ref[side]
-        wet = lanes_between(found, WET, WET + 8)
-        taken = wet * share_lanes
-        found = found - roll(wet, -WET, 1) * push_cols[side][0] - roll(wet, 8 - WET, 1) * push_cols[side][1]
+        taken = lanes_between(found, WET, WET + 8) * share_lanes
         for c in range(3):
             found = found + roll(taken, 8 * (2 + c) - WET, 1) * source[c]
         ring_cols.append(found)
-        above_cols.append(tail[0:rows, 4 + side : 5 + side] + tail[0:rows, 6 + side : 7 + side] * buoyancy_of(source[0], source[1]))
-    above = sums_ref[0:rows, cols : 2 * cols] + sums_ref[0:rows, 2 * cols : 3 * cols] * buoyancy_of(flux[0], flux[1])
-    east, west, north, south = around(above, above_cols[0], above_cols[1], above_rows[0], above_rows[1])
-    above_x, above_y = 0.5 * (east - west), 0.5 * (north - south)
+        drive_ref[0:rows, cols + side : cols + side + 1] = buoyancy_of(source[0], source[1])
 
     grid = [(r, j) for r in range(n_r) for j in range(n_j)]
 
     def cut(value, r, j):
         return value[r * DEEP : (r + 1) * DEEP, j * LANES : (j + 1) * LANES]
 
-    run = {at: (cut(above_x, *at), cut(above_y, *at)) for at in grid}
+    zero = jnp.zeros((DEEP, LANES), F32)
+    run = {at: (zero, zero) for at in grid}
     edge_cols = [edge_cols_ref[side] for side in range(2)]
+    copies = []
 
     def column(value, r, n):
         return jnp.broadcast_to(value[r * DEEP : (r + 1) * DEEP, n : n + 1], (DEEP, LANES))
@@ -711,9 +703,7 @@
                     value = jnp.where(sub8 == 0, edge_rows_ref[0, f, k : k + 1, at[1]], value)
                 if r == n_r - 1:
                     value = jnp.where(sub8 == DEEP - 1, edge_rows_ref[1, f, k : k + 1, at[1]], value)
-                if f < 2:
-                    value = value - wet * cut((push_x, push_y)[f], r, j)
-                else:
+                if f >= 2:
                     value = value + heats[r, j][f - 2]
                 grids[f][r][j] = value
         fields = [
@@ -743,7 +733,42 @@
                 heats[r, j],
             )
             for f in range(5):
-                out_ref[(f, *at)] = new[f]
+                if f < 2:
+                    flow_ref[(f, *at)] = new[f]
+                else:
+                    tracers_ref[(f - 2, *at)] = new[f]
+        whole = pl.ds(k * rows, rows)
+        copies.append(
+            pltpu.make_async_copy(tracers_ref.at[:, whole, :], out_hbm.at[pl.ds(2, 3), whole, :], sem.at[k])
+        )
+        copies[-1].start()
+    for copy in copies:
+        copy.wait()
+
+
+def last_kernel(out_in_hbm, flow_ref, mask_ref, sums_ref, drive_ref, out_hbm, moved_ref, sem):
+    del out_in_hbm
+    rows, cols = mask_ref.shape[0] // DEEP, mask_ref.shape[1]
+    wide = cols + LANES
+    above = sums_ref[:, 0:wide] + sums_ref[:, wide : 2 * wide] * drive_ref[...]
+    east, west, north, south = around(
+        above[0:rows, 0:cols],
+        above[0:rows, cols : cols + 1],
+        above[0:rows, cols + 1 : cols + 2],
+        above[rows : rows + 1, 0:cols],
+        above[rows + 1 : rows + 2, 0:cols],
+    )
+    push_x, push_y = (0.5 * PRESS) * (east - west), (0.5 * PRESS) * (north - south)
+    copies = []
+    for k in range(DEEP):
+        whole = pl.ds(k * rows, rows)
+        wet = mask_ref[whole, :].astype(F32)
+        moved_ref[0, whole, :] = flow_ref[0, whole, :] - wet * push_x
+        moved_ref[1, whole, :] = flow_ref[1, whole, :] - wet * push_y
+        copies.append(pltpu.make_async_copy(moved_ref.at[:, whole, :], out_hbm.at[pl.ds(0, 2), whole, :], sem.at[k]))
+        copies[-1].start()
+    for copy in copies:
+        copy.wait()
 
 
 def body(n_lon, n_lat, state, mask, coriolis, penetration, flux_tiles, flux_owner, flux_row, fold_partner):
@@ -752,10 +777,7 @@
     flat_mask = mask.reshape(levels * rows, cols)
     last = n_lat - 1
 
-    def across(d):
-        return [(a * n_lat + last, (a + d) % n_lon * n_lat + last) for a in range(n_lon)]
-
-    keep, send, west, east, top = prepare(
+    keep, send, west, east, total = prepare(
         flat_state, flat_mask, flux_tiles, flux_owner, flux_row, fold_partner, n_lon, n_lat
     )
 
@@ -766,6 +788,7 @@
             stages.append((axis, size, bit))
             bit //= 2
     got = lax.ppermute(send, "lat", [(i, i ^ 1) for i in range(n_lat)])
+    prefix = lax.ppermute(total, "lev", [(0, 1)])
 
     def merged(keep, got):
         half = shape(keep.shape[0] // 2, keep.shape[1])
@@ -778,37 +801,53 @@
     keep, send = merged(keep, got)
     got = passed_on(send, stages[0])
 
-    west, east, top = after((west, east, top), send)
+    prefix = after(prefix, send)
+    side = shape(rows, LANES)
+    west, east = call(columns_kernel, (side, side), [VMEM] * 3, (west, east, prefix), name="edge_columns")
     from_west = lax.ppermute(east, "lon", [(i, (i + 1) % n_lon) for i in range(n_lon)])
     from_east = lax.ppermute(west, "lon", [((i + 1) % n_lon, i) for i in range(n_lon)])
-    folded = {d: lax.ppermute(top, ("lon", "lat"), across(d)) for d in (1, n_lon - 1)}
     message = shape(SLABS + 1, DEEP, cols)
     pair, cross = call(
         rows_kernel,
         (message, message),
-        [VMEM, VMEM, SMEM, VMEM, VMEM],
-        (flat_state, flat_mask, coriolis, from_west, from_east),
+        [VMEM, VMEM, VMEM, SMEM, VMEM, VMEM],
+        (flat_state, flat_mask, prefix, coriolis, from_west, from_east),
         name="edge_rows",
     )
-    keep = after(keep, (pair, cross, folded))
+    hinge_block = fold_partner[0] >> (cols.bit_length() - 1)
+    keep = after(keep, (pair, cross, hinge_block))
     keep, send = merged(keep, got)
     got = passed_on(send, stages[1])
 
-    pair, cross, top = after((pair, cross, top), send)
-    folded.update({d: lax.ppermute(top, ("lon", "lat"), across(d)) for d in range(2, n_lon - 1)})
+    pair, cross = after((pair, cross), send)
     from_pair = lax.ppermute(pair, "lat", [(i, i ^ 1) for i in range(n_lat)])
     from_cross = lax.ppermute(cross, "lat", [(i, i + 1 if i % 2 else i - 1) for i in range(1, last)])
-    keep = after(keep, (from_pair, from_cross, folded))
+
+    def folded(block):
+        def swap(rows_out):
+            return tuple(
+                lax.ppermute(
+                    rows_out,
+                    ("lon", "lat"),
+                    [(a * n_lat + last, (block - more - a) % n_lon * n_lat + last) for a in range(n_lon)],
+                )
+                for more in (0, 1)
+            )
+
+        return swap
+
+    first, second = lax.switch(hinge_block, [folded(block) for block in range(n_lon)], cross)
+    keep = after(keep, (from_pair, from_cross, first, second))
     for stage in stages[2:]:
         keep, send = merged(keep, got)
         got = passed_on(send, stage)
 
     near_state, near_mask = after((flat_state, flat_mask), send)
     new_state, inside = call(
-        interior_kernel,
-        (shape(fields, levels * rows, cols), shape(rows, 3 * cols)),
-        [VMEM, VMEM, SMEM, SMEM],
-        (near_state, near_mask, coriolis, penetration),
+        inside_kernel,
+        (shape(fields, levels * rows, cols), shape(rows, 2 * cols)),
+        [VMEM, VMEM, VMEM, SMEM, SMEM],
+        (near_state, near_mask, prefix, coriolis, penetration),
         name="first_inside",
     )
     keep = after(keep, inside)
@@ -816,34 +855,48 @@
     theirs = lax.ppermute(mine, "lev", [(0, 1), (1, 0)])
 
     inside = after(inside, mine)
-    ring = (shape(2, 6, DEEP, cols), shape(2, rows, LANES), shape(2, 5, DEEP, cols), shape(2, rows, LANES))
-    blocks = [top] + [folded[d] for d in range(1, n_lon)]
+    wide = cols + LANES
     *ring, sums = call(
-        functools.partial(rim_kernel, n_lon, n_lat),
-        (*ring, shape(rows + DEEP, 3 * cols + LANES)),
-        [VMEM, VMEM, SMEM, SMEM, SMEM] + [VMEM] * 7 + [ANY] * n_lon,
+        functools.partial(rim_kernel, n_lat),
         (
-            flat_state, flat_mask, coriolis, penetration, fold_partner, west, east, from_west, from_east, from_pair,
-            from_cross, inside, *blocks,
+            shape(2, 6, DEEP, cols),
+            shape(2, rows, LANES),
+            shape(2, 5, DEEP, cols),
+            shape(2, rows, LANES),
+            shape(rows + DEEP, 2 * wide),
         ),
-        [
-            pltpu.VMEM((SLABS + 1, DEEP, cols), F32),
-            pltpu.VMEM((SLABS + 1, DEEP, cols), F32),
-            pltpu.VMEM((3, SLABS, DEEP, cols), F32),
-            pltpu.SemaphoreType.DMA((3,)),
-        ],
+        [VMEM, VMEM, VMEM, SMEM, SMEM, SMEM] + [VMEM] * 9,
+        (
+            flat_state, flat_mask, prefix, coriolis, penetration, fold_partner, west, east, from_west, from_east, from_pair,
+            from_cross, first, second, inside,
+        ),
+        [pltpu.VMEM((SLABS + 1, DEEP, cols), F32), pltpu.VMEM((SLABS + 1, DEEP, cols), F32)],
         name="first_rim",
     )
+    sums = after(sums, theirs)
     sums = lax.ppermute(sums, "lev", [(0, 1)])
 
-    out = call(
-        functools.partial(last_kernel, n_lon, n_lat),
-        shape(fields, levels * rows, cols),
-        [VMEM] * 9 + [SMEM] * 3,
-        (new_state, flat_mask, *ring, sums, mine, theirs, coriolis, penetration, fold_partner),
-        name="last_substep",
-    )
-    return out.reshape(fields, levels, rows, cols)
+    out = jax.ShapeDtypeStruct(flat_state.shape, F32)
+    result, flow, drive = call(
+        functools.partial(second_kernel, n_lat),
+        (out, shape(2, levels * rows, cols), shape(rows + DEEP, wide)),
+        [VMEM] * 8 + [SMEM] * 3,
+        (new_state, flat_mask, *ring, mine, theirs, coriolis, penetration, fold_partner),
+        [pltpu.VMEM((3, levels * rows, cols), F32), pltpu.SemaphoreType.DMA((DEEP,))],
+        name="second_substep",
+        out_specs=(ANY, VMEM, VMEM),
+    )
+    result = call(
+        last_kernel,
+        out,
+        [ANY] + [VMEM] * 4,
+        (result, flow, flat_mask, sums, drive),
+        [pltpu.VMEM((2, levels * rows, cols), F32), pltpu.SemaphoreType.DMA((DEEP,))],
+        name="deeper_pressure",
+        out_specs=ANY,
+        aliases={0: 0},
+    )
+    return result.reshape(fields, levels, rows, cols)
 
 
 def solution(mesh):

time: 55.3 us -> 47.3 us (0.86); the launches traced: 54.2 us -> 47.3 us
  starting transfers between devices: 19.5 us -> 15.8 us
  waiting for transfers between devices: 21.2 us -> 17.6 us
  between operations: 0.22 us -> 0.8 us
    ppermute x1, starting transfers between devices: 6.4 us -> 0.07 us  [body(): from_pair = lax.ppermute(pair, 'lat', [(i, i ^ 1) for i in range(n_lat)])]
    ppermute x3, waiting for transfers between devices: 0.01 us -> 4.51 us  [the longest x1 4.51 us: body(): prefix = lax.ppermute(total, 'lev', [(0, 1)])]
    ppermute x1, waiting for transfers between devices: 5.31 us -> 1.33 us  [body(): theirs = lax.ppermute(mine, 'lev', [(0, 1), (1, 0)])]
    ppermute x1, waiting for transfers between devices: 3.73 us -> 0.01 us  [body(): lax.ppermute(cross, 'lat', [(i, i + 1 if i % 2 else i - 1) for i in range...]
    ppermute x1, starting transfers between devices: 2.71 us -> 0.07 us  [body(): theirs = lax.ppermute(mine, 'lev', [(0, 1), (1, 0)])]
    ppermute x1, waiting for transfers between devices: 0.01 us -> 2.44 us  [body(): sums = lax.ppermute(sums, 'lev', [(0, 1)])]
    ppermute x3, starting transfers between devices: 2 us -> 3.94 us  [the longest x2 2.66 us: swap(): lax.ppermute(rows_out, ('lon', 'lat'), [(a * n_lat + last, (block - more...]
    ppermute x3, starting transfers between devices: 1.28 us -> 3.07 us  [passed_on(): return lax.ppermute(send, axis, [(i, i ^ bit) for i in range(size)])]
  transfers between devices with their start and end apart: 13 -> 13, of which waited for: 6 -> 7; matrix products, arithmetic and copies ran while one was open for 0% -> 1% of each run, Pallas kernels for 4% -> 19%
where the time goes in v2:
time: 47.3 us
  waiting for transfers between devices  17.6 us (37%)
  starting transfers between devices  15.8 us (33%)
  Pallas kernels  12.5 us (26%)
  between operations  0.8 us (2%)
  local copies, waits for them, and re-layouts  0.53 us (1%)
    pallas_call x10, Pallas kernels, call(): pl.pallas_call(kernel, out_shape=out_shape, in_specs=in_specs, out_specs=...  12.5 us
    ppermute x3, waiting for transfers between devices, passed_on(): return lax.ppermute(send, axis, [(i, i ^ bit) for i in range(size)])  7 us
    ppermute x1, waiting for transfers between devices, body(): prefix = lax.ppermute(total, 'lev', [(0, 1)])  4.51 us
    ppermute x1, starting transfers between devices, body(): lax.ppermute(cross, 'lat', [(i, i + 1 if i % 2 else i - 1) for i in range...  3.52 us
    ppermute x3, starting transfers between devices, passed_on(): return lax.ppermute(send, axis, [(i, i ^ bit) for i in range(size)])  3.07 us
    ppermute x2, starting transfers between devices, swap(): lax.ppermute(rows_out, ('lon', 'lat'), [(a * n_lat + last, (block - more...  2.66 us
    ppermute x1, waiting for transfers between devices, body(): sums = lax.ppermute(sums, 'lev', [(0, 1)])  2.44 us
    ppermute x1, starting transfers between devices, body(): lax.ppermute(west, 'lon', [((i + 1) % n_lon, i) for i in range(n_lon)])  2.25 us
  transfers between devices with their start and end apart: 13, of which 7 were waited for; matrix products, arithmetic and copies ran while one was open for 1% of the time, Pallas kernels for 19%

profile of v2, /device:TPU:6, one launch (start us, length us, event | category | flops | bytes accessed | tf_op | source)
XLA Modules:
  0.0 47.3 jit_solution(6385463561018621473)
XLA Ops:
  0.0 2.5 %prepare.1 = (f32[64,1920]{1,0:T(8,128)S(1)}, f32[64,1920]{1,0:T(8,128)S(1)}, f32[16,128]{1,0:T(8,128)S(1)}, f32[16,128]{1,0:T(8,128)S(1)}, f32[16,512]{1,0:T(8,128)S(1)}) custom-call(f32[5,128,512]{2,1,0:T(8,128)} %bitcast.7, s32[128,512]{1,0:T(8,128)} %bitcast.11, f32[3,128,512]{2,1,0:T(8,128)} %bitcast.17, s32[1,128]{1,0:T(1,128)} %bitcast.18, ...), custom_call_target="tpu_custom_call" | custom-call | tf_op jit(solution)/shard_map/prepare/pallas_call | solution.py:43
  2.6 1.9 %collective-permute-done.8.got_ref = f32[64,1920]{1,0:T(8,128)S(1)} collective-permute-done((f32[64,1920]{1,0:T(8,128)S(1)}, f32[64,1920]{1,0:T(8,128)S(1)}, u32[]{:S(2)}, u32[]{:S(2)}) %collective-permute-start.8) | collective-permute-done | bytes 491552 | tf_op jit(solution)/shard_map/ppermute | solution.py:790
  4.5 0.6 %collective-permute-start.12 = (f32[32,1920]{1,0:T(8,128)S(1)}, f32[32,1920]{1,0:T(8,128)S(1)}, u32[]{:S(2)}, u32[]{:S(2)}) collective-permute-start(f32[32,1920]{1,0:T(8,128)S(1)} %get-tuple-element.50), channel_id=1, source_target_pairs={{0,4},{2,6},{4,0},{6,2},{1,5},{3,7},{5,1},{7,3},{8,12},{10,14},{12... | collective-permute-start | bytes 737288 | tf_op jit(solution)/shard_map/ppermute | solution.py:799
  5.1 1.3 %collective-permute-start.9 = (f32[16,512]{1,0:T(8,128)S(1)}, f32[16,512]{1,0:T(8,128)S(1)}, u32[]{:S(2)}, u32[]{:S(2)}) collective-permute-start(f32[16,512]{1,0:T(8,128)S(1)} %get-tuple-element.49), channel_id=1, source_target_pairs={{0,1},{2,3},{4,5},{6,7},{8,9},{10,11},{12,13},{14,15},{16,17},{18,... | collective-permute-start | bytes 98312 | tf_op jit(solution)/shard_map/ppermute | solution.py:791
  6.4 4.5 %collective-permute-done.9.prefix_ref = f32[16,512]{1,0:T(8,128)S(1)} collective-permute-done((f32[16,512]{1,0:T(8,128)S(1)}, f32[16,512]{1,0:T(8,128)S(1)}, u32[]{:S(2)}, u32[]{:S(2)}) %collective-permute-start.9) | collective-permute-done | bytes 32800 | tf_op jit(solution)/shard_map/ppermute | solution.py:791
  11.0 1.6 %collective-permute-start.10 = (f32[16,128]{1,0:T(8,128)S(1)}, f32[16,128]{1,0:T(8,128)S(1)}, u32[]{:S(2)}, u32[]{:S(2)}) collective-permute-start(f32[16,128]{1,0:T(8,128)S(1)} %get-tuple-element.54.own_east_ref), channel_id=1, source_target_pairs={{0,8},{8,16},{16,24},{24,0},{1,9},{9,17},{17,25},{25,1},{2,10},{10... | collective-permute-start | bytes 24584 | tf_op jit(solution)/shard_map/ppermute | solution.py:807
  12.5 2.2 %collective-permute-start.11 = (f32[16,128]{1,0:T(8,128)S(1)}, f32[16,128]{1,0:T(8,128)S(1)}, u32[]{:S(2)}, u32[]{:S(2)}) collective-permute-start(f32[16,128]{1,0:T(8,128)S(1)} %get-tuple-element.55.own_west_ref), channel_id=1, source_target_pairs={{8,0},{16,8},{24,16},{0,24},{9,1},{17,9},{25,17},{1,25},{10,2},{18... | collective-permute-start | bytes 24584 | tf_op jit(solution)/shard_map/ppermute | solution.py:808
  14.8 0.5 %slice.3 = s32[1]{0:T(128)} slice(s32[2048]{0:T(1024)S(1)} %copy-done.2), slice={[0:1]} | slice | bytes 8 | tf_op jit(solution)/shard_map/slice | solution.py:817
  16.0 0.5 collective-permute-done.10.from_west_ref
  16.4 1.4 %edge_rows.1 = (f32[12,8,512]{2,1,0:T(8,128)S(1)}, f32[12,8,512]{2,1,0:T(8,128)}) custom-call(f32[5,128,512]{2,1,0:T(8,128)S(1)} %bitcast.8, s32[128,512]{1,0:T(8,128)S(1)} %bitcast.12, f32[16,512]{1,0:T(8,128)S(1)} %collective-permute-done.9.prefix_ref, f32[16]{0:T(128)S(1)} %copy-done.3, f32[16,128]{1,0:T(8,128)S(1)} %collective-permute-done.10.from_west_ref, ...), custom_call_target="tpu_custom_call" | custom-call | tf_op jit(solution)/shard_map/edge_rows/pallas_call | solution.py:43
  17.9 3.5 %collective-permute-start.14 = (f32[12,8,512]{2,1,0:T(8,128)}, f32[12,8,512]{2,1,0:T(8,128)S(1)}, u32[]{:S(2)}, u32[]{:S(2)}) collective-permute-start(f32[12,8,512]{2,1,0:T(8,128)} %get-tuple-element.62), channel_id=1, source_target_pairs={{2,4},{4,2},{3,5},{5,3},{10,12},{12,10},{11,13},{13,11},{18,20},{2... | collective-permute-start | bytes 589832 | tf_op jit(solution)/shard_map/ppermute | solution.py:824
  21.5 2.4 %collective-permute-start.15 = (f32[16,1920]{1,0:T(8,128)S(1)}, f32[16,1920]{1,0:T(8,128)S(1)}, u32[]{:S(2)}, u32[]{:S(2)}) collective-permute-start(f32[16,1920]{1,0:T(8,128)S(1)} %get-tuple-element.60), channel_id=1, source_target_pairs={{0,16},{8,24},{16,0},{24,8},{1,17},{9,25},{17,1},{25,9},{2,18},{10... | collective-permute-start | bytes 368648 | tf_op jit(solution)/shard_map/ppermute | solution.py:799
  23.9 2.7 %conditional.1 = (f32[12,8,512]{2,1,0:T(8,128)}, f32[12,8,512]{2,1,0:T(8,128)}) conditional(s32[]{:T(128)} %clamp.3, f32[12,8,512]{2,1,0:T(8,128)} %get-tuple-element.62, f32[12,8,512]{2,1,0:T(8,128)} %get-tuple-element.62, f32[12,8,512]{2,1,0:T(8,128)} %get-tuple-element.62, f32[12,8,512]{2,1,0:T(8,128)} %get-tuple-element.62), branch_computations={%region_0.0_spmd, %region_1.0_spmd, %region_2.0_spmd, %region_3.0_... | conditional | bytes 1572960 | solution.py:839
  23.9 1.3 %collective-permute-start.3 = (f32[12,8,512]{2,1,0:T(8,128)}, f32[12,8,512]{2,1,0:T(8,128)}, u32[]{:S(2)}, u32[]{:S(2)}) collective-permute-start(f32[12,8,512]{2,1,0:T(8,128)} %param.1), channel_id=1, source_target_pairs={{6,6},{14,30},{22,22},{30,14},{7,7},{15,31},{23,23},{31,15}} | collective-permute-start | bytes 589832 | tf_op jit(solution)/shard_map/cond/branch_1_fun/ppermute | solution.py:829
  25.2 1.3 %collective-permute-start.2 = (f32[12,8,512]{2,1,0:T(8,128)}, f32[12,8,512]{2,1,0:T(8,128)}, u32[]{:S(2)}, u32[]{:S(2)}) collective-permute-start(f32[12,8,512]{2,1,0:T(8,128)} %param.1), channel_id=1, source_target_pairs={{6,14},{14,6},{22,30},{30,22},{7,15},{15,7},{23,31},{31,23}} | collective-permute-start | bytes 589832 | tf_op jit(solution)/shard_map/cond/branch_1_fun/ppermute | solution.py:829
  26.6 4.3 %collective-permute-done.15.got_ref = f32[16,1920]{1,0:T(8,128)S(1)} collective-permute-done((f32[16,1920]{1,0:T(8,128)S(1)}, f32[16,1920]{1,0:T(8,128)S(1)}, u32[]{:S(2)}, u32[]{:S(2)}) %collective-permute-start.15) | collective-permute-done | bytes 122912 | tf_op jit(solution)/shard_map/ppermute | solution.py:799
  30.9 1.6 %first_inside.1 = (f32[5,128,512]{2,1,0:T(8,128)S(1)}, f32[16,1024]{1,0:T(8,128)S(1)}) custom-call(f32[5,128,512]{2,1,0:T(8,128)S(1)} %bitcast.9, s32[128,512]{1,0:T(8,128)S(1)} %bitcast.13, f32[16,512]{1,0:T(8,128)S(1)} %collective-permute-done.9.prefix_ref, f32[16]{0:T(128)S(1)} %copy-done.3, f32[8]{0:T(128)S(1)} %copy-done.4), custom_call_target="tpu_custom_call" | custom-call | tf_op jit(solution)/shard_map/first_inside/pallas_call | solution.py:43
  32.5 2.7 %collective-permute-done.16 = f32[8,1920]{1,0:T(8,128)S(1)} collective-permute-done((f32[8,1920]{1,0:T(8,128)S(1)}, f32[8,1920]{1,0:T(8,128)S(1)}, u32[]{:S(2)}, u32[]{:S(2)}) %collective-permute-start.16) | collective-permute-done | bytes 61472 | tf_op jit(solution)/shard_map/ppermute | solution.py:799
  35.4 2.9 %first_rim.1 = (f32[2,6,8,512]{3,2,1,0:T(8,128)S(1)}, f32[2,16,128]{2,1,0:T(8,128)S(1)}, f32[2,5,8,512]{3,2,1,0:T(8,128)S(1)}, f32[2,16,128]{2,1,0:T(8,128)S(1)}, f32[24,1280]{1,0:T(8,128)S(1)}) custom-call(f32[5,128,512]{2,1,0:T(8,128)S(1)} %bitcast.10, s32[128,512]{1,0:T(8,128)S(1)} %bitcast.14, f32[16,512]{1,0:T(8,128)S(1)} %collective-permute-done.9.prefix_ref, ...), custom_call_target="tpu_custom_call" | custom-call | tf_op jit(solution)/shard_map/first_rim/pallas_call | solution.py:43
  38.2 1.3 %collective-permute-done.17.theirs_ref = f32[8,1920]{1,0:T(8,128)S(1)} collective-permute-done((f32[8,1920]{1,0:T(8,128)S(1)}, f32[8,1920]{1,0:T(8,128)S(1)}, u32[]{:S(2)}, u32[]{:S(2)}) %collective-permute-start.17) | collective-permute-done | bytes 61472 | tf_op jit(solution)/shard_map/ppermute | solution.py:855
  39.6 1.3 %collective-permute-start.18 = (f32[24,1280]{1,0:T(8,128)S(1)}, f32[24,1280]{1,0:T(8,128)S(1)}, u32[]{:S(2)}, u32[]{:S(2)}) collective-permute-start(f32[24,1280]{1,0:T(8,128)S(1)} %get-tuple-element.81), channel_id=1, source_target_pairs={{0,1},{2,3},{4,5},{6,7},{8,9},{10,11},{12,13},{14,15},{16,17},{18,... | collective-permute-start | bytes 368648 | tf_op jit(solution)/shard_map/ppermute | solution.py:877
  40.9 3.0 %second_substep.1 = (f32[5,128,512]{2,1,0:T(8,128)}, f32[2,128,512]{2,1,0:T(8,128)S(1)}, f32[24,640]{1,0:T(8,128)S(1)}) custom-call(f32[5,128,512]{2,1,0:T(8,128)S(1)} %get-tuple-element.69.state_ref, s32[128,512]{1,0:T(8,128)S(1)} %bitcast.15, f32[2,6,8,512]{3,2,1,0:T(8,128)S(1)} %get-tuple-element.74.ring_rows_ref, ...), custom_call_target="tpu_custom_call" | custom-call | tf_op jit(solution)/shard_map/second_substep/pallas_call | solution.py:43
  43.9 2.4 %collective-permute-done.18.sums_ref = f32[24,1280]{1,0:T(8,128)S(1)} collective-permute-done((f32[24,1280]{1,0:T(8,128)S(1)}, f32[24,1280]{1,0:T(8,128)S(1)}, u32[]{:S(2)}, u32[]{:S(2)}) %collective-permute-start.18) | collective-permute-done | bytes 122912 | tf_op jit(solution)/shard_map/ppermute | solution.py:877
  46.3 1.0 %deeper_pressure.1 = f32[5,128,512]{2,1,0:T(8,128)} custom-call(f32[5,128,512]{2,1,0:T(8,128)} %get-tuple-element.78.out_in_hbm, f32[2,128,512]{2,1,0:T(8,128)S(1)} %get-tuple-element.79.flow_ref, s32[128,512]{1,0:T(8,128)S(1)} %bitcast.16, f32[24,1280]{1,0:T(8,128)S(1)} %collective-permute-done.18.sums_ref, ...), custom_call_target="tpu_custom_call", output_to_operand_aliasing={{}: (0, {})} | custom-call | tf_op jit(solution)/shard_map/deeper_pressure/pallas_call | solution.py:43
  (25 shorter events, 0.5 us)
Async XLA Ops:
  0.0 14.8 %copy-start.2 = (s32[2048]{0:T(1024)S(1)}, s32[2048]{0:T(1024)}, u32[]{:S(2)}) copy-start(s32[2048]{0:T(1024)} %partner_ref.3) | copy-start | bytes 24580
  0.0 16.4 %copy-start = (f32[5,8,16,512]{3,2,1,0:T(8,128)S(1)}, f32[5,8,16,512]{3,2,1,0:T(8,128)}, u32[]{:S(2)}) copy-start(f32[5,8,16,512]{3,2,1,0:T(8,128)} %param.12) | copy-start | bytes 3932164
  0.0 16.4 %copy-start.1 = (s32[8,16,512]{2,1,0:T(8,128)S(1)}, s32[8,16,512]{2,1,0:T(8,128)}, u32[]{:S(2)}) copy-start(s32[8,16,512]{2,1,0:T(8,128)} %param.13) | copy-start | bytes 786436
  0.0 16.4 %copy-start.3 = (f32[16]{0:T(128)S(1)}, f32[16]{0:T(128)}, u32[]{:S(2)}) copy-start(f32[16]{0:T(128)} %turn_ref.7) | copy-start | bytes 196
  2.5 1.9 %collective-permute-start.8 = (f32[64,1920]{1,0:T(8,128)S(1)}, f32[64,1920]{1,0:T(8,128)S(1)}, u32[]{:S(2)}, u32[]{:S(2)}) collective-permute-start(f32[64,1920]{1,0:T(8,128)S(1)} %get-tuple-element.47), channel_id=1, source_target_pairs={{0,2},{2,0},{4,6},{6,4},{1,3},{3,1},{5,7},{7,5},{8,10},{10,8},{12,... | collective-permute-start | bytes 1474568 | tf_op jit(solution)/shard_map/ppermute | solution.py:790
  4.5 26.4 %copy-start.4 = (f32[8]{0:T(128)S(1)}, f32[8]{0:T(128)}, u32[]{:S(2)}) copy-start(f32[8]{0:T(128)} %share_ref.5) | copy-start | bytes 100
  4.5 13.3 %collective-permute-start.12 = (f32[32,1920]{1,0:T(8,128)S(1)}, f32[32,1920]{1,0:T(8,128)S(1)}, u32[]{:S(2)}, u32[]{:S(2)}) collective-permute-start(f32[32,1920]{1,0:T(8,128)S(1)} %get-tuple-element.50), channel_id=1, source_target_pairs={{0,4},{2,6},{4,0},{6,2},{1,5},{3,7},{5,1},{7,3},{8,12},{10,14},{12... | collective-permute-start | bytes 737288 | tf_op jit(solution)/shard_map/ppermute | solution.py:799
  5.1 5.8 %collective-permute-start.9 = (f32[16,512]{1,0:T(8,128)S(1)}, f32[16,512]{1,0:T(8,128)S(1)}, u32[]{:S(2)}, u32[]{:S(2)}) collective-permute-start(f32[16,512]{1,0:T(8,128)S(1)} %get-tuple-element.49), channel_id=1, source_target_pairs={{0,1},{2,3},{4,5},{6,7},{8,9},{10,11},{12,13},{14,15},{16,17},{18,... | collective-permute-start | bytes 98312 | tf_op jit(solution)/shard_map/ppermute | solution.py:791
  11.0 5.5 %collective-permute-start.10 = (f32[16,128]{1,0:T(8,128)S(1)}, f32[16,128]{1,0:T(8,128)S(1)}, u32[]{:S(2)}, u32[]{:S(2)}) collective-permute-start(f32[16,128]{1,0:T(8,128)S(1)} %get-tuple-element.54.own_east_ref), channel_id=1, source_target_pairs={{0,8},{8,16},{16,24},{24,0},{1,9},{9,17},{17,25},{25,1},{2,10},{10... | collective-permute-start | bytes 24584 | tf_op jit(solution)/shard_map/ppermute | solution.py:807
  12.5 3.9 %collective-permute-start.11 = (f32[16,128]{1,0:T(8,128)S(1)}, f32[16,128]{1,0:T(8,128)S(1)}, u32[]{:S(2)}, u32[]{:S(2)}) collective-permute-start(f32[16,128]{1,0:T(8,128)S(1)} %get-tuple-element.55.own_west_ref), channel_id=1, source_target_pairs={{8,0},{16,8},{24,16},{0,24},{9,1},{17,9},{25,17},{1,25},{10,2},{18... | collective-permute-start | bytes 24584 | tf_op jit(solution)/shard_map/ppermute | solution.py:808
  17.8 8.7 %collective-permute-start.13 = (f32[12,8,512]{2,1,0:T(8,128)S(1)}, f32[12,8,512]{2,1,0:T(8,128)S(1)}, u32[]{:S(2)}, u32[]{:S(2)}) collective-permute-start(f32[12,8,512]{2,1,0:T(8,128)S(1)} %get-tuple-element.61), channel_id=1, source_target_pairs={{0,2},{2,0},{4,6},{6,4},{1,3},{3,1},{5,7},{7,5},{8,10},{10,8},{12,... | collective-permute-start | bytes 589832 | tf_op jit(solution)/shard_map/ppermute | solution.py:823
  17.9 8.6 %collective-permute-start.14 = (f32[12,8,512]{2,1,0:T(8,128)}, f32[12,8,512]{2,1,0:T(8,128)S(1)}, u32[]{:S(2)}, u32[]{:S(2)}) collective-permute-start(f32[12,8,512]{2,1,0:T(8,128)} %get-tuple-element.62), channel_id=1, source_target_pairs={{2,4},{4,2},{3,5},{5,3},{10,12},{12,10},{11,13},{13,11},{18,20},{2... | collective-permute-start | bytes 589832 | tf_op jit(solution)/shard_map/ppermute | solution.py:824
  21.5 9.4 %collective-permute-start.15 = (f32[16,1920]{1,0:T(8,128)S(1)}, f32[16,1920]{1,0:T(8,128)S(1)}, u32[]{:S(2)}, u32[]{:S(2)}) collective-permute-start(f32[16,1920]{1,0:T(8,128)S(1)} %get-tuple-element.60), channel_id=1, source_target_pairs={{0,16},{8,24},{16,0},{24,8},{1,17},{9,25},{17,1},{25,9},{2,18},{10... | collective-permute-start | bytes 368648 | tf_op jit(solution)/shard_map/ppermute | solution.py:799
  23.9 2.7 %collective-permute-start.3 = (f32[12,8,512]{2,1,0:T(8,128)}, f32[12,8,512]{2,1,0:T(8,128)}, u32[]{:S(2)}, u32[]{:S(2)}) collective-permute-start(f32[12,8,512]{2,1,0:T(8,128)} %param.1), channel_id=1, source_target_pairs={{6,6},{14,30},{22,22},{30,14},{7,7},{15,31},{23,23},{31,15}} | collective-permute-start | bytes 589832 | tf_op jit(solution)/shard_map/cond/branch_1_fun/ppermute | solution.py:829
  25.2 1.3 %collective-permute-start.2 = (f32[12,8,512]{2,1,0:T(8,128)}, f32[12,8,512]{2,1,0:T(8,128)}, u32[]{:S(2)}, u32[]{:S(2)}) collective-permute-start(f32[12,8,512]{2,1,0:T(8,128)} %param.1), channel_id=1, source_target_pairs={{6,14},{14,6},{22,30},{30,22},{7,15},{15,7},{23,31},{31,23}} | collective-permute-start | bytes 589832 | tf_op jit(solution)/shard_map/cond/branch_1_fun/ppermute | solution.py:829
  30.8 4.4 %collective-permute-start.16 = (f32[8,1920]{1,0:T(8,128)S(1)}, f32[8,1920]{1,0:T(8,128)S(1)}, u32[]{:S(2)}, u32[]{:S(2)}) collective-permute-start(f32[8,1920]{1,0:T(8,128)S(1)} %get-tuple-element.66), channel_id=1, source_target_pairs={{0,8},{8,0},{16,24},{24,16},{1,9},{9,1},{17,25},{25,17},{2,10},{10... | collective-permute-start | bytes 184328 | tf_op jit(solution)/shard_map/ppermute | solution.py:799
  35.3 4.3 %collective-permute-start.17 = (f32[8,1920]{1,0:T(8,128)S(1)}, f32[8,1920]{1,0:T(8,128)S(1)}, u32[]{:S(2)}, u32[]{:S(2)}) collective-permute-start(f32[8,1920]{1,0:T(8,128)S(1)} %add.3.mine_ref), channel_id=1, source_target_pairs={{0,1},{1,0},{2,3},{3,2},{4,5},{5,4},{6,7},{7,6},{8,9},{9,8},{10,11... | collective-permute-start | bytes 184328 | tf_op jit(solution)/shard_map/ppermute | solution.py:855
  39.6 6.8 %collective-permute-start.18 = (f32[24,1280]{1,0:T(8,128)S(1)}, f32[24,1280]{1,0:T(8,128)S(1)}, u32[]{:S(2)}, u32[]{:S(2)}) collective-permute-start(f32[24,1280]{1,0:T(8,128)S(1)} %get-tuple-element.81), channel_id=1, source_target_pairs={{0,1},{2,3},{4,5},{6,7},{8,9},{10,11},{12,13},{14,15},{16,17},{18,... | collective-permute-start | bytes 368648 | tf_op jit(solution)/shard_map/ppermute | solution.py:877

commit v3 on v2

--- a/solution.py
+++ b/solution.py
@@ -267,8 +267,10 @@
     out_ref[CORNERS, 4:5, :] = prefix_ref[far : far + 1, :]
 
 
-def rows_kernel(state_ref, mask_ref, prefix_ref, turn_ref, from_west_ref, from_east_ref, pair_ref, cross_ref):
-    rows = prefix_ref.shape[0]
+def rows_kernel(
+    state_ref, mask_ref, prefix_ref, turn_ref, from_west_ref, from_east_ref, pair_ref, cross_ref, top_ref
+):
+    rows, cols = prefix_ref.shape
     odd = lax.rem(lax.axis_index("lat"), 2) == 1
 
     def fill(out_ref, near, far):
@@ -279,11 +281,25 @@
     def _():
         fill(pair_ref, 0, 1)
         fill(cross_ref, rows - 1, rows - 2)
+        sub, lane = iota((DEEP, LANES), 0), iota((DEEP, LANES), 1)
+        pieces = cols // LANES
+        for piece in range(pieces):
+            top_ref[piece] = cross_ref[:, :, piece * LANES : (piece + 1) * LANES]
+            if piece < pieces - 1:
+                beyond = (piece + 1) * LANES
+                line = jnp.zeros((DEEP, LANES), F32)
+                for f in range(5):
+                    line = jnp.where(lane == f * DEEP + sub, cross_ref[2 * f, :, beyond : beyond + 1], line)
+                line = jnp.where((lane == ABOVE) & (sub == 3), cross_ref[CORNERS, :, beyond : beyond + 1], line)
+                top_ref[piece, CORNERS, 1:2, :] = jnp.sum(line, axis=0, keepdims=True)
+            else:
+                top_ref[piece, CORNERS, 1:2, :] = from_east_ref[rows - 1 : rows, :]
 
     @pl.when(jnp.logical_not(odd))
     def _():
         fill(pair_ref, rows - 1, rows - 2)
         fill(cross_ref, 0, 1)
+        top_ref[...] = jnp.zeros(top_ref.shape, F32)
 
 
 def around(value, west, east, south, north):
@@ -392,17 +408,13 @@
     return jnp.sum(here, axis=1, keepdims=True)
 
 
-def inside_kernel(state_ref, mask_ref, prefix_ref, turn_ref, share_ref, new_ref, sums_ref):
-    rows, cols = prefix_ref.shape
+def inside_kernel(state_ref, mask_ref, turn_ref, share_ref, new_ref, sums_ref):
+    rows, cols = sums_ref.shape[0], state_ref.shape[2]
     n_r, n_j = rows // DEEP, cols // LANES
     turn = turn_column(turn_ref, rows)
     grid = [(r, j) for r in range(n_r) for j in range(n_j)]
     zero = jnp.zeros((DEEP, LANES), F32)
-    prefix = Tiles([[prefix_ref[tile(r, j, 0, rows)] for j in range(n_j)] for r in range(n_r)])
-    run = {}
-    for at in grid:
-        east, west, north, south = prefix.around(*at)
-        run[at] = [0.5 * (east - west), 0.5 * (north - south), zero, zero]
+    run = {at: [zero] * 4 for at in grid}
     for k in range(DEEP):
         fields = [Tiles([[state_ref[(f, *tile(r, j, k, rows))] for j in range(n_j)] for r in range(n_r)]) for f in range(5)]
         for r, j in grid:
@@ -435,14 +447,13 @@
 
 def rim_kernel(
     n_lat, state_ref, mask_ref, prefix_ref, turn_ref, share_ref, partner_ref, own_west_ref, own_east_ref,
-    from_west_ref, from_east_ref, pair_ref, cross_ref, first_ref, second_ref, inside_ref, ring_rows_ref, ring_cols_ref,
+    from_west_ref, from_east_ref, pair_ref, cross_ref, fold_ref, inside_ref, ring_rows_ref, ring_cols_ref,
     edge_rows_ref, edge_cols_ref, sums_ref, south_ref, north_ref,
 ):
     rows, cols = prefix_ref.shape
     lat = lax.axis_index("lat")
     odd = lax.rem(lat, 2) == 1
-    hinge = partner_ref[0]
-    within = hinge - (hinge // cols) * cols
+    within = partner_ref[0] & (LANES - 1)
     at_top = lat == n_lat - 1
 
     @pl.when(odd)
@@ -473,8 +484,8 @@
         west = jnp.zeros((DEEP, LANES), F32)
         east = jnp.zeros((DEEP, LANES), F32)
         for slab in range(SLABS + 1):
-            row = jnp.concatenate([second_ref[slab], first_ref[slab]], axis=1)
-            row = pltpu.roll(row, 2 * cols - 1 - within, 1)
+            row = jnp.concatenate([fold_ref[piece, slab] for piece in range(fold_ref.shape[0])], axis=1)
+            row = pltpu.roll(row, cols + LANES - 1 - within, 1)
             if slab < 4:
                 row = -row
             north_ref[slab] = mirrored(row, cols)
@@ -485,10 +496,10 @@
             else:
                 continue
             west = jnp.where(here, row[:, cols : cols + 1], west)
-            east = jnp.where(here, row[:, 2 * cols - 1 :], east)
-        beyond = first_ref[CORNERS, 1:2, 0:LANES]
+            east = jnp.where(here, row[:, cols + LANES - 1 :], east)
+        beyond = fold_ref[fold_ref.shape[0] - 1, CORNERS, 1:2, :]
         beyond = jnp.where(iota((1, LANES), 1) < 16, -beyond, beyond)
-        west = jnp.where(within == cols - 1, beyond, jnp.sum(west, axis=0, keepdims=True))
+        west = jnp.where(within == LANES - 1, beyond, jnp.sum(west, axis=0, keepdims=True))
         north_ref[CORNERS, 0:1, 0:LANES] = west
         north_ref[CORNERS, 1:2, 0:LANES] = jnp.sum(east, axis=0, keepdims=True)
         north_ref[CORNERS, 2:3, :] = jnp.full((1, cols), turn_ref[rows - 1], F32)
@@ -581,7 +592,7 @@
     blocks = [jnp.zeros((rows, LANES), F32)] * 2
     sides = ((0, from_west_ref, own_west_ref), (1, from_east_ref, own_east_ref))
     for side, ghost_ref, own_ref in sides:
-        near, own = ghost_ref[...], own_ref[...]
+        near, own = ghost_ref[0:rows, :], own_ref[0:rows, :]
         far, own_next = roll(near, -FAR, 1), roll(own, -FAR, 1)
         north = jnp.where(row == rows - 1, north_ref[CORNERS, side : side + 1, 0:LANES], roll(near, -1, 0))
         south = jnp.where(row == 0, south_ref[CORNERS, side : side + 1, 0:LANES], roll(near, 1, 0))
@@ -602,12 +613,8 @@
         sums_ref[edge : edge + 1, 0:cols] = jnp.sum(here, axis=0, keepdims=True)
 
 
-def second_kernel(
-    n_lat, state_ref, mask_ref, ring_rows_ref, ring_cols_ref, edge_rows_ref, edge_cols_ref, mine_ref, theirs_ref,
-    turn_ref, share_ref, partner_ref, out_hbm, flow_ref, drive_ref, tracers_ref, sem,
-):
-    rows, cols = mask_ref.shape[0] // DEEP, mask_ref.shape[1]
-    n_r, n_j = rows // DEEP, cols // LANES
+def flux_kernel(n_lat, mine_ref, theirs_ref, partner_ref, flux_ref, flux_rows_ref, flux_cols_ref, drive_ref):
+    rows, cols = flux_ref.shape[1:]
     half_cols = cols // 2
     wide = 3 * half_cols
     mine, theirs = mine_ref[...], theirs_ref[...]
@@ -627,8 +634,6 @@
         return jnp.concatenate(found, axis=1)
 
     flux, flux_south, flux_north, flux_west, flux_east = [], [], [], [], []
-    sub8 = iota((DEEP, LANES), 0)
-    lane8 = iota((DEEP, LANES), 1)
     crossed = jnp.zeros((DEEP, 2 * cols), F32)
     for c in range(3):
         pair = jnp.concatenate([extra(2, c), extra(1, c)], axis=1)
@@ -648,6 +653,31 @@
             line = part[6:7, 2 * wide : 2 * wide + LANES]
             side.append(jnp.sum(jnp.where(here, line, 0.0), axis=1, keepdims=True))
 
+    flux_cols = jnp.zeros((rows, LANES), F32)
+    for c in range(3):
+        flux_ref[c] = flux[c]
+        flux_rows_ref[c : c + 1, :] = flux_south[c]
+        flux_rows_ref[3 + c : 4 + c, :] = flux_north[c]
+        flux_cols = jnp.where(lane == c, flux_west[c], jnp.where(lane == 3 + c, flux_east[c], flux_cols))
+    flux_rows_ref[6:8, :] = jnp.zeros((2, cols), F32)
+    flux_cols_ref[...] = flux_cols
+    drive_ref[rows:, :] = jnp.zeros((DEEP, cols + LANES), F32)
+    drive_ref[0:rows, 0:cols] = buoyancy_of(flux[0], flux[1])
+    ends = jnp.zeros((rows, LANES), F32)
+    for side, column, line in ((0, flux_west, flux_south), (1, flux_east, flux_north)):
+        drive_ref[rows + side : rows + side + 1, 0:cols] = buoyancy_of(line[0], line[1])
+        ends = jnp.where(lane == side, buoyancy_of(column[0], column[1]), ends)
+    drive_ref[0:rows, cols:] = ends
+
+
+def second_kernel(
+    state_ref, mask_ref, prefix_ref, ring_rows_ref, ring_cols_ref, edge_rows_ref, edge_cols_ref, flux_ref, flux_rows_ref,
+    flux_cols_ref, turn_ref, share_ref, out_hbm, flow_ref, tracers_ref, sem,
+):
+    rows, cols = flux_ref.shape[1:]
+    n_r, n_j = rows // DEEP, cols // LANES
+    sub8, lane8 = iota((DEEP, LANES), 0), iota((DEEP, LANES), 1)
+    lane = iota((rows, LANES), 1)
     turn = turn_column(turn_ref, rows)
     share_down = jnp.zeros((DEEP, LANES), F32)
     share_lanes = jnp.zeros((rows, LANES), F32)
@@ -655,22 +685,17 @@
         share_down = jnp.where(sub8 == k, share_ref[k], share_down)
         share_lanes = jnp.where((lane & 7) == k, share_ref[k], share_lanes)
 
-    drive_ref[...] = jnp.zeros(drive_ref.shape, F32)
-    drive_ref[0:rows, 0:cols] = buoyancy_of(flux[0], flux[1])
-
     ring_rows, ring_cols = [], []
-    for side, source in ((0, flux_south), (1, flux_north)):
+    for side in range(2):
         taken = ring_rows_ref[side, 5] * share_down[:, 0:1]
         values = [ring_rows_ref[side, f] for f in range(2)]
-        ring_rows.append(values + [ring_rows_ref[side, 2 + c] + taken * source[c] for c in range(3)])
-        drive_ref[rows + side : rows + side + 1, 0:cols] = buoyancy_of(source[0], source[1])
-    for side, source in ((0, flux_west), (1, flux_east)):
+        values += [ring_rows_ref[side, 2 + c] + taken * flux_rows_ref[3 * side + c : 3 * side + c + 1, :] for c in range(3)]
+        ring_rows.append(values)
         found = ring_cols_ref[side]
         taken = lanes_between(found, WET, WET + 8) * share_lanes
         for c in range(3):
-            found = found + roll(taken, 8 * (2 + c) - WET, 1) * source[c]
+            found = found + roll(taken, 8 * (2 + c) - WET, 1) * flux_cols_ref[:, 3 * side + c : 3 * side + c + 1]
         ring_cols.append(found)
-        drive_ref[0:rows, cols + side : cols + side + 1] = buoyancy_of(source[0], source[1])
 
     grid = [(r, j) for r in range(n_r) for j in range(n_j)]
 
@@ -679,6 +704,11 @@
 
     zero = jnp.zeros((DEEP, LANES), F32)
     run = {at: (zero, zero) for at in grid}
+    prefix = Tiles([[prefix_ref[tile(r, j, 0, rows)] for j in range(n_j)] for r in range(n_r)])
+    push = {}
+    for at in grid:
+        east, west, north, south = prefix.around(*at)
+        push[at] = (0.5 * PRESS) * (east - west), (0.5 * PRESS) * (north - south)
     edge_cols = [edge_cols_ref[side] for side in range(2)]
     copies = []
 
@@ -692,9 +722,11 @@
             wet = mask_ref[at].astype(F32)
             taken = wet * share_ref[k]
             wets[r, j] = wet
-            heats[r, j] = [taken * cut(flux[c], r, j) for c in range(3)]
+            heats[r, j] = [taken * cut(flux_ref[c], r, j) for c in range(3)]
             for f in range(5):
                 value = state_ref[(f, *at)]
+                if f < 2:
+                    value = value - wet * push[r, j][f]
                 if j == 0:
                     value = jnp.where(lane8 == 0, column(edge_cols[0], r, f * DEEP + k), value)
                 if j == n_j - 1:
@@ -798,6 +830,17 @@
         axis, size, bit = stage
         return lax.ppermute(send, axis, [(i, i ^ bit) for i in range(size)])
 
+    near_state, near_mask = after((flat_state, flat_mask), send)
+    new_state, inside = call(
+        inside_kernel,
+        (shape(fields, levels * rows, cols), shape(rows, 2 * cols)),
+        [VMEM, VMEM, SMEM, SMEM],
+        (near_state, near_mask, coriolis, penetration),
+        name="first_inside",
+    )
+    pieces = cols // LANES
+    hinge_piece = fold_partner[0] >> (LANES.bit_length() - 1)
+    keep = after(keep, (prefix, hinge_piece, inside))
     keep, send = merged(keep, got)
     got = passed_on(send, stages[0])
 
@@ -807,54 +850,40 @@
     from_west = lax.ppermute(east, "lon", [(i, (i + 1) % n_lon) for i in range(n_lon)])
     from_east = lax.ppermute(west, "lon", [((i + 1) % n_lon, i) for i in range(n_lon)])
     message = shape(SLABS + 1, DEEP, cols)
-    pair, cross = call(
+    pair, cross, top = call(
         rows_kernel,
-        (message, message),
+        (message, message, shape(pieces, SLABS + 1, DEEP, LANES)),
         [VMEM, VMEM, VMEM, SMEM, VMEM, VMEM],
         (flat_state, flat_mask, prefix, coriolis, from_west, from_east),
         name="edge_rows",
     )
-    hinge_block = fold_partner[0] >> (cols.bit_length() - 1)
-    keep = after(keep, (pair, cross, hinge_block))
+    from_pair = lax.ppermute(pair, "lat", [(i, i ^ 1) for i in range(n_lat)])
+    from_cross = lax.ppermute(cross, "lat", [(i, i + 1 if i % 2 else i - 1) for i in range(1, last)])
+    keep = after(keep, (pair, cross, top))
     keep, send = merged(keep, got)
     got = passed_on(send, stages[1])
 
-    pair, cross = after((pair, cross), send)
-    from_pair = lax.ppermute(pair, "lat", [(i, i ^ 1) for i in range(n_lat)])
-    from_cross = lax.ppermute(cross, "lat", [(i, i + 1 if i % 2 else i - 1) for i in range(1, last)])
-
-    def folded(block):
+    top = after(top, send)
+
+    def folded(hinge_piece):
+        block, piece = divmod(hinge_piece, pieces)
+
         def swap(rows_out):
-            return tuple(
-                lax.ppermute(
-                    rows_out,
-                    ("lon", "lat"),
-                    [(a * n_lat + last, (block - more - a) % n_lon * n_lat + last) for a in range(n_lon)],
-                )
-                for more in (0, 1)
-            )
+            def across(part, other):
+                pairs = [(a * n_lat + last, (other - a) % n_lon * n_lat + last) for a in range(n_lon)]
+                return lax.ppermute(part, ("lon", "lat"), pairs)
+
+            return jnp.concatenate([across(rows_out[piece:], block - 1), across(rows_out[: piece + 1], block)], axis=0)
 
         return swap
 
-    first, second = lax.switch(hinge_block, [folded(block) for block in range(n_lon)], cross)
-    keep = after(keep, (from_pair, from_cross, first, second))
+    fold = lax.switch(hinge_piece, [folded(n) for n in range(n_lon * pieces)], top)
+    keep = after(keep, (fold, from_pair, from_cross))
     for stage in stages[2:]:
         keep, send = merged(keep, got)
         got = passed_on(send, stage)
 
-    near_state, near_mask = after((flat_state, flat_mask), send)
-    new_state, inside = call(
-        inside_kernel,
-        (shape(fields, levels * rows, cols), shape(rows, 2 * cols)),
-        [VMEM, VMEM, VMEM, SMEM, SMEM],
-        (near_state, near_mask, prefix, coriolis, penetration),
-        name="first_inside",
-    )
-    keep = after(keep, inside)
-    mine = keep + got
-    theirs = lax.ppermute(mine, "lev", [(0, 1), (1, 0)])
-
-    inside = after(inside, mine)
+    inside = after(inside, send)
     wide = cols + LANES
     *ring, sums = call(
         functools.partial(rim_kernel, n_lat),
@@ -865,26 +894,35 @@
             shape(2, rows, LANES),
             shape(rows + DEEP, 2 * wide),
         ),
-        [VMEM, VMEM, VMEM, SMEM, SMEM, SMEM] + [VMEM] * 9,
+        [VMEM, VMEM, VMEM, SMEM, SMEM, SMEM] + [VMEM] * 8,
         (
             flat_state, flat_mask, prefix, coriolis, penetration, fold_partner, west, east, from_west, from_east, from_pair,
-            from_cross, first, second, inside,
+            from_cross, fold, inside,
         ),
         [pltpu.VMEM((SLABS + 1, DEEP, cols), F32), pltpu.VMEM((SLABS + 1, DEEP, cols), F32)],
         name="first_rim",
     )
-    sums = after(sums, theirs)
-    sums = lax.ppermute(sums, "lev", [(0, 1)])
+    keep = after(keep, sums)
+    mine = keep + got
+    theirs = lax.ppermute(mine, "lev", [(0, 1), (1, 0)])
+    sums = lax.ppermute(after(sums, mine), "lev", [(0, 1)])
+    *flux, drive = call(
+        functools.partial(flux_kernel, n_lat),
+        (shape(3, rows, cols), shape(DEEP, cols), shape(rows, LANES), shape(rows + DEEP, wide)),
+        [VMEM] * 2 + [SMEM],
+        (mine, theirs, fold_partner),
+        name="flux_parts",
+    )
 
     out = jax.ShapeDtypeStruct(flat_state.shape, F32)
-    result, flow, drive = call(
-        functools.partial(second_kernel, n_lat),
-        (out, shape(2, levels * rows, cols), shape(rows + DEEP, wide)),
-        [VMEM] * 8 + [SMEM] * 3,
-        (new_state, flat_mask, *ring, mine, theirs, coriolis, penetration, fold_partner),
+    result, flow = call(
+        second_kernel,
+        (out, shape(2, levels * rows, cols)),
+        [VMEM] * 10 + [SMEM] * 2,
+        (new_state, flat_mask, prefix, *ring, *flux, coriolis, penetration),
         [pltpu.VMEM((3, levels * rows, cols), F32), pltpu.SemaphoreType.DMA((DEEP,))],
         name="second_substep",
-        out_specs=(ANY, VMEM, VMEM),
+        out_specs=(ANY, VMEM),
     )
     result = call(
         last_kernel,

time: 47.3 us -> 53.2 us (1.12); the launches traced: 47.3 us -> 53.9 us
  waiting for transfers between devices: 17.6 us -> 20.1 us
  local copies, waits for them, and re-layouts: 0.53 us -> 2.93 us
  Pallas kernels: 12.5 us -> 14.7 us
  starting transfers between devices: 15.8 us -> 14.5 us
  other arithmetic: 0.01 us -> 0.72 us
    ppermute x1, waiting for transfers between devices: 1.33 us -> 5.14 us  [body(): theirs = lax.ppermute(mine, 'lev', [(0, 1), (1, 0)])]
    ppermute x1, waiting for transfers between devices: 0.46 us -> 4.08 us  [body(): lax.ppermute(east, 'lon', [(i, (i + 1) % n_lon) for i in range(n_lon)])]
    ppermute x1, waiting for transfers between devices: 4.51 us -> 1.69 us  [body(): prefix = lax.ppermute(total, 'lev', [(0, 1)])]
    ppermute x1, starting transfers between devices: 0.07 us -> 2.71 us  [body(): theirs = lax.ppermute(mine, 'lev', [(0, 1), (1, 0)])]
    ppermute x3, waiting for transfers between devices: 2.45 us -> 0.01 us  [the longest x2 0.01 us: across(): return lax.ppermute(part, ('lon', 'lat'), pairs)]
    ppermute x3, starting transfers between devices: 3.07 us -> 0.64 us  [passed_on(): return lax.ppermute(send, axis, [(i, i ^ bit) for i in range(size)])]
    unnamed x10 -> x18, local copies, waits for them, and re-layouts: 0.02 us -> 2.4 us
    pallas_call x10 -> x11, Pallas kernels: 12.5 us -> 14.7 us  [call(): pl.pallas_call(kernel, out_shape=out_shape, in_specs=in_specs, out_specs=...]
  transfers between devices with their start and end apart: 13 -> 13, of which waited for: 7 -> 7; matrix products, arithmetic and copies ran while one was open for 1% -> 2% of each run, Pallas kernels for 19% -> 19%
where the time goes in v3:
time: 53.2 us; the launch traced here: 53.9 us
  waiting for transfers between devices  20.1 us (38%)
  Pallas kernels  14.7 us (28%)
  starting transfers between devices  14.5 us (27%)
  local copies, waits for them, and re-layouts  2.93 us (6%)
  between operations  0.83 us (2%)
  other arithmetic  0.72 us (1%)
    pallas_call x11, Pallas kernels, call(): pl.pallas_call(kernel, out_shape=out_shape, in_specs=in_specs, out_specs=...  14.7 us
    ppermute x3, waiting for transfers between devices, passed_on(): return lax.ppermute(send, axis, [(i, i ^ bit) for i in range(size)])  7.63 us
    ppermute x1, waiting for transfers between devices, body(): theirs = lax.ppermute(mine, 'lev', [(0, 1), (1, 0)])  5.14 us
    ppermute x1, waiting for transfers between devices, body(): lax.ppermute(east, 'lon', [(i, (i + 1) % n_lon) for i in range(n_lon)])  4.08 us
    ppermute x1, starting transfers between devices, body(): lax.ppermute(west, 'lon', [((i + 1) % n_lon, i) for i in range(n_lon)])  3.61 us
    ppermute x1, starting transfers between devices, body(): lax.ppermute(cross, 'lat', [(i, i + 1 if i % 2 else i - 1) for i in range...  3.53 us
    ppermute x1, starting transfers between devices, body(): theirs = lax.ppermute(mine, 'lev', [(0, 1), (1, 0)])  2.71 us
    unnamed x18, local copies, waits for them, and re-layouts  2.4 us
  transfers between devices with their start and end apart: 13, of which 7 were waited for; matrix products, arithmetic and copies ran while one was open for 2% of the time, Pallas kernels for 19%

profile of v3, /device:TPU:6, one launch (start us, length us, event | category | flops | bytes accessed | tf_op | source)
XLA Modules:
  0.0 53.9 jit_solution(17718077513187476000)
XLA Ops:
  0.0 2.5 %prepare.1 = (f32[64,1920]{1,0:T(8,128)S(1)}, f32[64,1920]{1,0:T(8,128)S(1)}, f32[16,128]{1,0:T(8,128)S(1)}, f32[16,128]{1,0:T(8,128)S(1)}, f32[16,512]{1,0:T(8,128)S(1)}) custom-call(f32[5,128,512]{2,1,0:T(8,128)} %bitcast.7, s32[128,512]{1,0:T(8,128)} %bitcast.11, f32[3,128,512]{2,1,0:T(8,128)} %bitcast.17, s32[1,128]{1,0:T(1,128)} %bitcast.18, ...), custom_call_target="tpu_custom_call" | custom-call | tf_op jit(solution)/shard_map/prepare/pallas_call | solution.py:43
  2.6 1.3 %collective-permute-start.32 = (f32[16,512]{1,0:T(8,128)S(1)}, f32[16,512]{1,0:T(8,128)S(1)}, u32[]{:S(2)}, u32[]{:S(2)}) collective-permute-start(f32[16,512]{1,0:T(8,128)S(1)} %get-tuple-element.81), channel_id=1, source_target_pairs={{0,1},{2,3},{4,5},{6,7},{8,9},{10,11},{12,13},{14,15},{16,17},{18,... | collective-permute-start | bytes 98312 | tf_op jit(solution)/shard_map/ppermute | solution.py:823
  5.1 1.6 %first_inside.1 = (f32[5,128,512]{2,1,0:T(8,128)S(1)}, f32[16,1024]{1,0:T(8,128)S(1)}) custom-call(f32[5,128,512]{2,1,0:T(8,128)S(1)} %bitcast.8, s32[128,512]{1,0:T(8,128)S(1)} %bitcast.12, f32[16]{0:T(128)S(1)} %copy-done.7, f32[8]{0:T(128)S(1)} %copy-done.8), custom_call_target="tpu_custom_call" | custom-call | tf_op jit(solution)/shard_map/first_inside/pallas_call | solution.py:43
  6.7 1.7 %collective-permute-done.32.prefix_ref = f32[16,512]{1,0:T(8,128)S(1)} collective-permute-done((f32[16,512]{1,0:T(8,128)S(1)}, f32[16,512]{1,0:T(8,128)S(1)}, u32[]{:S(2)}, u32[]{:S(2)}) %collective-permute-start.32) | collective-permute-done | bytes 32800 | tf_op jit(solution)/shard_map/ppermute | solution.py:823
  9.1 3.6 %collective-permute-start.35 = (f32[16,128]{1,0:T(8,128)S(1)}, f32[16,128]{1,0:T(8,128)S(1)}, u32[]{:S(2)}, u32[]{:S(2)}) collective-permute-start(f32[16,128]{1,0:T(8,128)S(1)} %get-tuple-element.89.own_west_ref), channel_id=1, source_target_pairs={{8,0},{16,8},{24,16},{0,24},{9,1},{17,9},{25,17},{1,25},{10,2},{18... | collective-permute-start | bytes 24584 | tf_op jit(solution)/shard_map/ppermute | solution.py:851
  12.7 1.4 %collective-permute-done.35.from_east_ref = f32[16,128]{1,0:T(8,128)S(1)} collective-permute-done((f32[16,128]{1,0:T(8,128)S(1)}, f32[16,128]{1,0:T(8,128)S(1)}, u32[]{:S(2)}, u32[]{:S(2)}) %collective-permute-start.35) | collective-permute-done | bytes 8224 | tf_op jit(solution)/shard_map/ppermute | solution.py:851
  14.1 4.1 %collective-permute-done.34.from_west_ref = f32[16,128]{1,0:T(8,128)S(1)} collective-permute-done((f32[16,128]{1,0:T(8,128)S(1)}, f32[16,128]{1,0:T(8,128)S(1)}, u32[]{:S(2)}, u32[]{:S(2)}) %collective-permute-start.34) | collective-permute-done | bytes 8224 | tf_op jit(solution)/shard_map/ppermute | solution.py:850
  18.2 1.5 %edge_rows.1 = (f32[12,8,512]{2,1,0:T(8,128)}, f32[12,8,512]{2,1,0:T(8,128)}, f32[4,12,8,128]{3,2,1,0:T(8,128)S(1)}) custom-call(f32[5,128,512]{2,1,0:T(8,128)S(1)} %bitcast.9, s32[128,512]{1,0:T(8,128)S(1)} %bitcast.13, f32[16,512]{1,0:T(8,128)S(1)} %collective-permute-done.32.prefix_ref, f32[16]{0:T(128)S(1)} %copy-done.7, ...), custom_call_target="tpu_custom_call" | custom-call | tf_op jit(solution)/shard_map/edge_rows/pallas_call | solution.py:43
  19.6 3.5 %collective-permute-start.37 = (f32[12,8,512]{2,1,0:T(8,128)}, f32[12,8,512]{2,1,0:T(8,128)S(1)}, u32[]{:S(2)}, u32[]{:S(2)}) collective-permute-start(f32[12,8,512]{2,1,0:T(8,128)} %get-tuple-element.92), channel_id=1, source_target_pairs={{2,4},{4,2},{3,5},{5,3},{10,12},{12,10},{11,13},{13,11},{18,20},{2... | collective-permute-start | bytes 589832 | tf_op jit(solution)/shard_map/ppermute | solution.py:861
  23.2 0.7 %merge_flux.4 = (f32[16,1920]{1,0:T(8,128)S(1)}, f32[16,1920]{1,0:T(8,128)}) custom-call(f32[32,1920]{1,0:T(8,128)S(1)} %get-tuple-element.95.kept_ref, f32[32,1920]{1,0:T(8,128)S(1)} %collective-permute-done.38.got_ref), custom_call_target="tpu_custom_call" | custom-call | tf_op jit(solution)/shard_map/merge_flux/pallas_call | solution.py:43
  24.5 2.1 %conditional.1 = (f32[5,12,8,128]{3,2,1,0:T(8,128)}) conditional(s32[]{:T(128)} %clamp.3, f32[4,12,8,128]{3,2,1,0:T(8,128)S(1)} %get-tuple-element.97, f32[4,12,8,128]{3,2,1,0:T(8,128)S(1)} %get-tuple-element.97, f32[4,12,8,128]{3,2,1,0:T(8,128)S(1)} %get-tuple-element.97, ...), branch_computations={%region_0.0_spmd, %region_1.0_spmd, %region_2.0_spmd, %region_3.0_... | conditional | flops 61440 | bytes 1966168 | solution.py:880
  24.5 0.7 %collective-permute-start.2 = (f32[3,12,8,128]{3,2,1,0:T(8,128)S(1)}, f32[3,12,8,128]{3,2,1,0:T(8,128)S(1)}, u32[]{:S(2)}, u32[]{:S(2)}) collective-permute-start(f32[3,12,8,128]{3,2,1,0:T(8,128)S(1)} %slice.51), channel_id=1, source_target_pairs={{6,30},{14,22},{22,14},{30,6},{7,31},{15,23},{23,15},{31,7}} | collective-permute-start | bytes 442376 | tf_op jit(solution)/shard_map/cond/branch_1_fun/ppermute | solution.py:874
  25.9 0.7 %pad_maximum_fusion.1 = f32[5,12,8,128]{3,2,1,0:T(8,128)} fusion(f32[2,12,8,128]{3,2,1,0:T(8,128)S(1)} %collective-permute-done.3, f32[3,12,8,128]{3,2,1,0:T(8,128)S(1)} %collective-permute-done.2), kind=kLoop, calls=%fused_computation.1 | loop fusion | flops 61440 | bytes 491520 | tf_op jit(solution)/shard_map/cond/branch_1_fun/concatenate | solution.py:876
  26.8 7.0 %collective-permute-done.39.got_ref = f32[16,1920]{1,0:T(8,128)} collective-permute-done((f32[16,1920]{1,0:T(8,128)}, f32[16,1920]{1,0:T(8,128)}, u32[]{:S(2)}, u32[]{:S(2)}) %collective-permute-start.39) | collective-permute-done | bytes 122912 | tf_op jit(solution)/shard_map/ppermute | solution.py:831
  33.9 0.9 %copy-done.3 = f32[16,1920]{1,0:T(8,128)S(1)} copy-done((f32[16,1920]{1,0:T(8,128)S(1)}, f32[16,1920]{1,0:T(8,128)}, u32[]{:S(2)}) %copy-start.3) | copy-done | bytes 122904
  34.8 0.9 %merge_flux.5 = (f32[8,1920]{1,0:T(8,128)S(1)}, f32[8,1920]{1,0:T(8,128)S(1)}) custom-call(f32[16,1920]{1,0:T(8,128)S(1)} %copy-done.3, f32[16,1920]{1,0:T(8,128)} %collective-permute-done.39.got_ref), custom_call_target="tpu_custom_call" | custom-call | tf_op jit(solution)/shard_map/merge_flux/pallas_call | solution.py:43
  35.8 0.8 %copy-done.6 = f32[16,1024]{1,0:T(8,128)S(1)} copy-done((f32[16,1024]{1,0:T(8,128)S(1)}, f32[16,1024]{1,0:T(8,128)}, u32[]{:S(2)}) %copy-start.6) | copy-done | bytes 65560
  36.6 2.8 %first_rim.1 = (f32[2,6,8,512]{3,2,1,0:T(8,128)S(1)}, f32[2,16,128]{2,1,0:T(8,128)S(1)}, f32[2,5,8,512]{3,2,1,0:T(8,128)S(1)}, f32[2,16,128]{2,1,0:T(8,128)S(1)}, f32[24,1280]{1,0:T(8,128)S(1)}) custom-call(f32[5,128,512]{2,1,0:T(8,128)S(1)} %bitcast.10, s32[128,512]{1,0:T(8,128)S(1)} %bitcast.14, f32[16,512]{1,0:T(8,128)S(1)} %collective-permute-done.32.prefix_ref, ...), custom_call_target="tpu_custom_call" | custom-call | tf_op jit(solution)/shard_map/first_rim/pallas_call | solution.py:43
  40.0 1.3 %collective-permute-start.42 = (f32[24,1280]{1,0:T(8,128)S(1)}, f32[24,1280]{1,0:T(8,128)S(1)}, u32[]{:S(2)}, u32[]{:S(2)}) collective-permute-start(f32[24,1280]{1,0:T(8,128)S(1)} %get-tuple-element.114), channel_id=1, source_target_pairs={{0,1},{2,3},{4,5},{6,7},{8,9},{10,11},{12,13},{14,15},{16,17},{18,... | collective-permute-start | bytes 368648 | tf_op jit(solution)/shard_map/ppermute | solution.py:908
  41.3 2.7 %collective-permute-start.41 = (f32[8,1920]{1,0:T(8,128)S(1)}, f32[8,1920]{1,0:T(8,128)S(1)}, u32[]{:S(2)}, u32[]{:S(2)}) collective-permute-start(f32[8,1920]{1,0:T(8,128)S(1)} %add.3.mine_ref), channel_id=1, source_target_pairs={{0,1},{1,0},{2,3},{3,2},{4,5},{5,4},{6,7},{7,6},{8,9},{9,8},{10,11... | collective-permute-start | bytes 184328 | tf_op jit(solution)/shard_map/ppermute | solution.py:907
  44.0 5.1 %collective-permute-done.41.theirs_ref = f32[8,1920]{1,0:T(8,128)S(1)} collective-permute-done((f32[8,1920]{1,0:T(8,128)S(1)}, f32[8,1920]{1,0:T(8,128)S(1)}, u32[]{:S(2)}, u32[]{:S(2)}) %collective-permute-start.41) | collective-permute-done | bytes 61472 | tf_op jit(solution)/shard_map/ppermute | solution.py:907
  49.2 0.9 %flux_parts.1 = (f32[3,16,512]{2,1,0:T(8,128)S(1)}, f32[8,512]{1,0:T(8,128)S(1)}, f32[16,128]{1,0:T(8,128)S(1)}, f32[24,640]{1,0:T(8,128)S(1)}) custom-call(f32[8,1920]{1,0:T(8,128)S(1)} %add.3.mine_ref, f32[8,1920]{1,0:T(8,128)S(1)} %collective-permute-done.41.theirs_ref, s32[2048]{0:T(1024)S(1)} %copy-done.4), custom_call_target="tpu_custom_call" | custom-call | tf_op jit(solution)/shard_map/flux_parts/pallas_call | solution.py:43
  50.0 2.9 %second_substep.1 = (f32[5,128,512]{2,1,0:T(8,128)}, f32[2,128,512]{2,1,0:T(8,128)S(1)}) custom-call(f32[5,128,512]{2,1,0:T(8,128)S(1)} %get-tuple-element.80.state_ref, s32[128,512]{1,0:T(8,128)S(1)} %bitcast.15, f32[16,512]{1,0:T(8,128)S(1)} %collective-permute-done.32.prefix_ref, f32[2,6,8,512]{3,2,1,0:T(8,128)S(1)} %get-tuple-element.102.ring_rows_ref, ...), custom_call_target="tpu_custom_call" | custom-call | tf_op jit(solution)/shard_map/second_substep/pallas_call | solution.py:43
  52.9 1.0 %deeper_pressure.1 = f32[5,128,512]{2,1,0:T(8,128)} custom-call(f32[5,128,512]{2,1,0:T(8,128)} %get-tuple-element.112.out_in_hbm, f32[2,128,512]{2,1,0:T(8,128)S(1)} %get-tuple-element.113.flow_ref, s32[128,512]{1,0:T(8,128)S(1)} %bitcast.16, f32[24,1280]{1,0:T(8,128)S(1)} %collective-permute-done.42.sums_ref, ...), custom_call_target="tpu_custom_call", output_to_operand_aliasing={{}: (0, {})} | custom-call | tf_op jit(solution)/shard_map/deeper_pressure/pallas_call | solution.py:43
  (37 shorter events, 3.5 us)
Async XLA Ops:
  0.0 3.9 %copy-start.4 = (s32[2048]{0:T(1024)S(1)}, s32[2048]{0:T(1024)}, u32[]{:S(2)}) copy-start(s32[2048]{0:T(1024)} %partner_ref.3) | copy-start | bytes 24580
  0.0 5.1 %copy-start.1 = (s32[8,16,512]{2,1,0:T(8,128)S(1)}, s32[8,16,512]{2,1,0:T(8,128)}, u32[]{:S(2)}) copy-start(s32[8,16,512]{2,1,0:T(8,128)} %param.25) | copy-start | bytes 786436
  0.0 5.1 %copy-start = (f32[5,8,16,512]{3,2,1,0:T(8,128)S(1)}, f32[5,8,16,512]{3,2,1,0:T(8,128)}, u32[]{:S(2)}) copy-start(f32[5,8,16,512]{3,2,1,0:T(8,128)} %param.24) | copy-start | bytes 3932164
  0.0 5.1 %copy-start.7 = (f32[16]{0:T(128)S(1)}, f32[16]{0:T(128)}, u32[]{:S(2)}) copy-start(f32[16]{0:T(128)} %turn_ref.7) | copy-start | bytes 196
  0.0 5.1 %copy-start.8 = (f32[8]{0:T(128)S(1)}, f32[8]{0:T(128)}, u32[]{:S(2)}) copy-start(f32[8]{0:T(128)} %share_ref.5) | copy-start | bytes 100
  2.5 5.9 %collective-permute-start.33 = (f32[64,1920]{1,0:T(8,128)S(1)}, f32[64,1920]{1,0:T(8,128)S(1)}, u32[]{:S(2)}, u32[]{:S(2)}) collective-permute-start(f32[64,1920]{1,0:T(8,128)S(1)} %get-tuple-element.77), channel_id=1, source_target_pairs={{0,2},{2,0},{4,6},{6,4},{1,3},{3,1},{5,7},{7,5},{8,10},{10,8},{12,... | collective-permute-start | bytes 1474568 | tf_op jit(solution)/shard_map/ppermute | solution.py:822
  2.6 5.8 %collective-permute-start.32 = (f32[16,512]{1,0:T(8,128)S(1)}, f32[16,512]{1,0:T(8,128)S(1)}, u32[]{:S(2)}, u32[]{:S(2)}) collective-permute-start(f32[16,512]{1,0:T(8,128)S(1)} %get-tuple-element.81), channel_id=1, source_target_pairs={{0,1},{2,3},{4,5},{6,7},{8,9},{10,11},{12,13},{14,15},{16,17},{18,... | collective-permute-start | bytes 98312 | tf_op jit(solution)/shard_map/ppermute | solution.py:823
  6.7 12.9 %copy-start.5 = (f32[16,1024]{1,0:T(8,128)}, f32[16,1024]{1,0:T(8,128)S(1)}, u32[]{:S(2)}) copy-start(f32[16,1024]{1,0:T(8,128)S(1)} %get-tuple-element.101.inside_ref) | copy-start | bytes 196612
  8.5 14.7 %collective-permute-start.38 = (f32[32,1920]{1,0:T(8,128)S(1)}, f32[32,1920]{1,0:T(8,128)S(1)}, u32[]{:S(2)}, u32[]{:S(2)}) collective-permute-start(f32[32,1920]{1,0:T(8,128)S(1)} %get-tuple-element.85), channel_id=1, source_target_pairs={{0,4},{2,6},{4,0},{6,2},{1,5},{3,7},{5,1},{7,3},{8,12},{10,14},{12... | collective-permute-start | bytes 737288 | tf_op jit(solution)/shard_map/ppermute | solution.py:831
  9.1 5.0 %collective-permute-start.35 = (f32[16,128]{1,0:T(8,128)S(1)}, f32[16,128]{1,0:T(8,128)S(1)}, u32[]{:S(2)}, u32[]{:S(2)}) collective-permute-start(f32[16,128]{1,0:T(8,128)S(1)} %get-tuple-element.89.own_west_ref), channel_id=1, source_target_pairs={{8,0},{16,8},{24,16},{0,24},{9,1},{17,9},{25,17},{1,25},{10,2},{18... | collective-permute-start | bytes 24584 | tf_op jit(solution)/shard_map/ppermute | solution.py:851
  12.7 5.4 %collective-permute-start.34 = (f32[16,128]{1,0:T(8,128)S(1)}, f32[16,128]{1,0:T(8,128)S(1)}, u32[]{:S(2)}, u32[]{:S(2)}) collective-permute-start(f32[16,128]{1,0:T(8,128)S(1)} %get-tuple-element.90.own_east_ref), channel_id=1, source_target_pairs={{0,8},{8,16},{16,24},{24,0},{1,9},{9,17},{17,25},{25,1},{2,10},{10... | collective-permute-start | bytes 24584 | tf_op jit(solution)/shard_map/ppermute | solution.py:850
  19.6 7.0 %collective-permute-start.36 = (f32[12,8,512]{2,1,0:T(8,128)}, f32[12,8,512]{2,1,0:T(8,128)S(1)}, u32[]{:S(2)}, u32[]{:S(2)}) collective-permute-start(f32[12,8,512]{2,1,0:T(8,128)} %get-tuple-element.91), channel_id=1, source_target_pairs={{0,2},{2,0},{4,6},{6,4},{1,3},{3,1},{5,7},{7,5},{8,10},{10,8},{12,... | collective-permute-start | bytes 589832 | tf_op jit(solution)/shard_map/ppermute | solution.py:860
  19.6 7.2 %collective-permute-start.37 = (f32[12,8,512]{2,1,0:T(8,128)}, f32[12,8,512]{2,1,0:T(8,128)S(1)}, u32[]{:S(2)}, u32[]{:S(2)}) collective-permute-start(f32[12,8,512]{2,1,0:T(8,128)} %get-tuple-element.92), channel_id=1, source_target_pairs={{2,4},{4,2},{3,5},{5,3},{10,12},{12,10},{11,13},{13,11},{18,20},{2... | collective-permute-start | bytes 589832 | tf_op jit(solution)/shard_map/ppermute | solution.py:861
  23.9 0.6 %copy-start.2 = (f32[16,1920]{1,0:T(8,128)}, f32[16,1920]{1,0:T(8,128)S(1)}, u32[]{:S(2)}) copy-start(f32[16,1920]{1,0:T(8,128)S(1)} %get-tuple-element.99.kept_ref) | copy-start | bytes 368644
  24.5 9.4 %collective-permute-start.39 = (f32[16,1920]{1,0:T(8,128)}, f32[16,1920]{1,0:T(8,128)}, u32[]{:S(2)}, u32[]{:S(2)}) collective-permute-start(f32[16,1920]{1,0:T(8,128)} %get-tuple-element.96), channel_id=1, source_target_pairs={{0,16},{8,24},{16,0},{24,8},{1,17},{9,25},{17,1},{25,9},{2,18},{10... | collective-permute-start | bytes 368648 | tf_op jit(solution)/shard_map/ppermute | solution.py:831
  24.5 1.4 %collective-permute-start.2 = (f32[3,12,8,128]{3,2,1,0:T(8,128)S(1)}, f32[3,12,8,128]{3,2,1,0:T(8,128)S(1)}, u32[]{:S(2)}, u32[]{:S(2)}) collective-permute-start(f32[3,12,8,128]{3,2,1,0:T(8,128)S(1)} %slice.51), channel_id=1, source_target_pairs={{6,30},{14,22},{22,14},{30,6},{7,31},{15,23},{23,15},{31,7}} | collective-permute-start | bytes 442376 | tf_op jit(solution)/shard_map/cond/branch_1_fun/ppermute | solution.py:874
  25.2 0.7 %collective-permute-start.3 = (f32[2,12,8,128]{3,2,1,0:T(8,128)S(1)}, f32[2,12,8,128]{3,2,1,0:T(8,128)S(1)}, u32[]{:S(2)}, u32[]{:S(2)}) collective-permute-start(f32[2,12,8,128]{3,2,1,0:T(8,128)S(1)} %slice.52), channel_id=1, source_target_pairs={{6,6},{14,30},{22,22},{30,14},{7,7},{15,31},{23,23},{31,15}} | collective-permute-start | bytes 294920 | tf_op jit(solution)/shard_map/cond/branch_1_fun/ppermute | solution.py:874
  33.9 0.9 %copy-start.3 = (f32[16,1920]{1,0:T(8,128)S(1)}, f32[16,1920]{1,0:T(8,128)}, u32[]{:S(2)}) copy-start(f32[16,1920]{1,0:T(8,128)} %copy-done.2) | copy-start | bytes 368644
  35.7 4.3 %collective-permute-start.40 = (f32[8,1920]{1,0:T(8,128)S(1)}, f32[8,1920]{1,0:T(8,128)S(1)}, u32[]{:S(2)}, u32[]{:S(2)}) collective-permute-start(f32[8,1920]{1,0:T(8,128)S(1)} %get-tuple-element.100), channel_id=1, source_target_pairs={{0,8},{8,0},{16,24},{24,16},{1,9},{9,1},{17,25},{25,17},{2,10},{10... | collective-permute-start | bytes 184328 | tf_op jit(solution)/shard_map/ppermute | solution.py:831
  35.8 0.8 %copy-start.6 = (f32[16,1024]{1,0:T(8,128)S(1)}, f32[16,1024]{1,0:T(8,128)}, u32[]{:S(2)}) copy-start(f32[16,1024]{1,0:T(8,128)} %copy-done.5) | copy-start | bytes 196612
  40.0 12.9 %collective-permute-start.42 = (f32[24,1280]{1,0:T(8,128)S(1)}, f32[24,1280]{1,0:T(8,128)S(1)}, u32[]{:S(2)}, u32[]{:S(2)}) collective-permute-start(f32[24,1280]{1,0:T(8,128)S(1)} %get-tuple-element.114), channel_id=1, source_target_pairs={{0,1},{2,3},{4,5},{6,7},{8,9},{10,11},{12,13},{14,15},{16,17},{18,... | collective-permute-start | bytes 368648 | tf_op jit(solution)/shard_map/ppermute | solution.py:908
  41.3 7.9 %collective-permute-start.41 = (f32[8,1920]{1,0:T(8,128)S(1)}, f32[8,1920]{1,0:T(8,128)S(1)}, u32[]{:S(2)}, u32[]{:S(2)}) collective-permute-start(f32[8,1920]{1,0:T(8,128)S(1)} %add.3.mine_ref), channel_id=1, source_target_pairs={{0,1},{1,0},{2,3},{3,2},{4,5},{5,4},{6,7},{7,6},{8,9},{9,8},{10,11... | collective-permute-start | bytes 184328 | tf_op jit(solution)/shard_map/ppermute | solution.py:907
